TPU v7x, 128 devices: a whole 4x4x4 slice. The times are simulated.
128 devices in a mesh: seq: 32 (over y, z, core), chan: 4 (over x).
Axes of the slice: x: 4, y: 4, z: 4, core: 2. Of those that a mesh axis runs over, the one named last changes fastest.
Arguments:
- projected: bfloat16 [8192, 3, 1024], P('seq', None, 'chan'), may hold values from -6 to 6
- short_taps: float32 [3, 3, 1024], P(None, None, 'chan'), may hold values from -3.5 to 3.5
- filters: float32 [8192, 1024], P('seq', 'chan'), may hold values from -1 to 1, as said below
- skip_gain: float32 [1024], P('chan'), may hold values from -4 to 4
- out_weight: bfloat16 [1024, 1024], P('chan'), may hold values from -0.1875 to 0.1875
Outputs:
- block_out: bfloat16 [8192, 1024], P(('seq', 'chan'))
Inputs may be any that keep to these rules, and one draw needn't show every extreme that they name: `filters`: each column is one channel's long filter.
All inputs are finite; a program needn't handle non-finite values.
Results may differ from a plain program's by a relative error of at most 0.018.
Values may be sent and summed in bfloat16 or wider, within the bound.
No kernel may reach another device: no remote copies, remote signals or barrier semaphores. Data moves between devices by JAX's collectives and lax.ppermute only.
A program may use at most 64 MiB of HBM per device.

v0:
```python
import math

import jax
import jax.numpy as jnp
from jax import lax
from jax.sharding import PartitionSpec as P


def shifted(shard, axis, by):
    devices = lax.axis_size(axis)
    pairs = [(i, i + by) for i in range(devices) if 0 <= i + by < devices]
    return lax.ppermute(shard, axis, pairs)


def tables(size, sign):
    index_row = jnp.arange(size, dtype=jnp.int32)
    turns = index_row[:, None] * index_row[None, :] % size
    angle = sign * 2.0 * math.pi / size * turns.astype(jnp.float32)
    return (jnp.cos(angle), jnp.sin(angle))


def exact_dot(left, right):
    return jnp.dot(left, right, precision=lax.Precision.HIGHEST, preferred_element_type=jnp.float32)


def complex_apply(cos_table, sin_table, real_part, imag_part):
    real_out = exact_dot(cos_table, real_part)
    imag_out = exact_dot(sin_table, real_part)
    if imag_part is not None:
        real_out = real_out - exact_dot(sin_table, imag_part)
        imag_out = imag_out + exact_dot(cos_table, imag_part)
    return (real_out, imag_out)


def transform(real_part, imag_part, sign):
    size = real_part.shape[0]
    columns = real_part.shape[1]
    first = math.gcd(size, 128)
    if size <= 128 or first == 1:
        cos_table, sin_table = tables(size, sign)
        return complex_apply(cos_table, sin_table, real_part, imag_part)
    second = size // first
    real_view = real_part.reshape(first, second * columns)
    imag_view = None if imag_part is None else imag_part.reshape(first, second * columns)
    cos_table, sin_table = tables(first, sign)
    real_view, imag_view = complex_apply(cos_table, sin_table, real_view, imag_view)
    turns = (
        jnp.arange(first, dtype=jnp.int32)[:, None]
        * jnp.arange(second, dtype=jnp.int32)[None, :]
        % size
    )
    angle = sign * 2.0 * math.pi / size * turns.astype(jnp.float32)
    twist_cos = jnp.cos(angle)[:, :, None]
    twist_sin = jnp.sin(angle)[:, :, None]
    real_view = real_view.reshape(first, second, columns)
    imag_view = imag_view.reshape(first, second, columns)
    rot_real = real_view * twist_cos - imag_view * twist_sin
    rot_imag = real_view * twist_sin + imag_view * twist_cos
    rot_real = rot_real.transpose(1, 0, 2).reshape(second, first * columns)
    rot_imag = rot_imag.transpose(1, 0, 2).reshape(second, first * columns)
    out_real, out_imag = transform(rot_real, rot_imag, sign)
    return (out_real.reshape(size, columns), out_imag.reshape(size, columns))


def channel_conv(signal, filters):
    whole_sig = lax.all_to_all(signal, "seq", split_axis=1, concat_axis=0, tiled=True)
    whole_fil = lax.all_to_all(
        filters.astype(jnp.bfloat16), "seq", split_axis=1, concat_axis=0, tiled=True
    ).astype(filters.dtype)
    full_length = whole_fil.shape[0]
    zero_rows = jnp.zeros_like(whole_fil)
    sig_pad = jnp.concatenate([whole_sig.astype(jnp.float32), zero_rows], axis=0)
    fil_pad = jnp.concatenate([whole_fil, zero_rows], axis=0)
    spec_real, spec_imag = transform(sig_pad, None, -1.0)
    resp_real, resp_imag = transform(fil_pad, None, -1.0)
    prod_real = spec_real * resp_real - spec_imag * resp_imag
    prod_imag = spec_real * resp_imag + spec_imag * resp_real
    back_real, back_imag = transform(prod_real, prod_imag, 1.0)
    conv_whole = back_real[:full_length] * (1.0 / (2 * full_length))
    return lax.all_to_all(
        conv_whole.astype(jnp.bfloat16), "seq", split_axis=0, concat_axis=1, tiled=True
    ).astype(conv_whole.dtype)


def on_device(projected, short_taps, filters, skip_gain, out_weight):
    length = projected.shape[0]
    tap_count = short_taps.shape[0]
    rim_rows = shifted(projected[length - (tap_count - 1) :], "seq", 1)
    extended = jnp.concatenate([rim_rows, projected], axis=0).astype(jnp.float32)
    shaped = jnp.zeros(projected.shape, jnp.float32)
    for tap_index in range(tap_count):
        begin = tap_count - 1 - tap_index
        shaped = shaped + short_taps[tap_index] * extended[begin : begin + length]
    query_rows = shaped[:, 0, :]
    signal = (shaped[:, 1, :] * shaped[:, 2, :]).astype(jnp.bfloat16)
    signal_wide = lax.optimization_barrier(signal).astype(jnp.float32)
    conv = channel_conv(signal, filters)
    gated_rows = (query_rows * (conv + skip_gain * signal_wide)).astype(jnp.bfloat16)
    return lax.psum_scatter(
        jnp.dot(gated_rows, out_weight, preferred_element_type=jnp.float32).astype(jnp.bfloat16),
        "chan",
        scatter_dimension=0,
        tiled=True,
    )


def solution(mesh):
    return jax.shard_map(
        on_device,
        mesh=mesh,
        in_specs=(
            P("seq", None, "chan"),
            P(None, None, "chan"),
            P("seq", "chan"),
            P("chan"),
            P("chan", None),
        ),
        out_specs=P(("seq", "chan"), None),
        check_vma=False,
    )
```

profile of v0, /device:TPU:1, one launch (start us, length us, event | category | flops | bytes accessed | tf_op | source)
XLA Modules:
  0.0 136.2 jit_solution(965870182307688353)
XLA Ops:
  7.5 4.9 %collective-permute-start = (bf16[2,3,256]{0,2,1:T(8,128)(2,1)S(1)}, bf16[2,3,256]{0,2,1:T(8,128)(2,1)S(1)}, u32[]{:S(2)}, u32[]{:S(2)}) collective-permute-start(bf16[2,3,256]{0,2,1:T(8,128)(2,1)S(1)} %copy.33), channel_id=1, source_target_pairs={{0,4},{4,8},{8,12},{12,16},{16,20},{20,24},{24,28},{28,32},{32,36}... | collective-permute-start | bytes 9224 | tf_op jit(solution)/shard_map/ppermute | solution.py:12
  12.5 1.7 %copy.43 = bf16[256,256]{0,1:T(8,128)(2,1)} copy(f32[256,256]{1,0:T(8,128)} %param.7) | data formatting | bytes 393216 | tf_op args[2]
  14.2 7.8 %all-to-all-start.1 = ((bf16[256,32,8]{0,2,1:T(8,128)(2,1)}), bf16[256,32,8]{0,2,1:T(8,128)(2,1)S(1)}, u32[]{:S(2)}, u32[]{:S(2)}) async-start(bf16[256,32,8]{0,2,1:T(8,128)(2,1)} %bitcast.100), calls=%async_computation.1 | async-start | bytes 262144 | tf_op jit(solution)/shard_map/all_to_all | solution.py:67
  28.5 1.1 all-to-all-done.1
  29.6 6.3 %all-to-all-start = ((bf16[256,32,8]{0,2,1:T(8,128)(2,1)}), bf16[256,32,8]{0,2,1:T(8,128)(2,1)}, u32[]{:S(2)}, u32[]{:S(2)}) async-start(bf16[256,32,8]{0,2,1:T(8,128)(2,1)} %fusion.146), calls=%async_computation | async-start | bytes 262144 | tf_op jit(solution)/shard_map/all_to_all | solution.py:66
  37.0 8.9 %concatenate.11.clone = bf16[16384,8]{1,0:T(8,128)(2,1)} pad(bf16[8192,8]{1,0:T(8,128)(2,1)S(1)} %copy.58, bf16[]{:T(256)} %constant.54.clone.1), padding=0_8192x0_0 | pad | bytes 393218 | tf_op jit(solution)/shard_map/concatenate | solution.py:73
  45.9 7.0 %reshape.136 = bf16[128,1024]{1,0:T(8,128)(2,1)S(1)} reshape(bf16[16384,8]{1,0:T(8,128)(2,1)} %concatenate.11.clone) | data formatting | bytes 524288 | tf_op jit(solution)/shard_map/reshape | solution.py:43
  53.1 1.4 %convolution_bitcast_fusion.1 = f32[128,128,8]{0,1,2:T(8,128)} fusion(bf16[128,8,128]{2,1,0:T(8,128)(2,1)S(1)} %bitcast.112), kind=kOutput, calls=%fused_computation.2 | convolution fusion | flops 201555968 | bytes 786432 | tf_op jit(solution)/shard_map/dot_general | solution.py:23
  54.6 1.8 %copy.57 = bf16[8192,8]{1,0:T(8,128)(2,1)S(1)} copy(bf16[8192,8]{0,1:T(8,128)(2,1)} %bitcast.7) | data formatting | bytes 262144
  56.4 8.9 %concatenate.10.clone = bf16[16384,8]{1,0:T(8,128)(2,1)} pad(bf16[8192,8]{1,0:T(8,128)(2,1)S(1)} %copy.57, bf16[]{:T(256)} %constant.54.clone.1), padding=0_8192x0_0 | pad | bytes 393218 | tf_op jit(solution)/shard_map/concatenate | solution.py:72
  65.3 7.2 %reshape.133 = bf16[128,1024]{1,0:T(8,128)(2,1)S(1)} reshape(bf16[16384,8]{1,0:T(8,128)(2,1)} %concatenate.10.clone) | data formatting | bytes 524288 | tf_op jit(solution)/shard_map/reshape | solution.py:43
  74.9 1.0 fusion.14
  77.0 1.0 fusion.20
  80.2 1.1 convolution_add_fusion.1
  81.2 1.1 convolution_subtract_fusion.2
  82.3 1.2 multiply_add_fusion
  85.2 1.9 %convolution_add_fusion = f32[128,1024]{1,0:T(8,128)} fusion(f32[128,1024]{1,0:T(8,128)S(1)} %fusion.55, f32[128,1024]{1,0:T(8,128)S(1)} %get-tuple-element.5), kind=kOutput, calls=%fused_computation.5 | convolution fusion | flops 201687040 | bytes 1572864 | tf_op jit(solution)/shard_map/dot_general | solution.py:23
  87.1 1.2 copy.52
  91.9 2.5 %convert_element_type.150 = bf16[32,256,8]{2,1,0:T(8,128)(2,1)S(1)} reshape(bf16[64,1024]{1,0:T(8,128)(2,1)S(1)} %fusion.31) | data formatting | bytes 262144 | tf_op jit(solution)/shard_map/convert_element_type | solution.py:81
  94.4 1.4 %copy.56 = bf16[32,256,8]{1,2,0:T(8,128)(2,1)} copy(bf16[32,256,8]{2,1,0:T(8,128)(2,1)S(1)} %convert_element_type.150) | data formatting | bytes 262144 | tf_op jit(solution)/shard_map/convert_element_type | solution.py:81
  95.8 7.4 %all-to-all-start.2 = ((bf16[32,256,8]{1,2,0:T(8,128)(2,1)}), bf16[32,256,8]{1,2,0:T(8,128)(2,1)S(1)}, u32[]{:S(2)}, u32[]{:S(2)}) async-start(bf16[32,256,8]{1,2,0:T(8,128)(2,1)} %copy.56), calls=%async_computation.2 | async-start | bytes 262144 | tf_op jit(solution)/shard_map/all_to_all | solution.py:80
  103.3 7.6 %all-to-all-done.2 = bf16[32,256,8]{1,2,0:T(8,128)(2,1)S(1)} async-done(((bf16[32,256,8]{1,2,0:T(8,128)(2,1)}), bf16[32,256,8]{1,2,0:T(8,128)(2,1)S(1)}, u32[]{:S(2)}, u32[]{:S(2)}) %all-to-all-start.2) | async-done | bytes 131104 | tf_op jit(solution)/shard_map/all_to_all | solution.py:80
  110.9 1.2 convolution_convert_fusion
  112.1 17.2 %reduce-scatter.2.cloned.1.call-done = bf16[64,1024]{1,0:T(8,128)(2,1)} async-done(((bf16[256,1024]{1,0:T(8,128)(2,1)}), bf16[64,1024]{1,0:T(8,128)(2,1)}) %reduce-scatter.2.cloned.1.call-update) | async-done | bytes 131088 | tf_op jit(solution)/shard_map/reduce_scatter | solution.py:99
  (59 shorter events, 19.3 us)
Async XLA Ops:
  6.5 104.3 %copy-start = (bf16[256,1024]{1,0:T(8,128)(2,1)S(1)}, bf16[256,1024]{1,0:T(8,128)(2,1)}, u32[]{:S(2)}) copy-start(bf16[256,1024]{1,0:T(8,128)(2,1)} %param.9) | copy-start | bytes 1572868
  6.5 17.2 %copy-start.4 = (bf16[256,3,256]{2,0,1:T(8,128)(2,1)S(1)}, bf16[256,3,256]{2,0,1:T(8,128)(2,1)}, u32[]{:S(2)}) copy-start(bf16[256,3,256]{2,0,1:T(8,128)(2,1)} %param.5) | copy-start | bytes 1179652
  7.5 19.3 %collective-permute-start = (bf16[2,3,256]{0,2,1:T(8,128)(2,1)S(1)}, bf16[2,3,256]{0,2,1:T(8,128)(2,1)S(1)}, u32[]{:S(2)}, u32[]{:S(2)}) collective-permute-start(bf16[2,3,256]{0,2,1:T(8,128)(2,1)S(1)} %copy.33), channel_id=1, source_target_pairs={{0,4},{4,8},{8,12},{12,16},{16,20},{20,24},{24,28},{28,32},{32,36}... | collective-permute-start | bytes 9224 | tf_op jit(solution)/shard_map/ppermute | solution.py:12
  14.2 15.5 %all-to-all-start.1 = ((bf16[256,32,8]{0,2,1:T(8,128)(2,1)}), bf16[256,32,8]{0,2,1:T(8,128)(2,1)S(1)}, u32[]{:S(2)}, u32[]{:S(2)}) async-start(bf16[256,32,8]{0,2,1:T(8,128)(2,1)} %bitcast.100), calls=%async_computation.1 | async-start | bytes 262144 | tf_op jit(solution)/shard_map/all_to_all | solution.py:67
  29.6 24.9 %all-to-all-start = ((bf16[256,32,8]{0,2,1:T(8,128)(2,1)}), bf16[256,32,8]{0,2,1:T(8,128)(2,1)}, u32[]{:S(2)}, u32[]{:S(2)}) async-start(bf16[256,32,8]{0,2,1:T(8,128)(2,1)} %fusion.146), calls=%async_computation | async-start | bytes 262144 | tf_op jit(solution)/shard_map/all_to_all | solution.py:66
  53.1 1.4 %copy-start.1 = (bf16[1024,128]{1,0:T(8,128)(2,1)}, bf16[1024,128]{1,0:T(8,128)(2,1)S(1)}, u32[]{:S(2)}) copy-start(bf16[1024,128]{1,0:T(8,128)(2,1)S(1)} %copy.45) | copy-start | bytes 786436
  72.5 1.5 %copy-start.2 = (bf16[1024,128]{1,0:T(8,128)(2,1)S(1)}, bf16[1024,128]{1,0:T(8,128)(2,1)}, u32[]{:S(2)}) copy-start(bf16[1024,128]{1,0:T(8,128)(2,1)} %copy-done.1) | copy-start | bytes 786436
  72.5 1.5 %copy-start.3 = (f32[128,128,8]{0,1,2:T(8,128)S(1)}, f32[128,128,8]{0,1,2:T(8,128)}, u32[]{:S(2)}) copy-start(f32[128,128,8]{0,1,2:T(8,128)} %convolution_bitcast_fusion.1) | copy-start | bytes 1572868
  72.5 1.5 %copy-start.5 = (f32[128,128]{0,1:T(8,128)S(1)}, f32[128,128]{0,1:T(8,128)}, u32[]{:S(2)}) copy-start(f32[128,128]{0,1:T(8,128)} %copy.40) | copy-start | bytes 196612
  72.6 1.5 %copy-start.6 = (f32[128,128]{0,1:T(8,128)S(1)}, f32[128,128]{0,1:T(8,128)}, u32[]{:S(2)}) copy-start(f32[128,128]{0,1:T(8,128)} %copy.38) | copy-start | bytes 196612
  88.3 1.1 copy-start.7
  88.4 1.1 copy-start.8
  94.4 16.5 %copy-start.9 = (f32[256]{0:T(256)S(1)}, f32[256]{0:T(256)}, u32[]{:S(2)}) copy-start(f32[256]{0:T(256)} %param.8) | copy-start | bytes 3076
  95.8 15.1 %all-to-all-start.2 = ((bf16[32,256,8]{1,2,0:T(8,128)(2,1)}), bf16[32,256,8]{1,2,0:T(8,128)(2,1)S(1)}, u32[]{:S(2)}, u32[]{:S(2)}) async-start(bf16[32,256,8]{1,2,0:T(8,128)(2,1)} %copy.56), calls=%async_computation.2 | async-start | bytes 262144 | tf_op jit(solution)/shard_map/all_to_all | solution.py:80
  103.2 26.2 %reduce-scatter.2.cloned.1.call-start = ((), (), s32[]{:S(2)}) async-start(), calls=%async_computation.4 | async-start | bytes 655360 | tf_op jit(solution)/shard_map/reduce_scatter | solution.py:99
Sparse Core Ops, SparseCore 0:
  112.3 17.0 reduce-scatter.1
where the time goes:
time: 138 us; the launch traced here: 136 us
  local copies, waits for them, and re-layouts  47.6 us (34%)
  starting transfers between devices  26.5 us (19%)
  waiting for transfers between devices  26 us (19%)
  matrix products  19.4 us (14%)
  between operations  13.8 us (10%)
  other arithmetic  2.94 us (2%)
    dot_general x18, matrix products, exact_dot(): jnp.dot(left, right, precision=lax.Precision.HIGHEST, preferred_element_t...  18.2 us
    reduce_scatter x1, waiting for transfers between devices, on_device(): lax.psum_scatter(jnp.dot(gated_rows, out_weight, preferred_element_type=j...  17.2 us
    reshape x2, local copies, waits for them, and re-layouts, transform(): real_view = real_part.reshape(first, second * columns)  14.3 us
    concatenate x1, local copies, waits for them, and re-layouts, channel_conv(): fil_pad = jnp.concatenate([whole_fil, zero_rows], axis=0)  8.9 us
    concatenate x1, local copies, waits for them, and re-layouts, channel_conv(): jnp.concatenate([whole_sig.astype(jnp.float32), zero_rows], axis=0)  8.9 us
    all_to_all x1, starting transfers between devices, channel_conv(): lax.all_to_all(filters.astype(jnp.bfloat16), 'seq', split_axis=1, concat_...  7.76 us
    all_to_all x1, waiting for transfers between devices, channel_conv(): lax.all_to_all(conv_whole.astype(jnp.bfloat16), 'seq', split_axis=0, conc...  7.62 us
    all_to_all x1, starting transfers between devices, channel_conv(): lax.all_to_all(conv_whole.astype(jnp.bfloat16), 'seq', split_axis=0, conc...  7.39 us
  transfers between devices with their start and end apart: 5, of which 3 were waited for; matrix products, arithmetic and copies ran while one was open for 20% of the time, Pallas kernels for 0%

commit v1 on v0

v1 whole, which is shorter than its diff:
```python
import math

import jax
import jax.numpy as jnp
import numpy as np
from jax import lax
from jax.experimental import pallas as pl
from jax.experimental.pallas import tpu as pltpu
from jax.sharding import PartitionSpec as P

BLOCKS = 32
SPAN = 256
OWN = 8
BF = jnp.bfloat16
F32 = jnp.float32


def dot(left, right):
    return jnp.dot(left, right, preferred_element_type=F32)


def constants():
    total = BLOCKS * SPAN
    low = np.arange(BLOCKS)[:, None] + 0.25
    coarse = 2 * math.pi / BLOCKS * low * np.arange(BLOCKS)[None, :]
    eye = np.eye(OWN)
    ahead = np.concatenate([np.kron(np.cos(coarse), eye), np.kron(-np.sin(coarse), eye)], axis=0)
    back = ahead.T / total
    turn = 2 * math.pi / total * low * np.arange(SPAN)[None, :]
    turn = np.repeat(turn, OWN, axis=0)
    fine = 2 * math.pi / SPAN * (np.arange(SPAN)[:, None] * np.arange(SPAN)[None, :] % SPAN)
    cos, sin = np.cos(fine), np.sin(fine)
    spread = np.block([[cos, -sin], [sin, cos]])
    gather = np.block([[cos, sin], [-sin, cos]])
    pick = np.zeros((SPAN, SPAN))
    order = np.zeros((SPAN, SPAN))
    for i in range(BLOCKS):
        for h in range(2):
            for c in range(4):
                pick[8 * i + 4 * h + c, 128 * h + 4 * i + c] = 1
                order[128 * h + 4 * i + c, 8 * i + 4 * h + c] = 1
    as_bf = lambda table: jnp.asarray(table.astype(np.float32)).astype(BF)
    as_f32 = lambda table: jnp.asarray(table.astype(np.float32))
    return dict(
        ahead=as_bf(ahead),
        back=as_bf(back),
        spread=as_bf(spread),
        gather=as_bf(gather),
        cos=as_f32(np.cos(turn)),
        sin=as_f32(np.sin(turn)),
        pick=as_bf(pick),
        order=as_bf(order),
    )


def pack_kernel(projected_ref, filters_ref, pick_ref, out_ref):
    pick = pick_ref[...]
    for which in range(4):
        rows = projected_ref[which] if which < 3 else filters_ref[...].astype(BF)
        turned = lax.dot_general(pick, rows, (((1,), (1,)), ((), ())), preferred_element_type=F32)
        first = turned[:, :128].reshape(BLOCKS, OWN, 128)
        second = turned[:, 128:].reshape(BLOCKS, OWN, 128)
        out_ref[:, 16 * which : 16 * which + 16, :] = jnp.concatenate([first, second], axis=1).astype(BF)


def conv_kernel(
    got_ref, taps_ref, skip_ref, ahead_ref, back_ref, spread_ref, gather_ref, cos_ref, sin_ref, order_ref, out_ref
):
    place = lax.axis_index("seq")
    lane = lax.broadcasted_iota(jnp.int32, (OWN, SPAN), 1)
    row = lax.broadcasted_iota(jnp.int32, (OWN, SPAN), 0)
    mine = lane == 128 * (row // 4) + 4 * place + row % 4

    def own(values):
        return jnp.sum(jnp.where(mine, values, 0.0), axis=1, keepdims=True)[None]

    def block(which):
        both = got_ref[:, 16 * which : 16 * which + 16, :].astype(F32)
        first = both[:, :8].reshape(SPAN, 128)
        second = both[:, 8:].reshape(SPAN, 128)
        return jnp.concatenate([first, second], axis=1)

    wide_lane = lax.broadcasted_iota(jnp.int32, (SPAN, SPAN), 1)

    def later(rows, by):
        turned = pltpu.roll(rows, by, 1)
        earlier = jnp.concatenate([jnp.zeros((OWN, SPAN), F32), turned[:-OWN]], axis=0)
        return jnp.where(wide_lane < by, earlier, turned)

    def shaped(which):
        rows = block(which)
        total = None
        for tap, moved in enumerate((rows, later(rows, 1), later(rows, 2))):
            gain = own(taps_ref[3 * tap + which : 3 * tap + which + 1, :])
            term = moved.reshape(BLOCKS, OWN, SPAN) * gain
            total = term if total is None else total + term
        return total.reshape(SPAN, SPAN)

    signal = (shaped(1) * shaped(2)).astype(BF)
    response = block(3).astype(BF)
    cos, sin = cos_ref[...], sin_ref[...]

    def spectrum(rows):
        real, imag = dot(ahead_ref[:SPAN], rows), dot(ahead_ref[SPAN:], rows)
        turned = jnp.concatenate([real * cos + imag * sin, imag * cos - real * sin], axis=1)
        both = dot(turned.astype(BF), spread_ref[...])
        return both[:, :SPAN], both[:, SPAN:]

    sig_real, sig_imag = spectrum(signal)
    res_real, res_imag = spectrum(response)
    product = jnp.concatenate(
        [sig_real * res_real - sig_imag * res_imag, sig_real * res_imag + sig_imag * res_real], axis=1
    )
    both = dot(product.astype(BF), gather_ref[...])
    real, imag = both[:, :SPAN], both[:, SPAN:]
    turned = jnp.concatenate([real * cos - imag * sin, real * sin + imag * cos], axis=0)
    conv = dot(back_ref[...], turned.astype(BF))
    skip = own(skip_ref[...])
    direct = (signal.astype(F32).reshape(BLOCKS, OWN, SPAN) * skip).reshape(SPAN, SPAN)
    gated = (shaped(0) * (conv + direct)).astype(BF)
    gated = dot(order_ref[...], gated)
    half = lax.broadcasted_iota(jnp.int32, (128, 128), 1) < 64
    for h in range(2):
        low = gated[:128, 128 * h : 128 * h + 128]
        high = gated[128:, 128 * h : 128 * h + 128]
        even = jnp.where(half, low, pltpu.roll(high, 64, 1))
        odd = jnp.where(half, pltpu.roll(low, 64, 1), high)
        out_ref[256 * h : 256 * h + 128, :] = even.astype(BF)
        out_ref[256 * h + 128 : 256 * h + 256, :] = odd.astype(BF)


def project_kernel(got_ref, w0_ref, w1_ref, w2_ref, w3_ref, out_ref):
    place = lax.axis_index("chan")
    total = None
    for step, weight_ref in enumerate((w0_ref, w1_ref, w2_ref, w3_ref)):
        owner = lax.rem(place + step, 4)
        rows = got_ref[pl.ds(pl.multiple_of(owner * 128, 128), 128), :].astype(F32).T
        gated = jnp.concatenate([rows[:64], rows[64:]], axis=1).astype(BF)
        term = dot(gated, weight_ref[...])
        total = term if total is None else total + term
    out_ref[...] = total.astype(BF)


def call(kernel, shape, *args, flops=0):
    return pl.pallas_call(
        kernel,
        out_shape=jax.ShapeDtypeStruct(shape, BF),
        compiler_params=pltpu.CompilerParams(vmem_limit_bytes=40 * 1024 * 1024),
    )(*args)


def on_device(projected, short_taps, filters, skip_gain, out_weight):
    table = constants()
    weights = [out_weight]
    for step in range(1, 4):
        weights.append(lax.ppermute(out_weight, "chan", [(i, (i - step) % 4) for i in range(4)]))
    packed = call(pack_kernel, (BLOCKS, 64, 128), projected.transpose(1, 0, 2), filters, table["pick"])
    got = lax.all_to_all(packed, "seq", split_axis=0, concat_axis=0, tiled=True)
    gated = call(
        conv_kernel,
        (512, 128),
        got,
        short_taps.reshape(9, SPAN),
        skip_gain.reshape(1, SPAN),
        *(table[name] for name in ("ahead", "back", "spread", "gather", "cos", "sin", "order")),
    )
    got = lax.all_to_all(gated.reshape(128, 4, 128), ("chan", "seq"), split_axis=0, concat_axis=0, tiled=True)
    return call(project_kernel, (64, 1024), got.reshape(512, 128), *weights)


def solution(mesh):
    return jax.shard_map(
        on_device,
        mesh=mesh,
        in_specs=(
            P("seq", None, "chan"),
            P(None, None, "chan"),
            P("seq", "chan"),
            P("chan"),
            P("chan", None),
        ),
        out_specs=P(("seq", "chan"), None),
        check_vma=False,
    )
```

time: 138 us -> 49.4 us (0.36)
  local copies, waits for them, and re-layouts: 47.6 us -> 8.14 us
  matrix products: 19.4 us -> 0 us
  between operations: 13.8 us -> 0.05 us
  waiting for transfers between devices: 26 us -> 16.3 us
  starting transfers between devices: 26.5 us -> 19.5 us
  Pallas kernels: 0 us -> 4.82 us
  other arithmetic: 2.94 us -> 0 us
    dot_general x19 -> x0, matrix products: 19.4 us -> none  [the longest x18 18.2 us: exact_dot(): jnp.dot(left, right, precision=lax.Precision.HIGHEST, preferred_element_t...]
    concatenate x2 -> x0, local copies, waits for them, and re-layouts: 17.8 us -> none  [the longest x1 8.9 us: channel_conv(): fil_pad = jnp.concatenate([whole_fil, zero_rows], axis=0)]
    reduce_scatter x1 -> x0, waiting for transfers between devices: 17.2 us -> none  [on_device(): lax.psum_scatter(jnp.dot(gated_rows, out_weight, preferred_element_type=j...]
    reshape x2 -> x1, local copies, waits for them, and re-layouts: 14.3 us -> 0.72 us  [on_device(): short_taps.reshape(9, SPAN)]
    all_to_all x3 -> x2, starting transfers between devices: 21.5 us -> 15.3 us  [the longest x1 9.74 us: on_device(): got = lax.all_to_all(packed, 'seq', split_axis=0, concat_axis=0, tiled=True)]
    all_to_all x3 -> x2, waiting for transfers between devices: 8.73 us -> 13.9 us  [the longest x1 7.27 us: on_device(): lax.all_to_all(gated.reshape(128, 4, 128), ('chan', 'seq'), split_axis=0,...]
    pallas_call x0 -> x3, Pallas kernels: none -> 4.82 us  [call(): pl.pallas_call(kernel, out_shape=jax.ShapeDtypeStruct(shape, BF), compile...]
    convert_element_type x2 -> x0, local copies, waits for them, and re-layouts: 3.89 us -> none  [channel_conv(): conv_whole.astype(jnp.bfloat16)]
  transfers between devices with their start and end apart: 5 -> 5, of which waited for: 3 -> 4; matrix products, arithmetic and copies ran while one was open for 20% -> 1% of each run, Pallas kernels for 0% -> 5%
where the time goes in v1:
time: 49.4 us; the launch traced here: 48.9 us
  starting transfers between devices  19.5 us (39%)
  waiting for transfers between devices  16.3 us (33%)
  local copies, waits for them, and re-layouts  8.14 us (16%)
  Pallas kernels  4.82 us (10%)
    all_to_all x1, starting transfers between devices, on_device(): got = lax.all_to_all(packed, 'seq', split_axis=0, concat_axis=0, tiled=True)  9.74 us
    unnamed x24, local copies, waits for them, and re-layouts  7.42 us
    all_to_all x1, waiting for transfers between devices, on_device(): lax.all_to_all(gated.reshape(128, 4, 128), ('chan', 'seq'), split_axis=0,...  7.27 us
    all_to_all x1, waiting for transfers between devices, on_device(): got = lax.all_to_all(packed, 'seq', split_axis=0, concat_axis=0, tiled=True)  6.61 us
    all_to_all x1, starting transfers between devices, on_device(): lax.all_to_all(gated.reshape(128, 4, 128), ('chan', 'seq'), split_axis=0,...  5.51 us
    pallas_call x3, Pallas kernels, call(): pl.pallas_call(kernel, out_shape=jax.ShapeDtypeStruct(shape, BF), compile...  4.82 us
    ppermute x3, starting transfers between devices, on_device(): lax.ppermute(out_weight, 'chan', [(i, (i - step) % 4) for i in range(4)])  4.28 us
    ppermute x3, waiting for transfers between devices, on_device(): lax.ppermute(out_weight, 'chan', [(i, (i - step) % 4) for i in range(4)])  2.47 us
  transfers between devices with their start and end apart: 5, of which 4 were waited for; matrix products, arithmetic and copies ran while one was open for 1% of the time, Pallas kernels for 5%

profile of v1, /device:TPU:1, one launch (start us, length us, event | category | flops | bytes accessed | tf_op | source)
XLA Modules:
  0.0 48.9 jit_solution(2411969710945301622)
XLA Ops:
  0.0 1.0 %copy-done.3 = bf16[256,3,256]{2,0,1:T(8,128)(2,1)S(1)} copy-done((bf16[256,3,256]{2,0,1:T(8,128)(2,1)S(1)}, bf16[256,3,256]{2,0,1:T(8,128)(2,1)}, u32[]{:S(2)}) %copy-start.3) | copy-done | bytes 393240
  1.0 0.9 %copy-done.4 = f32[256,256]{1,0:T(8,128)S(1)} copy-done((f32[256,256]{1,0:T(8,128)S(1)}, f32[256,256]{1,0:T(8,128)}, u32[]{:S(2)}) %copy-start.4) | copy-done | bytes 262168
  1.9 0.9 %copy-done.9 = bf16[256,256]{1,0:T(8,128)(2,1)S(1)} copy-done((bf16[256,256]{1,0:T(8,128)(2,1)S(1)}, bf16[256,256]{1,0:T(8,128)(2,1)}, u32[]{:S(2)}) %copy-start.9) | copy-done | bytes 131096
  2.9 1.1 %shard_map.127 = bf16[32,64,128]{2,1,0:T(8,128)(2,1)} custom-call(bf16[3,256,256]{2,1,0:T(8,128)(2,1)S(1)} %bitcast.5, f32[256,256]{1,0:T(8,128)S(1)} %copy-done.4, bf16[256,256]{1,0:T(8,128)(2,1)S(1)} %copy-done.9), custom_call_target="tpu_custom_call" | custom-call | tf_op jit(solution)/shard_map/pallas_call | solution.py:145
  4.0 9.7 %all-to-all-start = ((bf16[32,64,128]{2,1,0:T(8,128)(2,1)}), bf16[32,64,128]{2,1,0:T(8,128)(2,1)S(1)}, u32[]{:S(2)}, u32[]{:S(2)}) async-start(bf16[32,64,128]{2,1,0:T(8,128)(2,1)} %shard_map.127), calls=%async_computation | async-start | bytes 1048576 | tf_op jit(solution)/shard_map/all_to_all | solution.py:158
  13.7 0.0 copy-done
  13.8 2.8 %collective-permute-start.1 = (bf16[256,1024]{1,0:T(8,128)(2,1)S(1)}, bf16[256,1024]{1,0:T(8,128)(2,1)S(1)}, u32[]{:S(2)}, u32[]{:S(2)}) collective-permute-start(bf16[256,1024]{1,0:T(8,128)(2,1)S(1)} %copy-done), channel_id=1, source_target_pairs={{0,2},{1,3},{2,0},{3,1},{4,6},{5,7},{6,4},{7,5},{8,10},{9,11},{10,... | collective-permute-start | bytes 1572872 | tf_op jit(solution)/shard_map/ppermute | solution.py:156
  16.6 0.9 %collective-permute-start = (bf16[256,1024]{1,0:T(8,128)(2,1)S(1)}, bf16[256,1024]{1,0:T(8,128)(2,1)S(1)}, u32[]{:S(2)}, u32[]{:S(2)}) collective-permute-start(bf16[256,1024]{1,0:T(8,128)(2,1)S(1)} %copy-done), channel_id=1, source_target_pairs={{0,3},{1,0},{2,1},{3,2},{4,7},{5,4},{6,5},{7,6},{8,11},{9,8},{10,9... | collective-permute-start | bytes 1572872 | tf_op jit(solution)/shard_map/ppermute | solution.py:156
  17.4 0.6 %collective-permute-start.2 = (bf16[256,1024]{1,0:T(8,128)(2,1)S(1)}, bf16[256,1024]{1,0:T(8,128)(2,1)S(1)}, u32[]{:S(2)}, u32[]{:S(2)}) collective-permute-start(bf16[256,1024]{1,0:T(8,128)(2,1)S(1)} %copy-done), channel_id=1, source_target_pairs={{0,1},{1,2},{2,3},{3,0},{4,5},{5,6},{6,7},{7,4},{8,9},{9,10},{10,1... | collective-permute-start | bytes 1572872 | tf_op jit(solution)/shard_map/ppermute | solution.py:156
  18.0 0.7 %reshape.12.taps_ref = f32[9,256]{1,0:T(8,128)S(1)} reshape(f32[3,3,256]{2,1,0:T(4,128)} %param.14) | data formatting | bytes 18432 | tf_op jit(solution)/shard_map/reshape | solution.py:163
  18.8 6.6 %all-to-all-done.got_ref = bf16[32,64,128]{2,1,0:T(8,128)(2,1)S(1)} async-done(((bf16[32,64,128]{2,1,0:T(8,128)(2,1)}), bf16[32,64,128]{2,1,0:T(8,128)(2,1)S(1)}, u32[]{:S(2)}, u32[]{:S(2)}) %all-to-all-start) | async-done | bytes 524320 | tf_op jit(solution)/shard_map/all_to_all | solution.py:158
  25.4 0.0 copy-done.5
  25.4 0.7 %copy-done.11 = f32[256]{0:T(256)S(1)} copy-done((f32[256]{0:T(256)S(1)}, f32[256]{0:T(256)}, u32[]{:S(2)}) %copy-start.11) | copy-done | bytes 1048
  26.0 1.0 %copy-done.2 = bf16[512,512]{1,0:T(8,128)(2,1)S(1)} copy-done((bf16[512,512]{1,0:T(8,128)(2,1)S(1)}, bf16[512,512]{1,0:T(8,128)(2,1)}, u32[]{:S(2)}) %copy-start.2) | copy-done | bytes 524312
  27.1 0.9 %copy-done.6 = bf16[512,256]{1,0:T(8,128)(2,1)S(1)} copy-done((bf16[512,256]{1,0:T(8,128)(2,1)S(1)}, bf16[512,256]{1,0:T(8,128)(2,1)}, u32[]{:S(2)}) %copy-start.6) | copy-done | bytes 262168
  28.0 0.9 %copy-done.7 = f32[256,256]{1,0:T(8,128)S(1)} copy-done((f32[256,256]{1,0:T(8,128)S(1)}, f32[256,256]{1,0:T(8,128)}, u32[]{:S(2)}) %copy-start.7) | copy-done | bytes 262168
  29.0 0.9 %copy-done.8 = f32[256,256]{1,0:T(8,128)S(1)} copy-done((f32[256,256]{1,0:T(8,128)S(1)}, f32[256,256]{1,0:T(8,128)}, u32[]{:S(2)}) %copy-start.8) | copy-done | bytes 262168
  29.9 2.5 %shard_map.128 = bf16[512,128]{1,0:T(8,128)(2,1)} custom-call(bf16[32,64,128]{2,1,0:T(8,128)(2,1)S(1)} %all-to-all-done.got_ref, f32[9,256]{1,0:T(8,128)S(1)} %reshape.12.taps_ref, f32[1,256]{1,0:T(1,128)S(1)} %bitcast.6, bf16[512,256]{1,0:T(8,128)(2,1)S(1)} %copy-done.6, bf16[256,512]{1,0:T(8,128)(2,1)S(1)} %copy-done.5, bf16[512,512]{1,0:T(8,128)(2,1)S(1)} %copy-done.2, ...), custom_call_target="tpu_custom_call" | custom-call | tf_op jit(solution)/shard_map/pallas_call | solution.py:145
  32.4 5.5 %all-to-all-start.1 = ((bf16[128,4,128]{2,1,0:T(4,128)(2,1)}), bf16[128,4,128]{2,1,0:T(4,128)(2,1)S(1)}, u32[]{:S(2)}, u32[]{:S(2)}) async-start(bf16[128,4,128]{2,1,0:T(4,128)(2,1)} %bitcast.2), calls=%async_computation.1 | async-start | bytes 262144 | tf_op jit(solution)/shard_map/all_to_all | solution.py:167
  37.9 0.0 collective-permute-done.1.w2_ref
  37.9 2.0 %collective-permute-done.w1_ref = bf16[256,1024]{1,0:T(8,128)(2,1)S(1)} collective-permute-done((bf16[256,1024]{1,0:T(8,128)(2,1)S(1)}, bf16[256,1024]{1,0:T(8,128)(2,1)S(1)}, u32[]{:S(2)}, u32[]{:S(2)}) %collective-permute-start) | collective-permute-done | bytes 524320 | tf_op jit(solution)/shard_map/ppermute | solution.py:156
  40.0 0.4 collective-permute-done.2.w3_ref
  40.4 7.3 %all-to-all-done.1 = bf16[128,4,128]{2,1,0:T(4,128)(2,1)S(1)} async-done(((bf16[128,4,128]{2,1,0:T(4,128)(2,1)}), bf16[128,4,128]{2,1,0:T(4,128)(2,1)S(1)}, u32[]{:S(2)}, u32[]{:S(2)}) %all-to-all-start.1) | async-done | bytes 131104 | tf_op jit(solution)/shard_map/all_to_all | solution.py:167
  47.7 1.2 %shard_map.129 = bf16[64,1024]{1,0:T(8,128)(2,1)} custom-call(bf16[512,128]{1,0:T(8,128)(2,1)S(1)} %bitcast.4, bf16[256,1024]{1,0:T(8,128)(2,1)S(1)} %copy-done, bf16[256,1024]{1,0:T(8,128)(2,1)S(1)} %collective-permute-done.w1_ref, bf16[256,1024]{1,0:T(8,128)(2,1)S(1)} %collective-permute-done.1.w2_ref, bf16[256,1024]{1,0:T(8,128)(2,1)S(1)} %collective-permute-done.2.w3_ref), custom_call_target="tpu_custom_call" | custom-call | tf_op jit(solution)/shard_map/pallas_call | solution.py:145
  (14 shorter events, 0.0 us)
Async XLA Ops:
  0.0 1.0 %copy-start.3 = (bf16[256,3,256]{2,0,1:T(8,128)(2,1)S(1)}, bf16[256,3,256]{2,0,1:T(8,128)(2,1)}, u32[]{:S(2)}) copy-start(bf16[256,3,256]{2,0,1:T(8,128)(2,1)} %param.13) | copy-start | bytes 1179652
  1.0 0.9 %copy-start.4 = (f32[256,256]{1,0:T(8,128)S(1)}, f32[256,256]{1,0:T(8,128)}, u32[]{:S(2)}) copy-start(f32[256,256]{1,0:T(8,128)} %filters_ref.1) | copy-start | bytes 786436
  1.9 0.9 %copy-start.9 = (bf16[256,256]{1,0:T(8,128)(2,1)S(1)}, bf16[256,256]{1,0:T(8,128)(2,1)}, u32[]{:S(2)}) copy-start(bf16[256,256]{1,0:T(8,128)(2,1)} %constant.24.pick_ref) | copy-start | bytes 393220
  2.9 22.5 %copy-start.5 = (bf16[256,512]{1,0:T(8,128)(2,1)S(1)}, bf16[256,512]{1,0:T(8,128)(2,1)}, u32[]{:S(2)}) copy-start(bf16[256,512]{1,0:T(8,128)(2,1)} %constant.26.back_ref) | copy-start | bytes 786436
  2.9 22.5 %copy-start.10 = (bf16[256,256]{1,0:T(8,128)(2,1)S(1)}, bf16[256,256]{1,0:T(8,128)(2,1)}, u32[]{:S(2)}) copy-start(bf16[256,256]{1,0:T(8,128)(2,1)} %constant.29.order_ref) | copy-start | bytes 393220
  4.0 9.8 %copy-start = (bf16[256,1024]{1,0:T(8,128)(2,1)S(1)}, bf16[256,1024]{1,0:T(8,128)(2,1)}, u32[]{:S(2)}) copy-start(bf16[256,1024]{1,0:T(8,128)(2,1)} %w0_ref.1) | copy-start | bytes 1572868
  4.0 21.4 %copy-start.1 = (bf16[512,512]{1,0:T(8,128)(2,1)S(1)}, bf16[512,512]{1,0:T(8,128)(2,1)}, u32[]{:S(2)}) copy-start(bf16[512,512]{1,0:T(8,128)(2,1)} %constant.28.gather_ref) | copy-start | bytes 1572868
  4.0 21.4 %all-to-all-start = ((bf16[32,64,128]{2,1,0:T(8,128)(2,1)}), bf16[32,64,128]{2,1,0:T(8,128)(2,1)S(1)}, u32[]{:S(2)}, u32[]{:S(2)}) async-start(bf16[32,64,128]{2,1,0:T(8,128)(2,1)} %shard_map.127), calls=%async_computation | async-start | bytes 1048576 | tf_op jit(solution)/shard_map/all_to_all | solution.py:158
  13.8 24.2 %collective-permute-start.1 = (bf16[256,1024]{1,0:T(8,128)(2,1)S(1)}, bf16[256,1024]{1,0:T(8,128)(2,1)S(1)}, u32[]{:S(2)}, u32[]{:S(2)}) collective-permute-start(bf16[256,1024]{1,0:T(8,128)(2,1)S(1)} %copy-done), channel_id=1, source_target_pairs={{0,2},{1,3},{2,0},{3,1},{4,6},{5,7},{6,4},{7,5},{8,10},{9,11},{10,... | collective-permute-start | bytes 1572872 | tf_op jit(solution)/shard_map/ppermute | solution.py:156
  16.6 23.4 %collective-permute-start = (bf16[256,1024]{1,0:T(8,128)(2,1)S(1)}, bf16[256,1024]{1,0:T(8,128)(2,1)S(1)}, u32[]{:S(2)}, u32[]{:S(2)}) collective-permute-start(bf16[256,1024]{1,0:T(8,128)(2,1)S(1)} %copy-done), channel_id=1, source_target_pairs={{0,3},{1,0},{2,1},{3,2},{4,7},{5,4},{6,5},{7,6},{8,11},{9,8},{10,9... | collective-permute-start | bytes 1572872 | tf_op jit(solution)/shard_map/ppermute | solution.py:156
  17.4 23.0 %collective-permute-start.2 = (bf16[256,1024]{1,0:T(8,128)(2,1)S(1)}, bf16[256,1024]{1,0:T(8,128)(2,1)S(1)}, u32[]{:S(2)}, u32[]{:S(2)}) collective-permute-start(bf16[256,1024]{1,0:T(8,128)(2,1)S(1)} %copy-done), channel_id=1, source_target_pairs={{0,1},{1,2},{2,3},{3,0},{4,5},{5,6},{6,7},{7,4},{8,9},{9,10},{10,1... | collective-permute-start | bytes 1572872 | tf_op jit(solution)/shard_map/ppermute | solution.py:156
  25.4 0.7 %copy-start.11 = (f32[256]{0:T(256)S(1)}, f32[256]{0:T(256)}, u32[]{:S(2)}) copy-start(f32[256]{0:T(256)} %param.16) | copy-start | bytes 3076
  26.0 1.0 %copy-start.2 = (bf16[512,512]{1,0:T(8,128)(2,1)S(1)}, bf16[512,512]{1,0:T(8,128)(2,1)}, u32[]{:S(2)}) copy-start(bf16[512,512]{1,0:T(8,128)(2,1)} %constant.27.spread_ref) | copy-start | bytes 1572868
  27.1 0.9 %copy-start.6 = (bf16[512,256]{1,0:T(8,128)(2,1)S(1)}, bf16[512,256]{1,0:T(8,128)(2,1)}, u32[]{:S(2)}) copy-start(bf16[512,256]{1,0:T(8,128)(2,1)} %constant.25.ahead_ref) | copy-start | bytes 786436
  28.0 0.9 %copy-start.7 = (f32[256,256]{1,0:T(8,128)S(1)}, f32[256,256]{1,0:T(8,128)}, u32[]{:S(2)}) copy-start(f32[256,256]{1,0:T(8,128)} %constant.21.clone.sin_ref) | copy-start | bytes 786436
  29.0 0.9 %copy-start.8 = (f32[256,256]{1,0:T(8,128)S(1)}, f32[256,256]{1,0:T(8,128)}, u32[]{:S(2)}) copy-start(f32[256,256]{1,0:T(8,128)} %constant.20.clone.cos_ref) | copy-start | bytes 786436
  32.4 15.3 %all-to-all-start.1 = ((bf16[128,4,128]{2,1,0:T(4,128)(2,1)}), bf16[128,4,128]{2,1,0:T(4,128)(2,1)S(1)}, u32[]{:S(2)}, u32[]{:S(2)}) async-start(bf16[128,4,128]{2,1,0:T(4,128)(2,1)} %bitcast.2), calls=%async_computation.1 | async-start | bytes 262144 | tf_op jit(solution)/shard_map/all_to_all | solution.py:167

commit v2 on v1

v2 whole, which is shorter than its diff:
```python
import math

import jax
import jax.numpy as jnp
import numpy as np
from jax import lax
from jax.experimental import pallas as pl
from jax.experimental.pallas import tpu as pltpu
from jax.sharding import PartitionSpec as P

BLOCKS = 32
SPAN = 256
OWN = 8
BF = jnp.bfloat16
F32 = jnp.float32


def dot(left, right):
    return jnp.dot(left, right, preferred_element_type=F32)


def constants():
    total = BLOCKS * SPAN
    low = np.arange(BLOCKS)[:, None] + 0.25
    coarse = 2 * math.pi / BLOCKS * low * np.arange(BLOCKS)[None, :]
    eye = np.eye(OWN)
    ahead = np.concatenate([np.kron(np.cos(coarse), eye), np.kron(-np.sin(coarse), eye)], axis=0)
    back = ahead.T / total
    turn = 2 * math.pi / total * low * np.arange(SPAN)[None, :]
    turn = np.repeat(turn, OWN, axis=0)
    fine = 2 * math.pi / SPAN * (np.arange(SPAN)[:, None] * np.arange(SPAN)[None, :] % SPAN)
    as_bf = lambda table: jnp.asarray(table.astype(np.float32)).astype(BF)
    return dict(
        ahead=as_bf(ahead),
        back=as_bf(back),
        fine=as_bf(np.concatenate([np.cos(fine), np.sin(fine)], axis=0)),
        turn=as_bf(np.concatenate([np.cos(turn), np.sin(turn)], axis=0)),
    )


def message_order(transposed):
    row = lax.broadcasted_iota(jnp.int32, (SPAN, SPAN), 0)
    column = lax.broadcasted_iota(jnp.int32, (SPAN, SPAN), 1)
    if transposed:
        row, column = column, row
    place = 128 * ((row >> 2) & 1) + 4 * (row >> 3) + (row & 3)
    return jnp.where(place == column, 1.0, 0.0).astype(BF)


def pack_kernel(projected_ref, filters_ref, out_ref, rows_ref, taps_ref, sent_ref, in_sems, out_sems):
    reads = []
    for which in (3, 0, 1, 2):
        source = projected_ref.at[which] if which < 3 else filters_ref
        target = rows_ref.at[which] if which < 3 else taps_ref
        reads.append((which, pltpu.make_async_copy(source, target, in_sems.at[which])))
    for _, read in reads:
        read.start()
    pick = message_order(False)
    writes = []
    for which, read in reads:
        read.wait()
        rows = rows_ref[which] if which < 3 else taps_ref[...].astype(BF)
        turned = lax.dot_general(pick, rows, (((1,), (1,)), ((), ())), preferred_element_type=F32)
        first = turned[:, :128].reshape(BLOCKS, OWN, 128)
        second = turned[:, 128:].reshape(BLOCKS, OWN, 128)
        sent_ref[which] = jnp.concatenate([first, second], axis=1).astype(BF)
        write = pltpu.make_async_copy(
            sent_ref.at[which], out_ref.at[:, pl.ds(16 * which, 16), :], out_sems.at[which]
        )
        write.start()
        writes.append(write)
    for write in writes:
        write.wait()


def conv_kernel(got_ref, taps_hbm, skip_hbm, ahead_hbm, fine_hbm, turn_hbm, back_hbm, out_ref, *scratch):
    taps_ref, skip_ref, ahead_ref, fine_ref, turn_ref, back_ref, sems = scratch
    reads = []
    for n, (source, target) in enumerate(
        zip((ahead_hbm, taps_hbm, turn_hbm, fine_hbm, skip_hbm, back_hbm),
            (ahead_ref, taps_ref, turn_ref, fine_ref, skip_ref, back_ref))
    ):
        reads.append(pltpu.make_async_copy(source, target, sems.at[n]))
        reads[-1].start()
    ahead_read, taps_read, turn_read, fine_read, skip_read, back_read = reads

    place = lax.axis_index("seq")
    lane = lax.broadcasted_iota(jnp.int32, (OWN, SPAN), 1)
    row = lax.broadcasted_iota(jnp.int32, (OWN, SPAN), 0)
    mine = lane == 128 * (row >> 2) + 4 * place + (row & 3)

    def own(values):
        return jnp.sum(jnp.where(mine, values, 0.0), axis=1, keepdims=True)[None]

    def block(which):
        both = got_ref[:, 16 * which : 16 * which + 16, :].astype(F32)
        first = both[:, :8].reshape(SPAN, 128)
        second = both[:, 8:].reshape(SPAN, 128)
        return jnp.concatenate([first, second], axis=1)

    wide_lane = lax.broadcasted_iota(jnp.int32, (SPAN, SPAN), 1)

    def later(rows, by):
        turned = pltpu.roll(rows, by, 1)
        earlier = jnp.concatenate([jnp.zeros((OWN, SPAN), F32), turned[:-OWN]], axis=0)
        return jnp.where(wide_lane < by, earlier, turned)

    def shaped(which):
        rows = block(which)
        total = None
        for tap, moved in enumerate((rows, later(rows, 1), later(rows, 2))):
            gain = own(taps_ref[tap, which : which + 1, :])
            term = moved.reshape(BLOCKS, OWN, SPAN) * gain
            total = term if total is None else total + term
        return total.reshape(SPAN, SPAN)

    response = block(3).astype(BF)
    taps_read.wait()
    signal = (shaped(1) * shaped(2)).astype(BF)
    ahead_read.wait()
    res_half = dot(ahead_ref[...], response)
    sig_half = dot(ahead_ref[...], signal)
    turn_read.wait()
    cos, sin = turn_ref[:SPAN].astype(F32), turn_ref[SPAN:].astype(F32)
    fine_read.wait()
    fine_cos, fine_sin = fine_ref[:SPAN], fine_ref[SPAN:]
    fine_less = -fine_sin
    spread = jnp.concatenate(
        [jnp.concatenate([fine_cos, fine_less], axis=1), jnp.concatenate([fine_sin, fine_cos], axis=1)], axis=0
    )
    gather = jnp.concatenate(
        [jnp.concatenate([fine_cos, fine_sin], axis=1), jnp.concatenate([fine_less, fine_cos], axis=1)], axis=0
    )

    def spectrum(half):
        real, imag = half[:SPAN], half[SPAN:]
        turned = jnp.concatenate([real * cos + imag * sin, imag * cos - real * sin], axis=1)
        both = dot(turned.astype(BF), spread)
        return both[:, :SPAN], both[:, SPAN:]

    res_real, res_imag = spectrum(res_half)
    sig_real, sig_imag = spectrum(sig_half)
    product = jnp.concatenate(
        [sig_real * res_real - sig_imag * res_imag, sig_real * res_imag + sig_imag * res_real], axis=1
    )
    both = dot(product.astype(BF), gather)
    real, imag = both[:, :SPAN], both[:, SPAN:]
    turned = jnp.concatenate([real * cos - imag * sin, real * sin + imag * cos], axis=0)
    skip_read.wait()
    back_read.wait()
    conv = dot(back_ref[...], turned.astype(BF))
    skip = own(skip_ref[...])
    direct = (signal.astype(F32).reshape(BLOCKS, OWN, SPAN) * skip).reshape(SPAN, SPAN)
    gated = (shaped(0) * (conv + direct)).astype(BF)
    gated = dot(message_order(True), gated)
    half = lax.broadcasted_iota(jnp.int32, (128, 128), 1) < 64
    for h in range(2):
        low = gated[:128, 128 * h : 128 * h + 128]
        high = gated[128:, 128 * h : 128 * h + 128]
        even = jnp.where(half, low, pltpu.roll(high, 64, 1))
        odd = jnp.where(half, pltpu.roll(low, 64, 1), high)
        out_ref[256 * h : 256 * h + 128, :] = even.astype(BF)
        out_ref[256 * h + 128 : 256 * h + 256, :] = odd.astype(BF)


def project_kernel(got_ref, own_ref, near_ref, swap_ref, far_ref, far_swap_ref, out_ref):
    place = lax.axis_index("chan")
    odd = lax.axis_index("seq") % 2

    def halves(step):
        owner = lax.rem(place + step, 4)
        rows = got_ref[pl.ds(pl.multiple_of(owner * 128, 128), 128), :].astype(F32).T
        return rows[:64], rows[64:]

    total = None
    for step, weight_ref in ((0, own_ref), (1 + 2 * odd, near_ref), (3 - 2 * odd, swap_ref)):
        term = dot(jnp.concatenate(halves(step), axis=1).astype(BF), weight_ref[...])
        total = term if total is None else total + term
    low, high = halves(2)
    total = total + dot(jnp.where(odd == 0, low, high).astype(BF), far_ref[...])
    total = total + dot(jnp.where(odd == 0, high, low).astype(BF), far_swap_ref[...])
    out_ref[...] = total.astype(BF)


HBM = pl.BlockSpec(memory_space=pltpu.HBM)
VMEM = pl.BlockSpec(memory_space=pltpu.VMEM)
PARAMS = pltpu.CompilerParams(vmem_limit_bytes=32 * 1024 * 1024)


TINY = pl.CostEstimate(flops=1000, bytes_accessed=1000, transcendentals=0)


def pack(projected, filters):
    return pl.pallas_call(
        pack_kernel,
        out_shape=jax.ShapeDtypeStruct((BLOCKS, 64, 128), BF),
        in_specs=[HBM, HBM],
        out_specs=HBM,
        scratch_shapes=[
            pltpu.VMEM((3, SPAN, SPAN), BF),
            pltpu.VMEM((SPAN, SPAN), F32),
            pltpu.VMEM((4, BLOCKS, 16, 128), BF),
            pltpu.SemaphoreType.DMA((4,)),
            pltpu.SemaphoreType.DMA((4,)),
        ],
        cost_estimate=TINY,
    )(projected.transpose(1, 0, 2), filters)


def convolve(got, short_taps, skip_gain):
    table = constants()
    held = [short_taps, skip_gain.reshape(1, SPAN)] + [table[name] for name in ("ahead", "fine", "turn", "back")]
    return pl.pallas_call(
        conv_kernel,
        out_shape=jax.ShapeDtypeStruct((512, 128), BF),
        in_specs=[VMEM] + [HBM] * 6,
        out_specs=VMEM,
        scratch_shapes=[pltpu.VMEM(array.shape, array.dtype) for array in held] + [pltpu.SemaphoreType.DMA((6,))],
        compiler_params=PARAMS,
        cost_estimate=TINY,
    )(got, *held)


def project(got, weights):
    return pl.pallas_call(
        project_kernel,
        out_shape=jax.ShapeDtypeStruct((64, 1024), BF),
        in_specs=[VMEM] * (1 + len(weights)),
        out_specs=VMEM,
        compiler_params=PARAMS,
        cost_estimate=TINY,
    )(got, *weights)


def on_device(projected, short_taps, filters, skip_gain, out_weight):
    near = lax.ppermute(
        out_weight,
        ("seq", "chan"),
        [(s * 4 + (j + (1 if s % 2 == 0 else 3)) % 4, s * 4 + j) for s in range(BLOCKS) for j in range(4)],
    )
    half = lax.dynamic_slice_in_dim(out_weight, 128 * (lax.axis_index("seq") % 2), 128, 0)
    far = lax.ppermute(half, "chan", [(j, (j + 2) % 4) for j in range(4)])
    got = lax.all_to_all(pack(projected, filters), "seq", split_axis=0, concat_axis=0, tiled=True)
    gated = convolve(got, short_taps, skip_gain)
    gated, near, far = lax.optimization_barrier((gated, near, far))
    pairs = [(s, s ^ 1) for s in range(BLOCKS)]
    weights = (out_weight, near, lax.ppermute(near, "seq", pairs), far, lax.ppermute(far, "seq", pairs))
    got = lax.all_to_all(gated.reshape(128, 4, 128), ("chan", "seq"), split_axis=0, concat_axis=0, tiled=True)
    return project(got.reshape(512, 128), weights)


def solution(mesh):
    return jax.shard_map(
        on_device,
        mesh=mesh,
        in_specs=(
            P("seq", None, "chan"),
            P(None, None, "chan"),
            P("seq", "chan"),
            P("chan"),
            P("chan", None),
        ),
        out_specs=P(("seq", "chan"), None),
        check_vma=False,
    )
```

time: 49.4 us -> 44.2 us (0.89)
  blocking collectives: 0 us -> 13.1 us
  local copies, waits for them, and re-layouts: 8.14 us -> 0.07 us
  starting transfers between devices: 19.5 us -> 13.7 us
  waiting for transfers between devices: 16.3 us -> 10.9 us
  Pallas kernels: 4.82 us -> 6.05 us
    all_to_all x0 -> x1, blocking collectives: none -> 13.1 us  [on_device(): lax.all_to_all(gated.reshape(128, 4, 128), ('chan', 'seq'), split_axis=0,...]
    unnamed x24 -> x14, local copies, waits for them, and re-layouts: 7.42 us -> 0.05 us
    all_to_all x2 -> x1, starting transfers between devices: 15.3 us -> 10.5 us  [on_device(): lax.all_to_all(pack(projected, filters), 'seq', split_axis=0, concat_axis...]
    all_to_all x2 -> x1, waiting for transfers between devices: 13.9 us -> 10.9 us  [on_device(): lax.all_to_all(pack(projected, filters), 'seq', split_axis=0, concat_axis...]
    ppermute x3 -> x4, waiting for transfers between devices: 2.47 us -> 0.01 us  [the longest x1 0.01 us: on_device(): far = lax.ppermute(half, 'chan', [(j, (j + 2) % 4) for j in range(4)])]
    pallas_call x3, Pallas kernels: 4.82 us -> 6.05 us  [the longest x1 2.72 us: pack(): pl.pallas_call(pack_kernel, out_shape=jax.ShapeDtypeStruct((BLOCKS, 64, 1...]
    ppermute x3 -> x4, starting transfers between devices: 4.28 us -> 3.22 us  [the longest x1 2.04 us: on_device(): lax.ppermute(out_weight, ('seq', 'chan'), [(s * 4 + (j + (1 if s % 2 == 0...]
    reshape x1 -> x0, local copies, waits for them, and re-layouts: 0.72 us -> none  [on_device(): short_taps.reshape(9, SPAN)]
  transfers between devices with their start and end apart: 5 -> 5, of which waited for: 4 -> 1; matrix products, arithmetic and copies ran while one was open for 1% -> 0% of each run, Pallas kernels for 5% -> 11%
where the time goes in v2:
time: 44.2 us; the launch traced here: 44 us
  starting transfers between devices  13.7 us (31%)
  blocking collectives  13.1 us (30%)
  waiting for transfers between devices  10.9 us (25%)
  Pallas kernels  6.05 us (14%)
    all_to_all x1, blocking collectives, on_device(): lax.all_to_all(gated.reshape(128, 4, 128), ('chan', 'seq'), split_axis=0,...  13.1 us
    all_to_all x1, waiting for transfers between devices, on_device(): lax.all_to_all(pack(projected, filters), 'seq', split_axis=0, concat_axis...  10.9 us
    all_to_all x1, starting transfers between devices, on_device(): lax.all_to_all(pack(projected, filters), 'seq', split_axis=0, concat_axis...  10.5 us
    pallas_call x1, Pallas kernels, pack(): pl.pallas_call(pack_kernel, out_shape=jax.ShapeDtypeStruct((BLOCKS, 64, 1...  2.72 us
    pallas_call x1, Pallas kernels, convolve(): pl.pallas_call(conv_kernel, out_shape=jax.ShapeDtypeStruct((512, 128), BF...  2.11 us
    ppermute x1, starting transfers between devices, on_device(): lax.ppermute(out_weight, ('seq', 'chan'), [(s * 4 + (j + (1 if s % 2 == 0...  2.04 us
    pallas_call x1, Pallas kernels, project(): pl.pallas_call(project_kernel, out_shape=jax.ShapeDtypeStruct((64, 1024),...  1.22 us
  transfers between devices with their start and end apart: 5, of which 1 were waited for; matrix products, arithmetic and copies ran while one was open for 0% of the time, Pallas kernels for 11%

profile of v2, /device:TPU:1, one launch (start us, length us, event | category | flops | bytes accessed | tf_op | source)
XLA Modules:
  0.0 44.0 jit_solution(4435766112159896976)
XLA Ops:
  0.0 2.0 %collective-permute-start = (bf16[256,1024]{1,0:T(8,128)(2,1)}, bf16[256,1024]{1,0:T(8,128)(2,1)S(1)}, u32[]{:S(2)}, u32[]{:S(2)}) collective-permute-start(bf16[256,1024]{1,0:T(8,128)(2,1)} %own_ref.1), channel_id=1, source_target_pairs={{1,0},{2,1},{3,2},{0,3},{7,4},{4,5},{5,6},{6,7},{9,8},{10,9},{11,1... | collective-permute-start | bytes 1572872 | tf_op jit(solution)/shard_map/ppermute | solution.py:236
  2.0 2.7 %shard_map.91 = bf16[32,64,128]{2,1,0:T(8,128)(2,1)} custom-call(bf16[3,256,256]{2,1,0:T(8,128)(2,1)} %bitcast.7, f32[256,256]{1,0:T(8,128)} %filters_ref.1), custom_call_target="tpu_custom_call" | custom-call | flops 1000 | bytes 1000 | tf_op jit(solution)/shard_map/pallas_call | solution.py:194
  4.8 0.0 copy-start
  4.8 0.0 copy-start.3
  4.8 0.0 copy-start.4
  4.8 10.5 %all-to-all-start = ((bf16[32,64,128]{2,1,0:T(8,128)(2,1)}), bf16[32,64,128]{2,1,0:T(8,128)(2,1)S(1)}, u32[]{:S(2)}, u32[]{:S(2)}) async-start(bf16[32,64,128]{2,1,0:T(8,128)(2,1)} %shard_map.91), calls=%async_computation | async-start | bytes 1048576 | tf_op jit(solution)/shard_map/all_to_all | solution.py:243
  15.3 0.0 copy-start.5
  15.3 0.0 copy-done
  15.3 0.0 copy-start.1
  15.3 0.0 copy-start.2
  15.4 0.0 copy-start.6
  15.4 0.6 %collective-permute-start.1 = (bf16[128,1024]{1,0:T(8,128)(2,1)S(1)}, bf16[128,1024]{1,0:T(8,128)(2,1)S(1)}, u32[]{:S(2)}, u32[]{:S(2)}) collective-permute-start(bf16[128,1024]{1,0:T(8,128)(2,1)S(1)} %constant_dynamic-slice_fusion), channel_id=1, source_target_pairs={{0,2},{1,3},{2,0},{3,1},{4,6},{5,7},{6,4},{7,5},{8,10},{9,11},{10,... | collective-permute-start | bytes 786440 | tf_op jit(solution)/shard_map/ppermute | solution.py:242
  16.0 10.9 %all-to-all-done.got_ref = bf16[32,64,128]{2,1,0:T(8,128)(2,1)S(1)} async-done(((bf16[32,64,128]{2,1,0:T(8,128)(2,1)}), bf16[32,64,128]{2,1,0:T(8,128)(2,1)S(1)}, u32[]{:S(2)}, u32[]{:S(2)}) %all-to-all-start) | async-done | bytes 524320 | tf_op jit(solution)/shard_map/all_to_all | solution.py:243
  26.9 0.0 copy-done.3
  26.9 0.0 copy-done.4
  26.9 2.1 %shard_map.92 = bf16[512,128]{1,0:T(8,128)(2,1)S(1)} custom-call(bf16[32,64,128]{2,1,0:T(8,128)(2,1)S(1)} %all-to-all-done.got_ref, f32[3,3,256]{2,1,0:T(4,128)S(1)} %copy-done.5, f32[1,256]{1,0:T(1,128)S(1)} %bitcast.6, bf16[512,256]{1,0:T(8,128)(2,1)S(1)} %copy-done.4, bf16[512,256]{1,0:T(8,128)(2,1)S(1)} %copy-done.3, bf16[512,256]{1,0:T(8,128)(2,1)S(1)} %copy-done.2, ...), custom_call_target="tpu_custom_call" | custom-call | flops 1000 | bytes 1000 | tf_op jit(solution)/shard_map/pallas_call | solution.py:213
  29.1 0.0 collective-permute-done.1.far_ref
  29.1 0.0 collective-permute-done.near_ref
  29.1 0.1 collective-permute-start.2
  29.2 0.5 %collective-permute-start.3 = (bf16[128,1024]{1,0:T(8,128)(2,1)S(1)}, bf16[128,1024]{1,0:T(8,128)(2,1)S(1)}, u32[]{:S(2)}, u32[]{:S(2)}) collective-permute-start(bf16[128,1024]{1,0:T(8,128)(2,1)S(1)} %collective-permute-done.1.far_ref), channel_id=1, source_target_pairs={{0,4},{4,0},{8,12},{12,8},{16,20},{20,16},{24,28},{28,24},{32,36},... | collective-permute-start | bytes 786440 | tf_op jit(solution)/shard_map/ppermute | solution.py:247
  29.7 13.1 %all_to_all.10 = bf16[128,4,128]{2,1,0:T(4,128)(2,1)S(1)} all-to-all(bf16[128,4,128]{2,1,0:T(4,128)(2,1)S(1)} %bitcast.4), channel_id=1, replica_groups=mesh['seq'=32,'chan'=4] {'chan','seq'}, dimensions={0} | all-to-all | bytes 262144 | tf_op jit(solution)/shard_map/all_to_all | solution.py:248
  42.7 0.0 collective-permute-done.3.far_swap_ref
  42.7 0.0 collective-permute-done.2.swap_ref
  42.7 1.2 %shard_map.93 = bf16[64,1024]{1,0:T(8,128)(2,1)} custom-call(bf16[512,128]{1,0:T(8,128)(2,1)S(1)} %bitcast.5, bf16[256,1024]{1,0:T(8,128)(2,1)S(1)} %copy-done, bf16[256,1024]{1,0:T(8,128)(2,1)S(1)} %collective-permute-done.near_ref, bf16[256,1024]{1,0:T(8,128)(2,1)S(1)} %collective-permute-done.2.swap_ref, ...), custom_call_target="tpu_custom_call" | custom-call | flops 1000 | bytes 1000 | tf_op jit(solution)/shard_map/pallas_call | solution.py:225
  (5 shorter events, 0.0 us)
Async XLA Ops:
  0.0 29.1 %collective-permute-start = (bf16[256,1024]{1,0:T(8,128)(2,1)}, bf16[256,1024]{1,0:T(8,128)(2,1)S(1)}, u32[]{:S(2)}, u32[]{:S(2)}) collective-permute-start(bf16[256,1024]{1,0:T(8,128)(2,1)} %own_ref.1), channel_id=1, source_target_pairs={{1,0},{2,1},{3,2},{0,3},{7,4},{4,5},{5,6},{6,7},{9,8},{10,9},{11,1... | collective-permute-start | bytes 1572872 | tf_op jit(solution)/shard_map/ppermute | solution.py:236
  4.8 10.5 %copy-start = (bf16[256,1024]{1,0:T(8,128)(2,1)S(1)}, bf16[256,1024]{1,0:T(8,128)(2,1)}, u32[]{:S(2)}) copy-start(bf16[256,1024]{1,0:T(8,128)(2,1)} %own_ref.1) | copy-start | bytes 1572868
  4.8 22.1 %copy-start.3 = (bf16[512,256]{1,0:T(8,128)(2,1)S(1)}, bf16[512,256]{1,0:T(8,128)(2,1)}, u32[]{:S(2)}) copy-start(bf16[512,256]{1,0:T(8,128)(2,1)} %constant.37.fine_hbm) | copy-start | bytes 786436
  4.8 22.1 %copy-start.4 = (bf16[512,256]{1,0:T(8,128)(2,1)S(1)}, bf16[512,256]{1,0:T(8,128)(2,1)}, u32[]{:S(2)}) copy-start(bf16[512,256]{1,0:T(8,128)(2,1)} %constant.36.ahead_hbm) | copy-start | bytes 786436
  4.8 22.1 %all-to-all-start = ((bf16[32,64,128]{2,1,0:T(8,128)(2,1)}), bf16[32,64,128]{2,1,0:T(8,128)(2,1)S(1)}, u32[]{:S(2)}, u32[]{:S(2)}) async-start(bf16[32,64,128]{2,1,0:T(8,128)(2,1)} %shard_map.91), calls=%async_computation | async-start | bytes 1048576 | tf_op jit(solution)/shard_map/all_to_all | solution.py:243
  15.3 11.6 %copy-start.5 = (f32[3,3,256]{2,1,0:T(4,128)S(1)}, f32[3,3,256]{2,1,0:T(4,128)}, u32[]{:S(2)}) copy-start(f32[3,3,256]{2,1,0:T(4,128)} %taps_hbm.1) | copy-start | bytes 27652
  15.3 11.6 %copy-start.1 = (bf16[256,512]{1,0:T(8,128)(2,1)S(1)}, bf16[256,512]{1,0:T(8,128)(2,1)}, u32[]{:S(2)}) copy-start(bf16[256,512]{1,0:T(8,128)(2,1)} %constant.39.back_hbm) | copy-start | bytes 786436
  15.3 11.6 %copy-start.2 = (bf16[512,256]{1,0:T(8,128)(2,1)S(1)}, bf16[512,256]{1,0:T(8,128)(2,1)}, u32[]{:S(2)}) copy-start(bf16[512,256]{1,0:T(8,128)(2,1)} %constant.38.turn_hbm) | copy-start | bytes 786436
  15.4 11.6 %copy-start.6 = (f32[256]{0:T(256)S(1)}, f32[256]{0:T(256)}, u32[]{:S(2)}) copy-start(f32[256]{0:T(256)} %param.12) | copy-start | bytes 3076
  15.4 13.7 %collective-permute-start.1 = (bf16[128,1024]{1,0:T(8,128)(2,1)S(1)}, bf16[128,1024]{1,0:T(8,128)(2,1)S(1)}, u32[]{:S(2)}, u32[]{:S(2)}) collective-permute-start(bf16[128,1024]{1,0:T(8,128)(2,1)S(1)} %constant_dynamic-slice_fusion), channel_id=1, source_target_pairs={{0,2},{1,3},{2,0},{3,1},{4,6},{5,7},{6,4},{7,5},{8,10},{9,11},{10,... | collective-permute-start | bytes 786440 | tf_op jit(solution)/shard_map/ppermute | solution.py:242
  29.1 13.7 %collective-permute-start.2 = (bf16[256,1024]{1,0:T(8,128)(2,1)S(1)}, bf16[256,1024]{1,0:T(8,128)(2,1)S(1)}, u32[]{:S(2)}, u32[]{:S(2)}) collective-permute-start(bf16[256,1024]{1,0:T(8,128)(2,1)S(1)} %collective-permute-done.near_ref), channel_id=1, source_target_pairs={{0,4},{4,0},{8,12},{12,8},{16,20},{20,16},{24,28},{28,24},{32,36},... | collective-permute-start | bytes 1572872 | tf_op jit(solution)/shard_map/ppermute | solution.py:247
  29.2 13.6 %collective-permute-start.3 = (bf16[128,1024]{1,0:T(8,128)(2,1)S(1)}, bf16[128,1024]{1,0:T(8,128)(2,1)S(1)}, u32[]{:S(2)}, u32[]{:S(2)}) collective-permute-start(bf16[128,1024]{1,0:T(8,128)(2,1)S(1)} %collective-permute-done.1.far_ref), channel_id=1, source_target_pairs={{0,4},{4,0},{8,12},{12,8},{16,20},{20,16},{24,28},{28,24},{32,36},... | collective-permute-start | bytes 786440 | tf_op jit(solution)/shard_map/ppermute | solution.py:247

commit v3 on v2

--- a/solution.py
+++ b/solution.py
@@ -38,13 +38,15 @@
     )
 
 
-def message_order(transposed):
-    row = lax.broadcasted_iota(jnp.int32, (SPAN, SPAN), 0)
-    column = lax.broadcasted_iota(jnp.int32, (SPAN, SPAN), 1)
-    if transposed:
-        row, column = column, row
-    place = 128 * ((row >> 2) & 1) + 4 * (row >> 3) + (row & 3)
-    return jnp.where(place == column, 1.0, 0.0).astype(BF)
+def swap_halves(tiles):
+    count, _, columns = tiles.shape
+    pairs = tiles.reshape(count // 2, 2, 8, columns)
+    first, second = pairs[:, 0], pairs[:, 1]
+    upper = lax.broadcasted_iota(jnp.int32, first.shape, 1) < 4
+    return (
+        jnp.where(upper, first, pltpu.roll(second, 4, 1)),
+        jnp.where(upper, pltpu.roll(first, 4, 1), second),
+    )
 
 
 def pack_kernel(projected_ref, filters_ref, out_ref, rows_ref, taps_ref, sent_ref, in_sems, out_sems):
@@ -55,15 +57,14 @@
         reads.append((which, pltpu.make_async_copy(source, target, in_sems.at[which])))
     for _, read in reads:
         read.start()
-    pick = message_order(False)
     writes = []
     for which, read in reads:
         read.wait()
         rows = rows_ref[which] if which < 3 else taps_ref[...].astype(BF)
-        turned = lax.dot_general(pick, rows, (((1,), (1,)), ((), ())), preferred_element_type=F32)
-        first = turned[:, :128].reshape(BLOCKS, OWN, 128)
-        second = turned[:, 128:].reshape(BLOCKS, OWN, 128)
-        sent_ref[which] = jnp.concatenate([first, second], axis=1).astype(BF)
+        turned = rows.T.astype(F32).reshape(2, BLOCKS // 2, OWN, SPAN)
+        both = jnp.stack([turned[0], turned[1]], axis=1).reshape(BLOCKS, OWN, SPAN)
+        both = jnp.stack(swap_halves(both), axis=1).reshape(BLOCKS, OWN, SPAN)
+        sent_ref[which] = jnp.concatenate([both[:, :, :128], both[:, :, 128:]], axis=1).astype(BF)
         write = pltpu.make_async_copy(
             sent_ref.at[which], out_ref.at[:, pl.ds(16 * which, 16), :], out_sems.at[which]
         )
@@ -73,17 +74,7 @@
         write.wait()
 
 
-def conv_kernel(got_ref, taps_hbm, skip_hbm, ahead_hbm, fine_hbm, turn_hbm, back_hbm, out_ref, *scratch):
-    taps_ref, skip_ref, ahead_ref, fine_ref, turn_ref, back_ref, sems = scratch
-    reads = []
-    for n, (source, target) in enumerate(
-        zip((ahead_hbm, taps_hbm, turn_hbm, fine_hbm, skip_hbm, back_hbm),
-            (ahead_ref, taps_ref, turn_ref, fine_ref, skip_ref, back_ref))
-    ):
-        reads.append(pltpu.make_async_copy(source, target, sems.at[n]))
-        reads[-1].start()
-    ahead_read, taps_read, turn_read, fine_read, skip_read, back_read = reads
-
+def conv_kernel(got_ref, taps_ref, skip_ref, ahead_ref, fine_ref, turn_ref, back_ref, out_ref):
     place = lax.axis_index("seq")
     lane = lax.broadcasted_iota(jnp.int32, (OWN, SPAN), 1)
     row = lax.broadcasted_iota(jnp.int32, (OWN, SPAN), 0)
@@ -115,14 +106,10 @@
         return total.reshape(SPAN, SPAN)
 
     response = block(3).astype(BF)
-    taps_read.wait()
     signal = (shaped(1) * shaped(2)).astype(BF)
-    ahead_read.wait()
     res_half = dot(ahead_ref[...], response)
     sig_half = dot(ahead_ref[...], signal)
-    turn_read.wait()
     cos, sin = turn_ref[:SPAN].astype(F32), turn_ref[SPAN:].astype(F32)
-    fine_read.wait()
     fine_cos, fine_sin = fine_ref[:SPAN], fine_ref[SPAN:]
     fine_less = -fine_sin
     spread = jnp.concatenate(
@@ -146,17 +133,15 @@
     both = dot(product.astype(BF), gather)
     real, imag = both[:, :SPAN], both[:, SPAN:]
     turned = jnp.concatenate([real * cos - imag * sin, real * sin + imag * cos], axis=0)
-    skip_read.wait()
-    back_read.wait()
     conv = dot(back_ref[...], turned.astype(BF))
     skip = own(skip_ref[...])
     direct = (signal.astype(F32).reshape(BLOCKS, OWN, SPAN) * skip).reshape(SPAN, SPAN)
-    gated = (shaped(0) * (conv + direct)).astype(BF)
-    gated = dot(message_order(True), gated)
+    gated = shaped(0) * (conv + direct)
+    lows, highs = (rows.reshape(128, SPAN) for rows in swap_halves(gated.reshape(BLOCKS, OWN, SPAN)))
     half = lax.broadcasted_iota(jnp.int32, (128, 128), 1) < 64
     for h in range(2):
-        low = gated[:128, 128 * h : 128 * h + 128]
-        high = gated[128:, 128 * h : 128 * h + 128]
+        low = lows[:, 128 * h : 128 * h + 128]
+        high = highs[:, 128 * h : 128 * h + 128]
         even = jnp.where(half, low, pltpu.roll(high, 64, 1))
         odd = jnp.where(half, pltpu.roll(low, 64, 1), high)
         out_ref[256 * h : 256 * h + 128, :] = even.astype(BF)
@@ -213,9 +198,8 @@
     return pl.pallas_call(
         conv_kernel,
         out_shape=jax.ShapeDtypeStruct((512, 128), BF),
-        in_specs=[VMEM] + [HBM] * 6,
+        in_specs=[VMEM] * 7,
         out_specs=VMEM,
-        scratch_shapes=[pltpu.VMEM(array.shape, array.dtype) for array in held] + [pltpu.SemaphoreType.DMA((6,))],
         compiler_params=PARAMS,
         cost_estimate=TINY,
     )(got, *held)
@@ -233,13 +217,10 @@
 
 
 def on_device(projected, short_taps, filters, skip_gain, out_weight):
-    near = lax.ppermute(
-        out_weight,
-        ("seq", "chan"),
-        [(s * 4 + (j + (1 if s % 2 == 0 else 3)) % 4, s * 4 + j) for s in range(BLOCKS) for j in range(4)],
-    )
-    half = lax.dynamic_slice_in_dim(out_weight, 128 * (lax.axis_index("seq") % 2), 128, 0)
-    far = lax.ppermute(half, "chan", [(j, (j + 2) % 4) for j in range(4)])
+    ring = [(s * 4 + (j + (1 if s % 2 == 0 else 3)) % 4, s * 4 + j) for s in range(BLOCKS) for j in range(4)]
+    near = lax.ppermute(out_weight, ("seq", "chan"), ring)
+    half = lax.dynamic_slice_in_dim(near, 128 * (lax.axis_index("seq") & 1), 128, 0)
+    far = lax.ppermute(half, ("seq", "chan"), ring)
     got = lax.all_to_all(pack(projected, filters), "seq", split_axis=0, concat_axis=0, tiled=True)
     gated = convolve(got, short_taps, skip_gain)
     gated, near, far = lax.optimization_barrier((gated, near, far))

time: 44.2 us -> 42.9 us (0.971)
  Pallas kernels: 6.05 us -> 4.77 us
  waiting for transfers between devices: 10.9 us -> 11.5 us
  starting transfers between devices: 13.7 us -> 13.2 us
    pallas_call x1, Pallas kernels: 2.11 us -> 1.47 us  [convolve(): pl.pallas_call(conv_kernel, out_shape=jax.ShapeDtypeStruct((512, 128), BF...]
    pallas_call x1, Pallas kernels: 2.72 us -> 2.08 us  [pack(): pl.pallas_call(pack_kernel, out_shape=jax.ShapeDtypeStruct((BLOCKS, 64, 1...]
    all_to_all x1, waiting for transfers between devices: 10.9 us -> 11.5 us  [on_device(): lax.all_to_all(pack(projected, filters), 'seq', split_axis=0, concat_axis...]
    ppermute x2, starting transfers between devices: 2.64 us -> 2.12 us  [the longest x1 2.04 us: on_device(): near = lax.ppermute(out_weight, ('seq', 'chan'), ring)]
  transfers between devices with their start and end apart: 5 -> 5, of which waited for: 1 -> 1; matrix products, arithmetic and copies ran while one was open for 0% -> 0% of each run, Pallas kernels for 11% -> 8%
where the time goes in v3:
time: 42.9 us; the launch traced here: 42.7 us
  starting transfers between devices  13.2 us (31%)
  blocking collectives  13.1 us (31%)
  waiting for transfers between devices  11.5 us (27%)
  Pallas kernels  4.77 us (11%)
    all_to_all x1, blocking collectives, on_device(): lax.all_to_all(gated.reshape(128, 4, 128), ('chan', 'seq'), split_axis=0,...  13.1 us
    all_to_all x1, waiting for transfers between devices, on_device(): lax.all_to_all(pack(projected, filters), 'seq', split_axis=0, concat_axis...  11.5 us
    all_to_all x1, starting transfers between devices, on_device(): lax.all_to_all(pack(projected, filters), 'seq', split_axis=0, concat_axis...  10.5 us
    pallas_call x1, Pallas kernels, pack(): pl.pallas_call(pack_kernel, out_shape=jax.ShapeDtypeStruct((BLOCKS, 64, 1...  2.08 us
    ppermute x1, starting transfers between devices, on_device(): near = lax.ppermute(out_weight, ('seq', 'chan'), ring)  2.04 us
    pallas_call x1, Pallas kernels, convolve(): pl.pallas_call(conv_kernel, out_shape=jax.ShapeDtypeStruct((512, 128), BF...  1.47 us
    pallas_call x1, Pallas kernels, project(): pl.pallas_call(project_kernel, out_shape=jax.ShapeDtypeStruct((64, 1024),...  1.22 us
  transfers between devices with their start and end apart: 5, of which 1 were waited for; matrix products, arithmetic and copies ran while one was open for 0% of the time, Pallas kernels for 8%

profile of v3, /device:TPU:1, one launch (start us, length us, event | category | flops | bytes accessed | tf_op | source)
XLA Modules:
  0.0 42.7 jit_solution(15896123625376718539)
XLA Ops:
  0.0 2.0 %collective-permute-start = (bf16[256,1024]{1,0:T(8,128)(2,1)}, bf16[256,1024]{1,0:T(8,128)(2,1)S(1)}, u32[]{:S(2)}, u32[]{:S(2)}) collective-permute-start(bf16[256,1024]{1,0:T(8,128)(2,1)} %own_ref.1), channel_id=1, source_target_pairs={{1,0},{2,1},{3,2},{0,3},{7,4},{4,5},{5,6},{6,7},{9,8},{10,9},{11,1... | collective-permute-start | bytes 1572872 | tf_op jit(solution)/shard_map/ppermute | solution.py:221
  2.0 2.1 %shard_map.91 = bf16[32,64,128]{2,1,0:T(8,128)(2,1)} custom-call(bf16[3,256,256]{2,1,0:T(8,128)(2,1)} %bitcast.7, f32[256,256]{1,0:T(8,128)} %filters_ref.1), custom_call_target="tpu_custom_call" | custom-call | flops 1000 | bytes 1000 | tf_op jit(solution)/shard_map/pallas_call | solution.py:179
  4.1 0.0 copy-start.3
  4.1 0.0 copy-start.4
  4.2 0.0 copy-start.5
  4.2 10.5 %all-to-all-start = ((bf16[32,64,128]{2,1,0:T(8,128)(2,1)}), bf16[32,64,128]{2,1,0:T(8,128)(2,1)S(1)}, u32[]{:S(2)}, u32[]{:S(2)}) async-start(bf16[32,64,128]{2,1,0:T(8,128)(2,1)} %shard_map.91), calls=%async_computation | async-start | bytes 1048576 | tf_op jit(solution)/shard_map/all_to_all | solution.py:224
  14.6 0.0 copy-start.1
  14.7 0.0 copy-start.2
  14.7 0.0 collective-permute-done.near_ref
  14.7 0.0 copy-start.6
  14.7 0.1 collective-permute-start.1
  14.8 11.5 %all-to-all-done.got_ref = bf16[32,64,128]{2,1,0:T(8,128)(2,1)S(1)} async-done(((bf16[32,64,128]{2,1,0:T(8,128)(2,1)}), bf16[32,64,128]{2,1,0:T(8,128)(2,1)S(1)}, u32[]{:S(2)}, u32[]{:S(2)}) %all-to-all-start) | async-done | bytes 524320 | tf_op jit(solution)/shard_map/all_to_all | solution.py:224
  26.3 0.0 copy-done.1
  26.3 0.0 copy-done.2
  26.3 0.0 copy-done.6
  26.3 0.0 copy-start
  26.3 1.5 %shard_map.92 = bf16[512,128]{1,0:T(8,128)(2,1)S(1)} custom-call(bf16[32,64,128]{2,1,0:T(8,128)(2,1)S(1)} %all-to-all-done.got_ref, f32[3,3,256]{2,1,0:T(4,128)S(1)} %copy-done.5, f32[1,256]{1,0:T(1,128)S(1)} %bitcast.6, bf16[512,256]{1,0:T(8,128)(2,1)S(1)} %copy-done.4, bf16[512,256]{1,0:T(8,128)(2,1)S(1)} %copy-done.3, bf16[512,256]{1,0:T(8,128)(2,1)S(1)} %copy-done.2, ...), custom_call_target="tpu_custom_call" | custom-call | flops 1000 | bytes 1000 | tf_op jit(solution)/shard_map/pallas_call | solution.py:198
  27.8 0.0 collective-permute-done.1.far_ref
  27.8 0.1 collective-permute-start.2
  27.9 0.5 %collective-permute-start.3 = (bf16[128,1024]{1,0:T(8,128)(2,1)S(1)}, bf16[128,1024]{1,0:T(8,128)(2,1)S(1)}, u32[]{:S(2)}, u32[]{:S(2)}) collective-permute-start(bf16[128,1024]{1,0:T(8,128)(2,1)S(1)} %collective-permute-done.1.far_ref), channel_id=1, source_target_pairs={{0,4},{4,0},{8,12},{12,8},{16,20},{20,16},{24,28},{28,24},{32,36},... | collective-permute-start | bytes 786440 | tf_op jit(solution)/shard_map/ppermute | solution.py:228
  28.4 13.1 %all_to_all.10 = bf16[128,4,128]{2,1,0:T(4,128)(2,1)S(1)} all-to-all(bf16[128,4,128]{2,1,0:T(4,128)(2,1)S(1)} %bitcast.4), channel_id=1, replica_groups=mesh['seq'=32,'chan'=4] {'chan','seq'}, dimensions={0} | all-to-all | bytes 262144 | tf_op jit(solution)/shard_map/all_to_all | solution.py:229
  41.5 0.0 collective-permute-done.3.far_swap_ref
  41.5 0.0 collective-permute-done.2.swap_ref
  41.5 1.2 %shard_map.93 = bf16[64,1024]{1,0:T(8,128)(2,1)} custom-call(bf16[512,128]{1,0:T(8,128)(2,1)S(1)} %bitcast.5, bf16[256,1024]{1,0:T(8,128)(2,1)S(1)} %copy-done, bf16[256,1024]{1,0:T(8,128)(2,1)S(1)} %collective-permute-done.near_ref, bf16[256,1024]{1,0:T(8,128)(2,1)S(1)} %collective-permute-done.2.swap_ref, ...), custom_call_target="tpu_custom_call" | custom-call | flops 1000 | bytes 1000 | tf_op jit(solution)/shard_map/pallas_call | solution.py:209
  (5 shorter events, 0.0 us)
Async XLA Ops:
  0.0 14.7 %collective-permute-start = (bf16[256,1024]{1,0:T(8,128)(2,1)}, bf16[256,1024]{1,0:T(8,128)(2,1)S(1)}, u32[]{:S(2)}, u32[]{:S(2)}) collective-permute-start(bf16[256,1024]{1,0:T(8,128)(2,1)} %own_ref.1), channel_id=1, source_target_pairs={{1,0},{2,1},{3,2},{0,3},{7,4},{4,5},{5,6},{6,7},{9,8},{10,9},{11,1... | collective-permute-start | bytes 1572872 | tf_op jit(solution)/shard_map/ppermute | solution.py:221
  4.1 22.1 %copy-start.3 = (bf16[512,256]{1,0:T(8,128)(2,1)S(1)}, bf16[512,256]{1,0:T(8,128)(2,1)}, u32[]{:S(2)}) copy-start(bf16[512,256]{1,0:T(8,128)(2,1)} %constant.27.fine_ref) | copy-start | bytes 786436
  4.1 22.1 %copy-start.4 = (bf16[512,256]{1,0:T(8,128)(2,1)S(1)}, bf16[512,256]{1,0:T(8,128)(2,1)}, u32[]{:S(2)}) copy-start(bf16[512,256]{1,0:T(8,128)(2,1)} %constant.26.ahead_ref) | copy-start | bytes 786436
  4.2 22.1 %copy-start.5 = (f32[3,3,256]{2,1,0:T(4,128)S(1)}, f32[3,3,256]{2,1,0:T(4,128)}, u32[]{:S(2)}) copy-start(f32[3,3,256]{2,1,0:T(4,128)} %taps_ref.1) | copy-start | bytes 27652
  4.2 22.1 %all-to-all-start = ((bf16[32,64,128]{2,1,0:T(8,128)(2,1)}), bf16[32,64,128]{2,1,0:T(8,128)(2,1)S(1)}, u32[]{:S(2)}, u32[]{:S(2)}) async-start(bf16[32,64,128]{2,1,0:T(8,128)(2,1)} %shard_map.91), calls=%async_computation | async-start | bytes 1048576 | tf_op jit(solution)/shard_map/all_to_all | solution.py:224
  14.6 11.6 %copy-start.1 = (bf16[256,512]{1,0:T(8,128)(2,1)S(1)}, bf16[256,512]{1,0:T(8,128)(2,1)}, u32[]{:S(2)}) copy-start(bf16[256,512]{1,0:T(8,128)(2,1)} %constant.29.back_ref) | copy-start | bytes 786436
  14.7 11.6 %copy-start.2 = (bf16[512,256]{1,0:T(8,128)(2,1)S(1)}, bf16[512,256]{1,0:T(8,128)(2,1)}, u32[]{:S(2)}) copy-start(bf16[512,256]{1,0:T(8,128)(2,1)} %constant.28.turn_ref) | copy-start | bytes 786436
  14.7 11.6 %copy-start.6 = (f32[256]{0:T(256)S(1)}, f32[256]{0:T(256)}, u32[]{:S(2)}) copy-start(f32[256]{0:T(256)} %param.12) | copy-start | bytes 3076
  14.7 13.1 %collective-permute-start.1 = (bf16[128,1024]{1,0:T(8,128)(2,1)S(1)}, bf16[128,1024]{1,0:T(8,128)(2,1)S(1)}, u32[]{:S(2)}, u32[]{:S(2)}) collective-permute-start(bf16[128,1024]{1,0:T(8,128)(2,1)S(1)} %constant_dynamic-slice_fusion), channel_id=1, source_target_pairs={{1,0},{2,1},{3,2},{0,3},{7,4},{4,5},{5,6},{6,7},{9,8},{10,9},{11,1... | collective-permute-start | bytes 786440 | tf_op jit(solution)/shard_map/ppermute | solution.py:223
  26.3 15.2 %copy-start = (bf16[256,1024]{1,0:T(8,128)(2,1)S(1)}, bf16[256,1024]{1,0:T(8,128)(2,1)}, u32[]{:S(2)}) copy-start(bf16[256,1024]{1,0:T(8,128)(2,1)} %own_ref.1) | copy-start | bytes 1572868
  27.8 13.7 %collective-permute-start.2 = (bf16[256,1024]{1,0:T(8,128)(2,1)S(1)}, bf16[256,1024]{1,0:T(8,128)(2,1)S(1)}, u32[]{:S(2)}, u32[]{:S(2)}) collective-permute-start(bf16[256,1024]{1,0:T(8,128)(2,1)S(1)} %collective-permute-done.near_ref), channel_id=1, source_target_pairs={{0,4},{4,0},{8,12},{12,8},{16,20},{20,16},{24,28},{28,24},{32,36},... | collective-permute-start | bytes 1572872 | tf_op jit(solution)/shard_map/ppermute | solution.py:228
  27.9 13.6 %collective-permute-start.3 = (bf16[128,1024]{1,0:T(8,128)(2,1)S(1)}, bf16[128,1024]{1,0:T(8,128)(2,1)S(1)}, u32[]{:S(2)}, u32[]{:S(2)}) collective-permute-start(bf16[128,1024]{1,0:T(8,128)(2,1)S(1)} %collective-permute-done.1.far_ref), channel_id=1, source_target_pairs={{0,4},{4,0},{8,12},{12,8},{16,20},{20,16},{24,28},{28,24},{32,36},... | collective-permute-start | bytes 786440 | tf_op jit(solution)/shard_map/ppermute | solution.py:228

commit v4 on v3

v4 whole, which is shorter than its diff:
```python
import math

import jax
import jax.numpy as jnp
import numpy as np
from jax import lax
from jax.experimental import pallas as pl
from jax.experimental.pallas import tpu as pltpu
from jax.sharding import PartitionSpec as P

BLOCKS = 32
SPAN = 256
OWN = 8
BF = jnp.bfloat16
F32 = jnp.float32


def dot(left, right):
    return jnp.dot(left, right, preferred_element_type=F32)


def constants():
    total = BLOCKS * SPAN
    low = np.arange(BLOCKS)[:, None] + 0.25
    coarse = 2 * math.pi / BLOCKS * low * np.arange(BLOCKS)[None, :]
    eye = np.eye(OWN)
    ahead = np.concatenate([np.kron(np.cos(coarse), eye), np.kron(-np.sin(coarse), eye)], axis=0)
    back = ahead.T / total
    turn = 2 * math.pi / total * low * np.arange(SPAN)[None, :]
    turn = np.repeat(turn, OWN, axis=0)
    fine = 2 * math.pi / SPAN * (np.arange(SPAN)[:, None] * np.arange(SPAN)[None, :] % SPAN)
    as_bf = lambda table: jnp.asarray(table.astype(np.float32)).astype(BF)
    return dict(
        ahead=as_bf(ahead),
        back=as_bf(back),
        fine=as_bf(np.concatenate([np.cos(fine), np.sin(fine)], axis=0)),
        turn=as_bf(np.concatenate([np.cos(turn), np.sin(turn)], axis=0)),
    )


def swap_halves(tiles):
    count, _, columns = tiles.shape
    pairs = tiles.reshape(count // 2, 2, 8, columns)
    first, second = pairs[:, 0], pairs[:, 1]
    upper = lax.broadcasted_iota(jnp.int32, first.shape, 1) < 4
    return (
        jnp.where(upper, first, pltpu.roll(second, 4, 1)),
        jnp.where(upper, pltpu.roll(first, 4, 1), second),
    )


def pack_kernel(projected_ref, filters_ref, taps_hbm, out_ref, rows_ref, long_ref, taps_ref, sent_ref, sems):
    parts = (
        (filters_ref, long_ref),
        (taps_hbm, taps_ref),
        (projected_ref.at[0], rows_ref.at[0]),
        (projected_ref.at[1], rows_ref.at[1]),
        (projected_ref.at[2], rows_ref.at[2]),
    )
    reads = [pltpu.make_async_copy(*part, sems.at[n]) for n, part in enumerate(parts)]
    for read in reads:
        read.start()

    def by_device(turned):
        columns = turned.shape[1]
        turned = turned.astype(F32).reshape(2, BLOCKS // 2, OWN, columns)
        both = jnp.stack([turned[0], turned[1]], axis=1).reshape(BLOCKS, OWN, columns)
        return jnp.stack(swap_halves(both), axis=1).reshape(BLOCKS, OWN, columns)

    def store(first_row, rows):
        both = by_device(rows.T)
        sent_ref[:, first_row : first_row + 16, :] = jnp.concatenate([both[:, :, :128], both[:, :, 128:]], axis=1).astype(BF)

    reads[0].wait()
    store(16, long_ref[...].astype(BF))
    reads[2].wait()
    store(32, rows_ref[0])
    for read in (reads[1], reads[3], reads[4]):
        read.wait()

    def shaped(which):
        rows = rows_ref[which].astype(F32)
        total = taps_ref[0, which : which + 1, :] * rows
        for tap in (1, 2):
            total = total + taps_ref[tap, which : which + 1, :] * pltpu.roll(rows, tap, 0)
        return total

    store(0, (shaped(1) * shaped(2)).astype(BF))
    key, value = rows_ref[1], rows_ref[2]
    first = [rows[:16].astype(F32)[:2] for rows in (key, value)]
    last = [rows[SPAN - 16 :].astype(F32)[14:] for rows in (key, value)]
    edges = jnp.concatenate(first + last + [jnp.zeros((120, SPAN), F32)], axis=0)
    sent_ref[:, 48:56, :] = by_device(edges.T).astype(BF)
    write = pltpu.make_async_copy(sent_ref, out_ref, sems.at[5])
    write.start()
    write.wait()


def conv_kernel(got_ref, taps_ref, skip_ref, ahead_ref, fine_ref, turn_ref, back_ref, out_ref):
    place = lax.axis_index("seq")
    lane = lax.broadcasted_iota(jnp.int32, (OWN, SPAN), 1)
    row = lax.broadcasted_iota(jnp.int32, (OWN, SPAN), 0)
    mine = lane == 128 * (row >> 2) + 4 * place + (row & 3)

    def own(values):
        return jnp.sum(jnp.where(mine, values, 0.0), axis=1, keepdims=True)[None]

    def block(first_row):
        both = got_ref[:, first_row : first_row + 16, :].astype(F32)
        return both[:, :8], both[:, 8:]

    edges = got_ref[:, 48:56, :].astype(F32)
    before = jnp.concatenate([jnp.zeros((1, OWN, 128), F32), edges[:-1]], axis=0)
    thin = lax.broadcasted_iota(jnp.int32, (BLOCKS, OWN, 128), 2)

    def left(rows, by):
        return rows if by == 0 else pltpu.roll(rows, -by % 128, 2)

    def gains(which):
        return [own(taps_ref[tap, which : which + 1, :]) for tap in range(3)]

    def edge(which, at):
        first, second, third = gains(which)
        once = jnp.where(thin == 0, left(before, at + 5), left(edges, at - 1))
        return left(edges, at) * first + once * second + left(before, at + 4) * third

    def later(rows, by):
        turned = pltpu.roll(rows, by, 2)
        earlier = jnp.concatenate([jnp.zeros((1, OWN, SPAN), F32), turned[:-1]], axis=0)
        return jnp.where(lax.broadcasted_iota(jnp.int32, turned.shape, 2) < by, earlier, turned)

    early, late = block(0)
    early = jnp.where(thin < 2, edge(1, 0) * edge(2, 2), early)
    signal = jnp.concatenate([early.reshape(SPAN, 128), late.reshape(SPAN, 128)], axis=1).astype(BF)
    response = jnp.concatenate([half.reshape(SPAN, 128) for half in block(16)], axis=1).astype(BF)
    res_half = dot(ahead_ref[...], response)
    sig_half = dot(ahead_ref[...], signal)
    raw = jnp.concatenate(block(32), axis=2)
    first, second, third = gains(0)
    query = raw * first + later(raw, 1) * second + later(raw, 2) * third
    cos, sin = turn_ref[:SPAN].astype(F32), turn_ref[SPAN:].astype(F32)
    fine_cos, fine_sin = fine_ref[:SPAN], fine_ref[SPAN:]
    fine_less = -fine_sin
    spread = jnp.concatenate(
        [jnp.concatenate([fine_cos, fine_less], axis=1), jnp.concatenate([fine_sin, fine_cos], axis=1)], axis=0
    )
    gather = jnp.concatenate(
        [jnp.concatenate([fine_cos, fine_sin], axis=1), jnp.concatenate([fine_less, fine_cos], axis=1)], axis=0
    )

    def spectrum(half):
        real, imag = half[:SPAN], half[SPAN:]
        turned = jnp.concatenate([real * cos + imag * sin, imag * cos - real * sin], axis=1)
        both = dot(turned.astype(BF), spread)
        return both[:, :SPAN], both[:, SPAN:]

    res_real, res_imag = spectrum(res_half)
    sig_real, sig_imag = spectrum(sig_half)
    product = jnp.concatenate(
        [sig_real * res_real - sig_imag * res_imag, sig_real * res_imag + sig_imag * res_real], axis=1
    )
    both = dot(product.astype(BF), gather)
    real, imag = both[:, :SPAN], both[:, SPAN:]
    turned = jnp.concatenate([real * cos - imag * sin, real * sin + imag * cos], axis=0)
    conv = dot(back_ref[...], turned.astype(BF))
    skip = own(skip_ref[...])
    direct = (signal.astype(F32).reshape(BLOCKS, OWN, SPAN) * skip).reshape(SPAN, SPAN)
    gated = query * (conv + direct).reshape(BLOCKS, OWN, SPAN)
    lows, highs = (rows.reshape(128, SPAN) for rows in swap_halves(gated))
    half = lax.broadcasted_iota(jnp.int32, (128, 128), 1) < 64
    for h in range(2):
        low, high = lows[:, 128 * h : 128 * h + 128], highs[:, 128 * h : 128 * h + 128]
        even = jnp.where(half, low, pltpu.roll(high, 64, 1))
        odd = jnp.where(half, pltpu.roll(low, 64, 1), high)
        out_ref[256 * h : 256 * h + 128, :] = even.astype(BF)
        out_ref[256 * h + 128 : 256 * h + 256, :] = odd.astype(BF)


def project_kernel(got_ref, own_ref, near_ref, swap_ref, other_ref, far_ref, far_swap_ref, out_ref):
    place = lax.axis_index("chan")
    odd = lax.axis_index("seq") % 2

    def block(step):
        owner = lax.rem(place + step, 4)
        rows = got_ref[pl.ds(pl.multiple_of(owner * 128, 128), 128), :].astype(F32).T
        return jnp.concatenate([rows[:64], rows[64:]], axis=1).astype(BF)

    total = dot(block(0), own_ref[...]) + dot(block(1 + 2 * odd), near_ref[...])
    for step, here_ref, there_ref in ((3 - 2 * odd, other_ref, swap_ref), (2, far_ref, far_swap_ref)):
        rows = block(step)
        total = total + dot(jnp.where(odd == 0, rows[:, :128], rows[:, 128:]), here_ref[...])
        total = total + dot(jnp.where(odd == 0, rows[:, 128:], rows[:, :128]), there_ref[...])
    out_ref[...] = total.astype(BF)


HBM = pl.BlockSpec(memory_space=pltpu.HBM)
VMEM = pl.BlockSpec(memory_space=pltpu.VMEM)
PARAMS = pltpu.CompilerParams(vmem_limit_bytes=32 * 1024 * 1024)


TINY = pl.CostEstimate(flops=1000, bytes_accessed=1000, transcendentals=0)


def pack(projected, filters, short_taps):
    return pl.pallas_call(
        pack_kernel,
        out_shape=jax.ShapeDtypeStruct((BLOCKS, 56, 128), BF),
        in_specs=[HBM] * 3,
        out_specs=HBM,
        scratch_shapes=[
            pltpu.VMEM((3, SPAN, SPAN), BF),
            pltpu.VMEM((SPAN, SPAN), F32),
            pltpu.VMEM((3, 3, SPAN), F32),
            pltpu.VMEM((BLOCKS, 56, 128), BF),
            pltpu.SemaphoreType.DMA((6,)),
        ],
        cost_estimate=TINY,
    )(projected, filters, short_taps)


def convolve(got, short_taps, skip_gain):
    table = constants()
    held = [short_taps, skip_gain.reshape(1, SPAN)] + [table[name] for name in ("ahead", "fine", "turn", "back")]
    return pl.pallas_call(
        conv_kernel,
        out_shape=jax.ShapeDtypeStruct((512, 128), BF),
        in_specs=[VMEM] * 7,
        out_specs=VMEM,
        compiler_params=PARAMS,
        cost_estimate=TINY,
    )(got, *held)


def project(got, weights):
    return pl.pallas_call(
        project_kernel,
        out_shape=jax.ShapeDtypeStruct((64, 1024), BF),
        in_specs=[VMEM] * (1 + len(weights)),
        out_specs=VMEM,
        compiler_params=PARAMS,
        cost_estimate=TINY,
    )(got, *weights)


def on_device(projected, short_taps, filters, skip_gain, out_weight):
    ring = [(s * 4 + (j + (1 if s % 2 == 0 else 3)) % 4, s * 4 + j) for s in range(BLOCKS) for j in range(4)]
    near = lax.ppermute(out_weight, ("seq", "chan"), ring)
    core = lax.axis_index("seq") & 1
    half = lax.dynamic_slice_in_dim(near, 128 * core, 128, 0)
    other = lax.dynamic_slice_in_dim(near, 128 - 128 * core, 128, 0)
    far = lax.ppermute(half, ("seq", "chan"), ring)
    pairs = [(s, s ^ 1) for s in range(BLOCKS)]
    swaps = [lax.ppermute(part, "seq", pairs) for part in (half, other)]
    got = lax.all_to_all(pack(projected.transpose(1, 0, 2), filters, short_taps), "seq", split_axis=0, concat_axis=0, tiled=True)
    got, *swaps = lax.optimization_barrier((got, *swaps))
    gated = convolve(got, short_taps, skip_gain)
    gated, far = lax.optimization_barrier((gated, far))
    weights = (out_weight, near, *swaps, far, lax.ppermute(far, "seq", pairs))
    got = lax.all_to_all(gated.reshape(128, 4, 128), ("chan", "seq"), split_axis=0, concat_axis=0, tiled=True)
    return project(got.reshape(512, 128), weights)


def solution(mesh):
    return jax.shard_map(
        on_device,
        mesh=mesh,
        in_specs=(
            P("seq", None, "chan"),
            P(None, None, "chan"),
            P("seq", "chan"),
            P("chan"),
            P("chan", None),
        ),
        out_specs=P(("seq", "chan"), None),
        check_vma=False,
    )
```

time: 42.9 us -> 42 us (0.979)
  waiting for transfers between devices: 11.5 us -> 10.3 us
    all_to_all x1, waiting for transfers between devices: 11.5 us -> 10.3 us  [on_device(): lax.all_to_all(pack(projected.transpose(1, 0, 2), filters, short_taps), '...]
  transfers between devices with their start and end apart: 5 -> 6, of which waited for: 1 -> 1; matrix products, arithmetic and copies ran while one was open for 0% -> 0% of each run, Pallas kernels for 8% -> 9%
where the time goes in v4:
time: 42 us; the launch traced here: 41.7 us
  blocking collectives  13.3 us (32%)
  starting transfers between devices  13 us (31%)
  waiting for transfers between devices  10.3 us (25%)
  Pallas kernels  4.79 us (11%)
    all_to_all x1, blocking collectives, on_device(): lax.all_to_all(gated.reshape(128, 4, 128), ('chan', 'seq'), split_axis=0,...  13.3 us
    all_to_all x1, starting transfers between devices, on_device(): lax.all_to_all(pack(projected.transpose(1, 0, 2), filters, short_taps), '...  10.3 us
    all_to_all x1, waiting for transfers between devices, on_device(): lax.all_to_all(pack(projected.transpose(1, 0, 2), filters, short_taps), '...  10.3 us
    pallas_call x1, Pallas kernels, pack(): pl.pallas_call(pack_kernel, out_shape=jax.ShapeDtypeStruct((BLOCKS, 56, 1...  2.21 us
    ppermute x1, starting transfers between devices, on_device(): near = lax.ppermute(out_weight, ('seq', 'chan'), ring)  2.04 us
    pallas_call x1, Pallas kernels, convolve(): pl.pallas_call(conv_kernel, out_shape=jax.ShapeDtypeStruct((512, 128), BF...  1.38 us
    pallas_call x1, Pallas kernels, project(): pl.pallas_call(project_kernel, out_shape=jax.ShapeDtypeStruct((64, 1024),...  1.2 us
  transfers between devices with their start and end apart: 6, of which 1 were waited for; matrix products, arithmetic and copies ran while one was open for 0% of the time, Pallas kernels for 9%

profile of v4, /device:TPU:1, one launch (start us, length us, event | category | flops | bytes accessed | tf_op | source)
XLA Modules:
  0.0 41.7 jit_solution(17544568419420702059)
XLA Ops:
  0.0 2.0 %collective-permute-start = (bf16[256,1024]{1,0:T(8,128)(2,1)}, bf16[256,1024]{1,0:T(8,128)(2,1)S(1)}, u32[]{:S(2)}, u32[]{:S(2)}) collective-permute-start(bf16[256,1024]{1,0:T(8,128)(2,1)} %own_ref.1), channel_id=1, source_target_pairs={{1,0},{2,1},{3,2},{0,3},{7,4},{4,5},{5,6},{6,7},{9,8},{10,9},{11,1... | collective-permute-start | bytes 1572872 | tf_op jit(solution)/shard_map/ppermute | solution.py:247
  2.0 2.2 %shard_map.91 = bf16[32,56,128]{2,1,0:T(8,128)(2,1)} custom-call(bf16[3,256,256]{2,1,0:T(8,128)(2,1)} %bitcast.7, f32[256,256]{1,0:T(8,128)} %filters_ref.1, f32[3,3,256]{2,1,0:T(4,128)} %taps_ref.1), custom_call_target="tpu_custom_call" | custom-call | flops 1000 | bytes 1000 | tf_op jit(solution)/shard_map/pallas_call | solution.py:205
  4.3 0.0 copy-start.5
  4.3 10.3 %all-to-all-start = ((bf16[32,56,128]{2,1,0:T(8,128)(2,1)}), bf16[32,56,128]{2,1,0:T(8,128)(2,1)S(1)}, u32[]{:S(2)}, u32[]{:S(2)}) async-start(bf16[32,56,128]{2,1,0:T(8,128)(2,1)} %shard_map.91), calls=%async_computation | async-start | bytes 917504 | tf_op jit(solution)/shard_map/all_to_all | solution.py:254
  14.6 0.0 copy-start.1
  14.6 0.0 copy-start.2
  14.6 0.0 copy-start.3
  14.7 0.0 copy-start.4
  14.7 0.0 collective-permute-done.near_ref
  14.7 0.3 collective-permute-start.2
  15.0 0.3 collective-permute-start.1
  15.3 0.0 collective-permute-start.3
  15.3 10.3 %all-to-all-done.got_ref = bf16[32,56,128]{2,1,0:T(8,128)(2,1)S(1)} async-done(((bf16[32,56,128]{2,1,0:T(8,128)(2,1)}), bf16[32,56,128]{2,1,0:T(8,128)(2,1)S(1)}, u32[]{:S(2)}, u32[]{:S(2)}) %all-to-all-start) | async-done | bytes 458784 | tf_op jit(solution)/shard_map/all_to_all | solution.py:254
  25.6 0.0 collective-permute-done.2.other_ref
  25.6 0.0 collective-permute-done.1.swap_ref
  25.6 0.0 copy-done.5
  25.6 0.0 copy-done.1
  25.6 0.0 copy-start
  25.7 1.4 %shard_map.92 = bf16[512,128]{1,0:T(8,128)(2,1)S(1)} custom-call(bf16[32,56,128]{2,1,0:T(8,128)(2,1)S(1)} %all-to-all-done.got_ref, f32[3,3,256]{2,1,0:T(4,128)S(1)} %copy-done.5, f32[1,256]{1,0:T(1,128)S(1)} %bitcast.6, bf16[512,256]{1,0:T(8,128)(2,1)S(1)} %copy-done.4, bf16[512,256]{1,0:T(8,128)(2,1)S(1)} %copy-done.3, bf16[512,256]{1,0:T(8,128)(2,1)S(1)} %copy-done.2, ...), custom_call_target="tpu_custom_call" | custom-call | flops 1000 | bytes 1000 | tf_op jit(solution)/shard_map/pallas_call | solution.py:224
  27.0 0.0 collective-permute-done.3.far_ref
  27.1 0.1 collective-permute-start.4
  27.1 13.3 %all_to_all.10 = bf16[128,4,128]{2,1,0:T(4,128)(2,1)S(1)} all-to-all(bf16[128,4,128]{2,1,0:T(4,128)(2,1)S(1)} %bitcast.4), channel_id=1, replica_groups=mesh['seq'=32,'chan'=4] {'chan','seq'}, dimensions={0} | all-to-all | bytes 262144 | tf_op jit(solution)/shard_map/all_to_all | solution.py:259
  40.5 0.0 collective-permute-done.4.far_swap_ref
  40.5 1.2 %shard_map.93 = bf16[64,1024]{1,0:T(8,128)(2,1)} custom-call(bf16[512,128]{1,0:T(8,128)(2,1)S(1)} %bitcast.5, bf16[256,1024]{1,0:T(8,128)(2,1)S(1)} %copy-done, bf16[256,1024]{1,0:T(8,128)(2,1)S(1)} %collective-permute-done.near_ref, bf16[128,1024]{1,0:T(8,128)(2,1)S(1)} %collective-permute-done.1.swap_ref, ...), custom_call_target="tpu_custom_call" | custom-call | flops 1000 | bytes 1000 | tf_op jit(solution)/shard_map/pallas_call | solution.py:235
  (7 shorter events, 0.1 us)
Async XLA Ops:
  0.0 14.7 %collective-permute-start = (bf16[256,1024]{1,0:T(8,128)(2,1)}, bf16[256,1024]{1,0:T(8,128)(2,1)S(1)}, u32[]{:S(2)}, u32[]{:S(2)}) collective-permute-start(bf16[256,1024]{1,0:T(8,128)(2,1)} %own_ref.1), channel_id=1, source_target_pairs={{1,0},{2,1},{3,2},{0,3},{7,4},{4,5},{5,6},{6,7},{9,8},{10,9},{11,1... | collective-permute-start | bytes 1572872 | tf_op jit(solution)/shard_map/ppermute | solution.py:247
  4.3 21.3 %copy-start.5 = (f32[3,3,256]{2,1,0:T(4,128)S(1)}, f32[3,3,256]{2,1,0:T(4,128)}, u32[]{:S(2)}) copy-start(f32[3,3,256]{2,1,0:T(4,128)} %taps_ref.1) | copy-start | bytes 27652
  4.3 21.3 %all-to-all-start = ((bf16[32,56,128]{2,1,0:T(8,128)(2,1)}), bf16[32,56,128]{2,1,0:T(8,128)(2,1)S(1)}, u32[]{:S(2)}, u32[]{:S(2)}) async-start(bf16[32,56,128]{2,1,0:T(8,128)(2,1)} %shard_map.91), calls=%async_computation | async-start | bytes 917504 | tf_op jit(solution)/shard_map/all_to_all | solution.py:254
  14.6 11.0 %copy-start.1 = (bf16[256,512]{1,0:T(8,128)(2,1)S(1)}, bf16[256,512]{1,0:T(8,128)(2,1)}, u32[]{:S(2)}) copy-start(bf16[256,512]{1,0:T(8,128)(2,1)} %constant.31.back_ref) | copy-start | bytes 786436
  14.6 11.0 %copy-start.2 = (bf16[512,256]{1,0:T(8,128)(2,1)S(1)}, bf16[512,256]{1,0:T(8,128)(2,1)}, u32[]{:S(2)}) copy-start(bf16[512,256]{1,0:T(8,128)(2,1)} %constant.30.turn_ref) | copy-start | bytes 786436
  14.6 11.0 %copy-start.3 = (bf16[512,256]{1,0:T(8,128)(2,1)S(1)}, bf16[512,256]{1,0:T(8,128)(2,1)}, u32[]{:S(2)}) copy-start(bf16[512,256]{1,0:T(8,128)(2,1)} %constant.29.fine_ref) | copy-start | bytes 786436
  14.7 11.0 %copy-start.4 = (bf16[512,256]{1,0:T(8,128)(2,1)S(1)}, bf16[512,256]{1,0:T(8,128)(2,1)}, u32[]{:S(2)}) copy-start(bf16[512,256]{1,0:T(8,128)(2,1)} %constant.28.ahead_ref) | copy-start | bytes 786436
  14.7 10.8 %collective-permute-start.2 = (bf16[128,1024]{1,0:T(8,128)(2,1)S(1)}, bf16[128,1024]{1,0:T(8,128)(2,1)S(1)}, u32[]{:S(2)}, u32[]{:S(2)}) collective-permute-start(bf16[128,1024]{1,0:T(8,128)(2,1)S(1)} %get-tuple-element.15), channel_id=1, source_target_pairs={{0,4},{4,0},{8,12},{12,8},{16,20},{20,16},{24,28},{28,24},{32,36},... | collective-permute-start | bytes 786440 | tf_op jit(solution)/shard_map/ppermute | solution.py:253
  15.0 10.6 %copy-start.6 = (f32[256]{0:T(256)S(1)}, f32[256]{0:T(256)}, u32[]{:S(2)}) copy-start(f32[256]{0:T(256)} %param.12) | copy-start | bytes 3076
  15.0 10.5 %collective-permute-start.1 = (bf16[128,1024]{1,0:T(8,128)(2,1)S(1)}, bf16[128,1024]{1,0:T(8,128)(2,1)S(1)}, u32[]{:S(2)}, u32[]{:S(2)}) collective-permute-start(bf16[128,1024]{1,0:T(8,128)(2,1)S(1)} %get-tuple-element.16), channel_id=1, source_target_pairs={{0,4},{4,0},{8,12},{12,8},{16,20},{20,16},{24,28},{28,24},{32,36},... | collective-permute-start | bytes 786440 | tf_op jit(solution)/shard_map/ppermute | solution.py:253
  15.3 11.7 %collective-permute-start.3 = (bf16[128,1024]{1,0:T(8,128)(2,1)S(1)}, bf16[128,1024]{1,0:T(8,128)(2,1)S(1)}, u32[]{:S(2)}, u32[]{:S(2)}) collective-permute-start(bf16[128,1024]{1,0:T(8,128)(2,1)S(1)} %get-tuple-element.16), channel_id=1, source_target_pairs={{1,0},{2,1},{3,2},{0,3},{7,4},{4,5},{5,6},{6,7},{9,8},{10,9},{11,1... | collective-permute-start | bytes 786440 | tf_op jit(solution)/shard_map/ppermute | solution.py:251
  25.6 14.9 %copy-start = (bf16[256,1024]{1,0:T(8,128)(2,1)S(1)}, bf16[256,1024]{1,0:T(8,128)(2,1)}, u32[]{:S(2)}) copy-start(bf16[256,1024]{1,0:T(8,128)(2,1)} %own_ref.1) | copy-start | bytes 1572868
  27.1 13.4 %collective-permute-start.4 = (bf16[128,1024]{1,0:T(8,128)(2,1)S(1)}, bf16[128,1024]{1,0:T(8,128)(2,1)S(1)}, u32[]{:S(2)}, u32[]{:S(2)}) collective-permute-start(bf16[128,1024]{1,0:T(8,128)(2,1)S(1)} %collective-permute-done.3.far_ref), channel_id=1, source_target_pairs={{0,4},{4,0},{8,12},{12,8},{16,20},{20,16},{24,28},{28,24},{32,36},... | collective-permute-start | bytes 786440 | tf_op jit(solution)/shard_map/ppermute | solution.py:258

commit v5 on v4

--- a/solution.py
+++ b/solution.py
@@ -49,13 +49,14 @@
     )
 
 
-def pack_kernel(projected_ref, filters_ref, taps_hbm, out_ref, rows_ref, long_ref, taps_ref, sent_ref, sems):
+def pack_kernel(projected_ref, filters_ref, taps_hbm, out_ref, rows_ref, rim_ref, long_ref, taps_ref, sent_ref, sems):
     parts = (
         (filters_ref, long_ref),
         (taps_hbm, taps_ref),
-        (projected_ref.at[0], rows_ref.at[0]),
-        (projected_ref.at[1], rows_ref.at[1]),
-        (projected_ref.at[2], rows_ref.at[2]),
+        (projected_ref.at[1], rows_ref.at[0]),
+        (projected_ref.at[2], rows_ref.at[1]),
+        (projected_ref.at[0, pl.ds(0, 16)], rim_ref.at[0]),
+        (projected_ref.at[0, pl.ds(SPAN - 16, 16)], rim_ref.at[1]),
     )
     reads = [pltpu.make_async_copy(*part, sems.at[n]) for n, part in enumerate(parts)]
     for read in reads:
@@ -73,27 +74,45 @@
 
     reads[0].wait()
     store(16, long_ref[...].astype(BF))
-    reads[2].wait()
-    store(32, rows_ref[0])
-    for read in (reads[1], reads[3], reads[4]):
+    for read in reads[1:]:
         read.wait()
 
     def shaped(which):
         rows = rows_ref[which].astype(F32)
-        total = taps_ref[0, which : which + 1, :] * rows
+        total = taps_ref[0, which + 1 : which + 2, :] * rows
         for tap in (1, 2):
-            total = total + taps_ref[tap, which : which + 1, :] * pltpu.roll(rows, tap, 0)
+            total = total + taps_ref[tap, which + 1 : which + 2, :] * pltpu.roll(rows, tap, 0)
         return total
 
-    store(0, (shaped(1) * shaped(2)).astype(BF))
-    key, value = rows_ref[1], rows_ref[2]
-    first = [rows[:16].astype(F32)[:2] for rows in (key, value)]
-    last = [rows[SPAN - 16 :].astype(F32)[14:] for rows in (key, value)]
-    edges = jnp.concatenate(first + last + [jnp.zeros((120, SPAN), F32)], axis=0)
-    sent_ref[:, 48:56, :] = by_device(edges.T).astype(BF)
-    write = pltpu.make_async_copy(sent_ref, out_ref, sems.at[5])
+    store(0, (shaped(0) * shaped(1)).astype(BF))
+    key, value, query = rows_ref[0], rows_ref[1], rim_ref[...]
+    first = [key[:16], value[:16], query[0]]
+    last = [key[SPAN - 16 :], value[SPAN - 16 :], query[1]]
+    first = [rows.astype(F32)[:2] for rows in first]
+    last = [rows.astype(F32)[14:] for rows in last]
+    blank = jnp.zeros((2, SPAN), F32)
+    edges = jnp.concatenate(first + [blank] + last + [blank, jnp.zeros((112, SPAN), F32)], axis=0)
+    sent_ref[:, 32:40, :] = by_device(edges.T).astype(BF)
+    write = pltpu.make_async_copy(sent_ref, out_ref, sems.at[6])
     write.start()
     write.wait()
+
+
+def query_kernel(projected_ref, taps_ref, *rest):
+    *out_refs, rows_ref, sem = rest
+    read = pltpu.make_async_copy(projected_ref.at[0], rows_ref, sem)
+    read.start()
+    place = lax.axis_index("chan")
+    read.wait()
+    rows = rows_ref[...].astype(F32)
+    total = taps_ref[0, 0:1, :] * rows
+    for tap in (1, 2):
+        total = total + taps_ref[tap, 0:1, :] * pltpu.roll(rows, tap, 0)
+    total = jnp.where(lax.broadcasted_iota(jnp.int32, (SPAN, SPAN), 0) < 2, 1.0, total)
+    rows_ref[...] = total.astype(BF)
+    for step, out_ref in enumerate(out_refs):
+        block = lax.rem(place + 4 - step, 4)
+        out_ref[...] = rows_ref[pl.ds(pl.multiple_of(64 * block, 64), 64), :]
 
 
 def conv_kernel(got_ref, taps_ref, skip_ref, ahead_ref, fine_ref, turn_ref, back_ref, out_ref):
@@ -109,35 +128,25 @@
         both = got_ref[:, first_row : first_row + 16, :].astype(F32)
         return both[:, :8], both[:, 8:]
 
-    edges = got_ref[:, 48:56, :].astype(F32)
+    edges = got_ref[:, 32:40, :].astype(F32)
     before = jnp.concatenate([jnp.zeros((1, OWN, 128), F32), edges[:-1]], axis=0)
     thin = lax.broadcasted_iota(jnp.int32, (BLOCKS, OWN, 128), 2)
 
-    def left(rows, by):
-        return rows if by == 0 else pltpu.roll(rows, -by % 128, 2)
-
-    def gains(which):
-        return [own(taps_ref[tap, which : which + 1, :]) for tap in range(3)]
-
-    def edge(which, at):
-        first, second, third = gains(which)
-        once = jnp.where(thin == 0, left(before, at + 5), left(edges, at - 1))
-        return left(edges, at) * first + once * second + left(before, at + 4) * third
-
-    def later(rows, by):
-        turned = pltpu.roll(rows, by, 2)
-        earlier = jnp.concatenate([jnp.zeros((1, OWN, SPAN), F32), turned[:-1]], axis=0)
-        return jnp.where(lax.broadcasted_iota(jnp.int32, turned.shape, 2) < by, earlier, turned)
+    def shaped(which):
+        at = (4, 0, 2)[which]
+        left = lambda rows, by: rows if by % 128 == 0 else pltpu.roll(rows, -by % 128, 2)
+        now = left(edges, at)
+        once = jnp.where(thin == 0, left(before, at + 9), left(edges, at - 1))
+        twice = left(before, at + 8)
+        gains = [own(taps_ref[tap, which : which + 1, :]) for tap in range(3)]
+        return now * gains[0] + once * gains[1] + twice * gains[2]
 
     early, late = block(0)
-    early = jnp.where(thin < 2, edge(1, 0) * edge(2, 2), early)
+    early = jnp.where(thin < 2, shaped(1) * shaped(2), early)
     signal = jnp.concatenate([early.reshape(SPAN, 128), late.reshape(SPAN, 128)], axis=1).astype(BF)
     response = jnp.concatenate([half.reshape(SPAN, 128) for half in block(16)], axis=1).astype(BF)
     res_half = dot(ahead_ref[...], response)
     sig_half = dot(ahead_ref[...], signal)
-    raw = jnp.concatenate(block(32), axis=2)
-    first, second, third = gains(0)
-    query = raw * first + later(raw, 1) * second + later(raw, 2) * third
     cos, sin = turn_ref[:SPAN].astype(F32), turn_ref[SPAN:].astype(F32)
     fine_cos, fine_sin = fine_ref[:SPAN], fine_ref[SPAN:]
     fine_less = -fine_sin
@@ -165,29 +174,34 @@
     conv = dot(back_ref[...], turned.astype(BF))
     skip = own(skip_ref[...])
     direct = (signal.astype(F32).reshape(BLOCKS, OWN, SPAN) * skip).reshape(SPAN, SPAN)
-    gated = query * (conv + direct).reshape(BLOCKS, OWN, SPAN)
-    lows, highs = (rows.reshape(128, SPAN) for rows in swap_halves(gated))
+    mixed = (conv + direct).reshape(BLOCKS, OWN, SPAN)
+    early = jnp.where(thin < 2, mixed[:, :, :128] * shaped(0), mixed[:, :, :128])
+    halves = [[rows.reshape(128, 128) for rows in swap_halves(part)] for part in (early, mixed[:, :, 128:])]
     half = lax.broadcasted_iota(jnp.int32, (128, 128), 1) < 64
     for h in range(2):
-        low, high = lows[:, 128 * h : 128 * h + 128], highs[:, 128 * h : 128 * h + 128]
+        low, high = halves[h]
         even = jnp.where(half, low, pltpu.roll(high, 64, 1))
         odd = jnp.where(half, pltpu.roll(low, 64, 1), high)
         out_ref[256 * h : 256 * h + 128, :] = even.astype(BF)
         out_ref[256 * h + 128 : 256 * h + 256, :] = odd.astype(BF)
 
 
-def project_kernel(got_ref, own_ref, near_ref, swap_ref, other_ref, far_ref, far_swap_ref, out_ref):
+def project_kernel(got_ref, own_ref, near_ref, swap_ref, other_ref, far_ref, far_swap_ref, *rest):
+    *query_refs, out_ref = rest
     place = lax.axis_index("chan")
     odd = lax.axis_index("seq") % 2
 
-    def block(step):
+    def gated(step):
         owner = lax.rem(place + step, 4)
         rows = got_ref[pl.ds(pl.multiple_of(owner * 128, 128), 128), :].astype(F32).T
-        return jnp.concatenate([rows[:64], rows[64:]], axis=1).astype(BF)
-
-    total = dot(block(0), own_ref[...]) + dot(block(1 + 2 * odd), near_ref[...])
-    for step, here_ref, there_ref in ((3 - 2 * odd, other_ref, swap_ref), (2, far_ref, far_swap_ref)):
-        rows = block(step)
+        return (jnp.concatenate([rows[:64], rows[64:]], axis=1) * query_refs[step][...].astype(F32)).astype(BF)
+
+    blocks = [gated(step) for step in range(4)]
+    total = dot(blocks[0], own_ref[...]) + dot(jnp.where(odd == 0, blocks[1], blocks[3]), near_ref[...])
+    for rows, here_ref, there_ref in (
+        (jnp.where(odd == 0, blocks[3], blocks[1]), other_ref, swap_ref),
+        (blocks[2], far_ref, far_swap_ref),
+    ):
         total = total + dot(jnp.where(odd == 0, rows[:, :128], rows[:, 128:]), here_ref[...])
         total = total + dot(jnp.where(odd == 0, rows[:, 128:], rows[:, :128]), there_ref[...])
     out_ref[...] = total.astype(BF)
@@ -204,18 +218,31 @@
 def pack(projected, filters, short_taps):
     return pl.pallas_call(
         pack_kernel,
-        out_shape=jax.ShapeDtypeStruct((BLOCKS, 56, 128), BF),
+        out_shape=jax.ShapeDtypeStruct((BLOCKS, 40, 128), BF),
         in_specs=[HBM] * 3,
         out_specs=HBM,
         scratch_shapes=[
-            pltpu.VMEM((3, SPAN, SPAN), BF),
+            pltpu.VMEM((2, SPAN, SPAN), BF),
+            pltpu.VMEM((2, 16, SPAN), BF),
             pltpu.VMEM((SPAN, SPAN), F32),
             pltpu.VMEM((3, 3, SPAN), F32),
-            pltpu.VMEM((BLOCKS, 56, 128), BF),
-            pltpu.SemaphoreType.DMA((6,)),
+            pltpu.VMEM((BLOCKS, 40, 128), BF),
+            pltpu.SemaphoreType.DMA((7,)),
         ],
         cost_estimate=TINY,
     )(projected, filters, short_taps)
+
+
+def queries(projected, short_taps):
+    return pl.pallas_call(
+        query_kernel,
+        out_shape=[jax.ShapeDtypeStruct((64, SPAN), BF)] * 4,
+        in_specs=[HBM, VMEM],
+        out_specs=[VMEM] * 4,
+        scratch_shapes=[pltpu.VMEM((SPAN, SPAN), BF), pltpu.SemaphoreType.DMA],
+        compiler_params=PARAMS,
+        cost_estimate=TINY,
+    )(projected, short_taps)
 
 
 def convolve(got, short_taps, skip_gain):
@@ -231,33 +258,38 @@
     )(got, *held)
 
 
-def project(got, weights):
+def project(got, weights, query_blocks):
     return pl.pallas_call(
         project_kernel,
         out_shape=jax.ShapeDtypeStruct((64, 1024), BF),
-        in_specs=[VMEM] * (1 + len(weights)),
+        in_specs=[VMEM] * (1 + len(weights) + len(query_blocks)),
         out_specs=VMEM,
         compiler_params=PARAMS,
         cost_estimate=TINY,
-    )(got, *weights)
+    )(got, *weights, *query_blocks)
 
 
 def on_device(projected, short_taps, filters, skip_gain, out_weight):
     ring = [(s * 4 + (j + (1 if s % 2 == 0 else 3)) % 4, s * 4 + j) for s in range(BLOCKS) for j in range(4)]
+    pairs = [(s, s ^ 1) for s in range(BLOCKS)]
     near = lax.ppermute(out_weight, ("seq", "chan"), ring)
     core = lax.axis_index("seq") & 1
     half = lax.dynamic_slice_in_dim(near, 128 * core, 128, 0)
     other = lax.dynamic_slice_in_dim(near, 128 - 128 * core, 128, 0)
     far = lax.ppermute(half, ("seq", "chan"), ring)
-    pairs = [(s, s ^ 1) for s in range(BLOCKS)]
     swaps = [lax.ppermute(part, "seq", pairs) for part in (half, other)]
-    got = lax.all_to_all(pack(projected.transpose(1, 0, 2), filters, short_taps), "seq", split_axis=0, concat_axis=0, tiled=True)
+    by_part = projected.transpose(1, 0, 2)
+    got = lax.all_to_all(pack(by_part, filters, short_taps), "seq", split_axis=0, concat_axis=0, tiled=True)
+    query_blocks = [
+        block if step == 0 else lax.ppermute(block, "chan", [(j, (j - step) % 4) for j in range(4)])
+        for step, block in enumerate(queries(by_part, short_taps))
+    ]
     got, *swaps = lax.optimization_barrier((got, *swaps))
-    gated = convolve(got, short_taps, skip_gain)
-    gated, far = lax.optimization_barrier((gated, far))
+    mixed = convolve(got, short_taps, skip_gain)
+    _, far = lax.optimization_barrier((mixed, far))
     weights = (out_weight, near, *swaps, far, lax.ppermute(far, "seq", pairs))
-    got = lax.all_to_all(gated.reshape(128, 4, 128), ("chan", "seq"), split_axis=0, concat_axis=0, tiled=True)
-    return project(got.reshape(512, 128), weights)
+    got = lax.all_to_all(mixed.reshape(128, 4, 128), ("chan", "seq"), split_axis=0, concat_axis=0, tiled=True)
+    return project(got.reshape(512, 128), weights, query_blocks)
 
 
 def solution(mesh):

time: 42 us -> 41.6 us (level)
  blocking collectives: 13.3 us -> 0 us
  starting transfers between devices: 13 us -> 20.7 us
  waiting for transfers between devices: 10.3 us -> 14.6 us
  Pallas kernels: 4.79 us -> 5.71 us
    all_to_all x1 -> x0, blocking collectives: 13.3 us -> none  [on_device(): lax.all_to_all(gated.reshape(128, 4, 128), ('chan', 'seq'), split_axis=0,...]
    all_to_all x1 -> x2, starting transfers between devices: 10.3 us -> 14.2 us  [the longest x1 10.3 us: on_device(): lax.all_to_all(pack(by_part, filters, short_taps), 'seq', split_axis=0, c...]
    ppermute x0 -> x3, starting transfers between devices: none -> 3.84 us  [on_device(): lax.ppermute(block, 'chan', [(j, (j - step) % 4) for j in range(4)])]
    ppermute x0 -> x3, waiting for transfers between devices: none -> 3.78 us  [on_device(): lax.ppermute(block, 'chan', [(j, (j - step) % 4) for j in range(4)])]
    pallas_call x1, Pallas kernels: 1.38 us -> 2.06 us  [convolve(): pl.pallas_call(conv_kernel, out_shape=jax.ShapeDtypeStruct((512, 128), BF...]
    all_to_all x1 -> x2, waiting for transfers between devices: 10.3 us -> 10.8 us  [the longest x1 8.93 us: on_device(): lax.all_to_all(pack(by_part, filters, short_taps), 'seq', split_axis=0, c...]
    pallas_call x1 -> x2, Pallas kernels: 2.21 us -> 2.46 us  [the longest x1 2.11 us: pack(): pl.pallas_call(pack_kernel, out_shape=jax.ShapeDtypeStruct((BLOCKS, 40, 1...]
  transfers between devices with their start and end apart: 6 -> 10, of which waited for: 1 -> 4; matrix products, arithmetic and copies ran while one was open for 0% -> 0% of each run, Pallas kernels for 9% -> 11%
where the time goes in v5:
time: 41.6 us; the launch traced here: 41.3 us
  starting transfers between devices  20.7 us (50%)
  waiting for transfers between devices  14.6 us (35%)
  Pallas kernels  5.71 us (14%)
    all_to_all x1, starting transfers between devices, on_device(): lax.all_to_all(pack(by_part, filters, short_taps), 'seq', split_axis=0, c...  10.3 us
    all_to_all x1, waiting for transfers between devices, on_device(): lax.all_to_all(pack(by_part, filters, short_taps), 'seq', split_axis=0, c...  8.93 us
    all_to_all x1, starting transfers between devices, on_device(): lax.all_to_all(mixed.reshape(128, 4, 128), ('chan', 'seq'), split_axis=0,...  3.91 us
    ppermute x3, starting transfers between devices, on_device(): lax.ppermute(block, 'chan', [(j, (j - step) % 4) for j in range(4)])  3.84 us
    ppermute x3, waiting for transfers between devices, on_device(): lax.ppermute(block, 'chan', [(j, (j - step) % 4) for j in range(4)])  3.78 us
    pallas_call x1, Pallas kernels, pack(): pl.pallas_call(pack_kernel, out_shape=jax.ShapeDtypeStruct((BLOCKS, 40, 1...  2.11 us
    pallas_call x1, Pallas kernels, convolve(): pl.pallas_call(conv_kernel, out_shape=jax.ShapeDtypeStruct((512, 128), BF...  2.06 us
    ppermute x1, starting transfers between devices, on_device(): near = lax.ppermute(out_weight, ('seq', 'chan'), ring)  2.04 us
  transfers between devices with their start and end apart: 10, of which 4 were waited for; matrix products, arithmetic and copies ran while one was open for 0% of the time, Pallas kernels for 11%

profile of v5, /device:TPU:1, one launch (start us, length us, event | category | flops | bytes accessed | tf_op | source)
XLA Modules:
  0.0 41.3 jit_solution(17827025903311750611)
XLA Ops:
  0.0 2.0 %collective-permute-start = (bf16[256,1024]{1,0:T(8,128)(2,1)}, bf16[256,1024]{1,0:T(8,128)(2,1)S(1)}, u32[]{:S(2)}, u32[]{:S(2)}) collective-permute-start(bf16[256,1024]{1,0:T(8,128)(2,1)} %own_ref.1), channel_id=1, source_target_pairs={{1,0},{2,1},{3,2},{0,3},{7,4},{4,5},{5,6},{6,7},{9,8},{10,9},{11,1... | collective-permute-start | bytes 1572872 | tf_op jit(solution)/shard_map/ppermute | solution.py:275
  2.0 2.1 %shard_map.91 = bf16[32,40,128]{2,1,0:T(8,128)(2,1)} custom-call(bf16[3,256,256]{2,1,0:T(8,128)(2,1)} %bitcast.4, f32[256,256]{1,0:T(8,128)} %filters_ref.1, f32[3,3,256]{2,1,0:T(4,128)} %taps_ref.3), custom_call_target="tpu_custom_call" | custom-call | flops 1000 | bytes 1000 | tf_op jit(solution)/shard_map/pallas_call | solution.py:219
  4.2 0.0 copy-start.6
  4.2 10.3 %all-to-all-start = ((bf16[32,40,128]{2,1,0:T(8,128)(2,1)}), bf16[32,40,128]{2,1,0:T(8,128)(2,1)S(1)}, u32[]{:S(2)}, u32[]{:S(2)}) async-start(bf16[32,40,128]{2,1,0:T(8,128)(2,1)} %shard_map.91), calls=%async_computation | async-start | bytes 655360 | tf_op jit(solution)/shard_map/all_to_all | solution.py:282
  14.5 0.0 copy-start.2
  14.5 0.0 copy-start.3
  14.5 0.0 copy-start.4
  14.6 0.0 copy-start.5
  14.6 0.3 collective-permute-start.1
  14.9 0.3 collective-permute-start.2
  15.2 0.0 collective-permute-start.3
  15.2 8.9 %all-to-all-done.got_ref = bf16[32,40,128]{2,1,0:T(8,128)(2,1)S(1)} async-done(((bf16[32,40,128]{2,1,0:T(8,128)(2,1)}), bf16[32,40,128]{2,1,0:T(8,128)(2,1)S(1)}, u32[]{:S(2)}, u32[]{:S(2)}) %all-to-all-start) | async-done | bytes 327712 | tf_op jit(solution)/shard_map/all_to_all | solution.py:282
  24.2 0.0 copy-start
  24.2 2.1 %shard_map.92 = bf16[512,128]{1,0:T(8,128)(2,1)} custom-call(bf16[32,40,128]{2,1,0:T(8,128)(2,1)S(1)} %all-to-all-done.got_ref, f32[3,3,256]{2,1,0:T(4,128)S(1)} %copy-done.6, f32[1,256]{1,0:T(1,128)S(1)} %bitcast.7, bf16[512,256]{1,0:T(8,128)(2,1)S(1)} %copy-done.2, bf16[512,256]{1,0:T(8,128)(2,1)S(1)} %copy-done.3, bf16[512,256]{1,0:T(8,128)(2,1)S(1)} %copy-done.4, ...), custom_call_target="tpu_custom_call" | custom-call | flops 1000 | bytes 1000 | tf_op jit(solution)/shard_map/pallas_call | solution.py:251
  26.3 0.0 collective-permute-start.4
  26.3 3.9 %all-to-all-start.1 = ((bf16[128,4,128]{2,1,0:T(4,128)(2,1)}), bf16[128,4,128]{2,1,0:T(4,128)(2,1)S(1)}, u32[]{:S(2)}, u32[]{:S(2)}) async-start(bf16[128,4,128]{2,1,0:T(4,128)(2,1)} %bitcast.2), calls=%async_computation.1 | async-start | bytes 262144 | tf_op jit(solution)/shard_map/all_to_all | solution.py:291
  30.2 0.3 shard_map.93
  30.6 2.7 %collective-permute-start.5 = (bf16[64,256]{1,0:T(8,128)(2,1)S(1)}, bf16[64,256]{1,0:T(8,128)(2,1)S(1)}, u32[]{:S(2)}, u32[]{:S(2)}) collective-permute-start(bf16[64,256]{1,0:T(8,128)(2,1)S(1)} %get-tuple-element.18), channel_id=1, source_target_pairs={{0,3},{1,0},{2,1},{3,2},{4,7},{5,4},{6,5},{7,6},{8,11},{9,8},{10,9... | collective-permute-start | bytes 98312 | tf_op jit(solution)/shard_map/ppermute | solution.py:284
  33.3 0.5 %collective-permute-start.6 = (bf16[64,256]{1,0:T(8,128)(2,1)S(1)}, bf16[64,256]{1,0:T(8,128)(2,1)S(1)}, u32[]{:S(2)}, u32[]{:S(2)}) collective-permute-start(bf16[64,256]{1,0:T(8,128)(2,1)S(1)} %get-tuple-element.19), channel_id=1, source_target_pairs={{0,2},{1,3},{2,0},{3,1},{4,6},{5,7},{6,4},{7,5},{8,10},{9,11},{10,... | collective-permute-start | bytes 98312 | tf_op jit(solution)/shard_map/ppermute | solution.py:284
  33.8 0.6 %collective-permute-start.7 = (bf16[64,256]{1,0:T(8,128)(2,1)S(1)}, bf16[64,256]{1,0:T(8,128)(2,1)S(1)}, u32[]{:S(2)}, u32[]{:S(2)}) collective-permute-start(bf16[64,256]{1,0:T(8,128)(2,1)S(1)} %get-tuple-element.20), channel_id=1, source_target_pairs={{0,1},{1,2},{2,3},{3,0},{4,5},{5,6},{6,7},{7,4},{8,9},{9,10},{10,1... | collective-permute-start | bytes 98312 | tf_op jit(solution)/shard_map/ppermute | solution.py:284
  34.4 3.4 %collective-permute-done.6.rest_2_ = bf16[64,256]{1,0:T(8,128)(2,1)S(1)} collective-permute-done((bf16[64,256]{1,0:T(8,128)(2,1)S(1)}, bf16[64,256]{1,0:T(8,128)(2,1)S(1)}, u32[]{:S(2)}, u32[]{:S(2)}) %collective-permute-start.6) | collective-permute-done | bytes 32800 | tf_op jit(solution)/shard_map/ppermute | solution.py:284
  37.9 0.4 collective-permute-done.7.rest_3_
  38.2 1.9 %all-to-all-done.1 = bf16[128,4,128]{2,1,0:T(4,128)(2,1)S(1)} async-done(((bf16[128,4,128]{2,1,0:T(4,128)(2,1)}), bf16[128,4,128]{2,1,0:T(4,128)(2,1)S(1)}, u32[]{:S(2)}, u32[]{:S(2)}) %all-to-all-start.1) | async-done | bytes 131104 | tf_op jit(solution)/shard_map/all_to_all | solution.py:291
  40.1 1.2 %shard_map.94 = bf16[64,1024]{1,0:T(8,128)(2,1)} custom-call(bf16[512,128]{1,0:T(8,128)(2,1)S(1)} %bitcast.6, bf16[256,1024]{1,0:T(8,128)(2,1)S(1)} %copy-done.1, bf16[256,1024]{1,0:T(8,128)(2,1)S(1)} %collective-permute-done.near_ref, bf16[128,1024]{1,0:T(8,128)(2,1)S(1)} %collective-permute-done.1.swap_ref, ...), custom_call_target="tpu_custom_call" | custom-call | flops 1000 | bytes 1000 | tf_op jit(solution)/shard_map/pallas_call | solution.py:262
  (17 shorter events, 0.1 us)
Async XLA Ops:
  0.0 14.6 %collective-permute-start = (bf16[256,1024]{1,0:T(8,128)(2,1)}, bf16[256,1024]{1,0:T(8,128)(2,1)S(1)}, u32[]{:S(2)}, u32[]{:S(2)}) collective-permute-start(bf16[256,1024]{1,0:T(8,128)(2,1)} %own_ref.1), channel_id=1, source_target_pairs={{1,0},{2,1},{3,2},{0,3},{7,4},{4,5},{5,6},{6,7},{9,8},{10,9},{11,1... | collective-permute-start | bytes 1572872 | tf_op jit(solution)/shard_map/ppermute | solution.py:275
  4.2 20.0 %copy-start.6 = (f32[3,3,256]{2,1,0:T(4,128)S(1)}, f32[3,3,256]{2,1,0:T(4,128)}, u32[]{:S(2)}) copy-start(f32[3,3,256]{2,1,0:T(4,128)} %taps_ref.3) | copy-start | bytes 27652
  4.2 20.0 %all-to-all-start = ((bf16[32,40,128]{2,1,0:T(8,128)(2,1)}), bf16[32,40,128]{2,1,0:T(8,128)(2,1)S(1)}, u32[]{:S(2)}, u32[]{:S(2)}) async-start(bf16[32,40,128]{2,1,0:T(8,128)(2,1)} %shard_map.91), calls=%async_computation | async-start | bytes 655360 | tf_op jit(solution)/shard_map/all_to_all | solution.py:282
  14.5 9.7 %copy-start.2 = (bf16[512,256]{1,0:T(8,128)(2,1)S(1)}, bf16[512,256]{1,0:T(8,128)(2,1)}, u32[]{:S(2)}) copy-start(bf16[512,256]{1,0:T(8,128)(2,1)} %constant.28.ahead_ref) | copy-start | bytes 786436
  14.5 9.7 %copy-start.3 = (bf16[512,256]{1,0:T(8,128)(2,1)S(1)}, bf16[512,256]{1,0:T(8,128)(2,1)}, u32[]{:S(2)}) copy-start(bf16[512,256]{1,0:T(8,128)(2,1)} %constant.29.fine_ref) | copy-start | bytes 786436
  14.5 9.7 %copy-start.4 = (bf16[512,256]{1,0:T(8,128)(2,1)S(1)}, bf16[512,256]{1,0:T(8,128)(2,1)}, u32[]{:S(2)}) copy-start(bf16[512,256]{1,0:T(8,128)(2,1)} %constant.30.turn_ref) | copy-start | bytes 786436
  14.6 9.6 %copy-start.5 = (bf16[256,512]{1,0:T(8,128)(2,1)S(1)}, bf16[256,512]{1,0:T(8,128)(2,1)}, u32[]{:S(2)}) copy-start(bf16[256,512]{1,0:T(8,128)(2,1)} %constant.31.back_ref) | copy-start | bytes 786436
  14.6 9.5 %collective-permute-start.1 = (bf16[128,1024]{1,0:T(8,128)(2,1)S(1)}, bf16[128,1024]{1,0:T(8,128)(2,1)S(1)}, u32[]{:S(2)}, u32[]{:S(2)}) collective-permute-start(bf16[128,1024]{1,0:T(8,128)(2,1)S(1)} %get-tuple-element.22), channel_id=1, source_target_pairs={{0,4},{4,0},{8,12},{12,8},{16,20},{20,16},{24,28},{28,24},{32,36},... | collective-permute-start | bytes 786440 | tf_op jit(solution)/shard_map/ppermute | solution.py:280
  14.9 9.3 %copy-start.7 = (f32[256]{0:T(256)S(1)}, f32[256]{0:T(256)}, u32[]{:S(2)}) copy-start(f32[256]{0:T(256)} %param.12) | copy-start | bytes 3076
  14.9 9.2 %collective-permute-start.2 = (bf16[128,1024]{1,0:T(8,128)(2,1)S(1)}, bf16[128,1024]{1,0:T(8,128)(2,1)S(1)}, u32[]{:S(2)}, u32[]{:S(2)}) collective-permute-start(bf16[128,1024]{1,0:T(8,128)(2,1)S(1)} %get-tuple-element.21), channel_id=1, source_target_pairs={{0,4},{4,0},{8,12},{12,8},{16,20},{20,16},{24,28},{28,24},{32,36},... | collective-permute-start | bytes 786440 | tf_op jit(solution)/shard_map/ppermute | solution.py:280
  15.2 11.1 %collective-permute-start.3 = (bf16[128,1024]{1,0:T(8,128)(2,1)S(1)}, bf16[128,1024]{1,0:T(8,128)(2,1)S(1)}, u32[]{:S(2)}, u32[]{:S(2)}) collective-permute-start(bf16[128,1024]{1,0:T(8,128)(2,1)S(1)} %get-tuple-element.22), channel_id=1, source_target_pairs={{1,0},{2,1},{3,2},{0,3},{7,4},{4,5},{5,6},{6,7},{9,8},{10,9},{11,1... | collective-permute-start | bytes 786440 | tf_op jit(solution)/shard_map/ppermute | solution.py:279
  24.2 6.0 %copy-start = (bf16[256,3,256]{2,0,1:T(8,128)(2,1)S(1)}, bf16[256,3,256]{2,0,1:T(8,128)(2,1)}, u32[]{:S(2)}) copy-start(bf16[256,3,256]{2,0,1:T(8,128)(2,1)} %param.9) | copy-start | bytes 1179652
  26.3 13.8 %copy-start.1 = (bf16[256,1024]{1,0:T(8,128)(2,1)S(1)}, bf16[256,1024]{1,0:T(8,128)(2,1)}, u32[]{:S(2)}) copy-start(bf16[256,1024]{1,0:T(8,128)(2,1)} %own_ref.1) | copy-start | bytes 1572868
  26.3 13.8 %collective-permute-start.4 = (bf16[128,1024]{1,0:T(8,128)(2,1)S(1)}, bf16[128,1024]{1,0:T(8,128)(2,1)S(1)}, u32[]{:S(2)}, u32[]{:S(2)}) collective-permute-start(bf16[128,1024]{1,0:T(8,128)(2,1)S(1)} %collective-permute-done.3.far_ref), channel_id=1, source_target_pairs={{0,4},{4,0},{8,12},{12,8},{16,20},{20,16},{24,28},{28,24},{32,36},... | collective-permute-start | bytes 786440 | tf_op jit(solution)/shard_map/ppermute | solution.py:290
  26.3 13.8 %all-to-all-start.1 = ((bf16[128,4,128]{2,1,0:T(4,128)(2,1)}), bf16[128,4,128]{2,1,0:T(4,128)(2,1)S(1)}, u32[]{:S(2)}, u32[]{:S(2)}) async-start(bf16[128,4,128]{2,1,0:T(4,128)(2,1)} %bitcast.2), calls=%async_computation.1 | async-start | bytes 262144 | tf_op jit(solution)/shard_map/all_to_all | solution.py:291
  30.6 3.8 %collective-permute-start.5 = (bf16[64,256]{1,0:T(8,128)(2,1)S(1)}, bf16[64,256]{1,0:T(8,128)(2,1)S(1)}, u32[]{:S(2)}, u32[]{:S(2)}) collective-permute-start(bf16[64,256]{1,0:T(8,128)(2,1)S(1)} %get-tuple-element.18), channel_id=1, source_target_pairs={{0,3},{1,0},{2,1},{3,2},{4,7},{5,4},{6,5},{7,6},{8,11},{9,8},{10,9... | collective-permute-start | bytes 98312 | tf_op jit(solution)/shard_map/ppermute | solution.py:284
  33.3 4.6 %collective-permute-start.6 = (bf16[64,256]{1,0:T(8,128)(2,1)S(1)}, bf16[64,256]{1,0:T(8,128)(2,1)S(1)}, u32[]{:S(2)}, u32[]{:S(2)}) collective-permute-start(bf16[64,256]{1,0:T(8,128)(2,1)S(1)} %get-tuple-element.19), channel_id=1, source_target_pairs={{0,2},{1,3},{2,0},{3,1},{4,6},{5,7},{6,4},{7,5},{8,10},{9,11},{10,... | collective-permute-start | bytes 98312 | tf_op jit(solution)/shard_map/ppermute | solution.py:284
  33.8 4.4 %collective-permute-start.7 = (bf16[64,256]{1,0:T(8,128)(2,1)S(1)}, bf16[64,256]{1,0:T(8,128)(2,1)S(1)}, u32[]{:S(2)}, u32[]{:S(2)}) collective-permute-start(bf16[64,256]{1,0:T(8,128)(2,1)S(1)} %get-tuple-element.20), channel_id=1, source_target_pairs={{0,1},{1,2},{2,3},{3,0},{4,5},{5,6},{6,7},{7,4},{8,9},{9,10},{10,1... | collective-permute-start | bytes 98312 | tf_op jit(solution)/shard_map/ppermute | solution.py:284

commit v6 on v5

--- a/solution.py
+++ b/solution.py
@@ -68,12 +68,12 @@
         both = jnp.stack([turned[0], turned[1]], axis=1).reshape(BLOCKS, OWN, columns)
         return jnp.stack(swap_halves(both), axis=1).reshape(BLOCKS, OWN, columns)
 
-    def store(first_row, rows):
+    def halves(rows):
         both = by_device(rows.T)
-        sent_ref[:, first_row : first_row + 16, :] = jnp.concatenate([both[:, :, :128], both[:, :, 128:]], axis=1).astype(BF)
+        return [both[:, :, :128], both[:, :, 128:]]
 
     reads[0].wait()
-    store(16, long_ref[...].astype(BF))
+    long = halves(long_ref[...].astype(BF))
     for read in reads[1:]:
         read.wait()
 
@@ -84,7 +84,7 @@
             total = total + taps_ref[tap, which + 1 : which + 2, :] * pltpu.roll(rows, tap, 0)
         return total
 
-    store(0, (shaped(0) * shaped(1)).astype(BF))
+    signal = halves((shaped(0) * shaped(1)).astype(BF))
     key, value, query = rows_ref[0], rows_ref[1], rim_ref[...]
     first = [key[:16], value[:16], query[0]]
     last = [key[SPAN - 16 :], value[SPAN - 16 :], query[1]]
@@ -92,7 +92,8 @@
     last = [rows.astype(F32)[14:] for rows in last]
     blank = jnp.zeros((2, SPAN), F32)
     edges = jnp.concatenate(first + [blank] + last + [blank, jnp.zeros((112, SPAN), F32)], axis=0)
-    sent_ref[:, 32:40, :] = by_device(edges.T).astype(BF)
+    message = jnp.concatenate(signal + long + [by_device(edges.T)], axis=1)
+    sent_ref[...] = message.reshape(BLOCKS * 40, 128).astype(BF)
     write = pltpu.make_async_copy(sent_ref, out_ref, sems.at[6])
     write.start()
     write.wait()
@@ -124,11 +125,12 @@
     def own(values):
         return jnp.sum(jnp.where(mine, values, 0.0), axis=1, keepdims=True)[None]
 
+    got = got_ref[...].astype(F32).reshape(BLOCKS, 40, 128)
+
     def block(first_row):
-        both = got_ref[:, first_row : first_row + 16, :].astype(F32)
-        return both[:, :8], both[:, 8:]
-
-    edges = got_ref[:, 32:40, :].astype(F32)
+        return got[:, first_row : first_row + 8], got[:, first_row + 8 : first_row + 16]
+
+    edges = got[:, 32:40]
     before = jnp.concatenate([jnp.zeros((1, OWN, 128), F32), edges[:-1]], axis=0)
     thin = lax.broadcasted_iota(jnp.int32, (BLOCKS, OWN, 128), 2)
 
@@ -218,7 +220,7 @@
 def pack(projected, filters, short_taps):
     return pl.pallas_call(
         pack_kernel,
-        out_shape=jax.ShapeDtypeStruct((BLOCKS, 40, 128), BF),
+        out_shape=jax.ShapeDtypeStruct((BLOCKS * 40, 128), BF),
         in_specs=[HBM] * 3,
         out_specs=HBM,
         scratch_shapes=[
@@ -226,7 +228,7 @@
             pltpu.VMEM((2, 16, SPAN), BF),
             pltpu.VMEM((SPAN, SPAN), F32),
             pltpu.VMEM((3, 3, SPAN), F32),
-            pltpu.VMEM((BLOCKS, 40, 128), BF),
+            pltpu.VMEM((BLOCKS * 40, 128), BF),
             pltpu.SemaphoreType.DMA((7,)),
         ],
         cost_estimate=TINY,
@@ -279,7 +281,8 @@
     far = lax.ppermute(half, ("seq", "chan"), ring)
     swaps = [lax.ppermute(part, "seq", pairs) for part in (half, other)]
     by_part = projected.transpose(1, 0, 2)
-    got = lax.all_to_all(pack(by_part, filters, short_taps), "seq", split_axis=0, concat_axis=0, tiled=True)
+    packed = pack(by_part, filters, short_taps).reshape(BLOCKS, 40, 128)
+    got = lax.all_to_all(packed, "seq", split_axis=0, concat_axis=0, tiled=True).reshape(BLOCKS * 40, 128)
     query_blocks = [
         block if step == 0 else lax.ppermute(block, "chan", [(j, (j - step) % 4) for j in range(4)])
         for step, block in enumerate(queries(by_part, short_taps))

time: 41.6 us -> 41.6 us (level)
  no operation moved by 1% of the time
where the time goes in v6:
time: 41.6 us; the launch traced here: 41.3 us
  starting transfers between devices  20.7 us (50%)
  waiting for transfers between devices  14.6 us (35%)
  Pallas kernels  5.71 us (14%)
    all_to_all x1, starting transfers between devices, on_device(): lax.all_to_all(packed, 'seq', split_axis=0, concat_axis=0, tiled=True)  10.3 us
    all_to_all x1, waiting for transfers between devices, on_device(): lax.all_to_all(packed, 'seq', split_axis=0, concat_axis=0, tiled=True)  8.92 us
    all_to_all x1, starting transfers between devices, on_device(): lax.all_to_all(mixed.reshape(128, 4, 128), ('chan', 'seq'), split_axis=0,...  3.91 us
    ppermute x3, starting transfers between devices, on_device(): lax.ppermute(block, 'chan', [(j, (j - step) % 4) for j in range(4)])  3.84 us
    ppermute x3, waiting for transfers between devices, on_device(): lax.ppermute(block, 'chan', [(j, (j - step) % 4) for j in range(4)])  3.78 us
    pallas_call x1, Pallas kernels, pack(): pl.pallas_call(pack_kernel, out_shape=jax.ShapeDtypeStruct((BLOCKS * 40,...  2.14 us
    ppermute x1, starting transfers between devices, on_device(): near = lax.ppermute(out_weight, ('seq', 'chan'), ring)  2.04 us
    pallas_call x1, Pallas kernels, convolve(): pl.pallas_call(conv_kernel, out_shape=jax.ShapeDtypeStruct((512, 128), BF...  2.03 us
  transfers between devices with their start and end apart: 10, of which 4 were waited for; matrix products, arithmetic and copies ran while one was open for 0% of the time, Pallas kernels for 11%

profile of v6, /device:TPU:1, one launch (start us, length us, event | category | flops | bytes accessed | tf_op | source)
XLA Modules:
  0.0 41.3 jit_solution(13206633445268862782)
XLA Ops:
  0.0 2.0 %collective-permute-start = (bf16[256,1024]{1,0:T(8,128)(2,1)}, bf16[256,1024]{1,0:T(8,128)(2,1)S(1)}, u32[]{:S(2)}, u32[]{:S(2)}) collective-permute-start(bf16[256,1024]{1,0:T(8,128)(2,1)} %own_ref.1), channel_id=1, source_target_pairs={{1,0},{2,1},{3,2},{0,3},{7,4},{4,5},{5,6},{6,7},{9,8},{10,9},{11,1... | collective-permute-start | bytes 1572872 | tf_op jit(solution)/shard_map/ppermute | solution.py:277
  2.0 2.1 %shard_map.91 = bf16[1280,128]{1,0:T(8,128)(2,1)} custom-call(bf16[3,256,256]{2,1,0:T(8,128)(2,1)} %bitcast.6, f32[256,256]{1,0:T(8,128)} %filters_ref.1, f32[3,3,256]{2,1,0:T(4,128)} %taps_ref.3), custom_call_target="tpu_custom_call" | custom-call | flops 1000 | bytes 1000 | tf_op jit(solution)/shard_map/pallas_call | solution.py:221
  4.2 0.0 copy-start.7
  4.2 10.3 %all-to-all-start = ((bf16[32,40,128]{2,1,0:T(8,128)(2,1)}), bf16[32,40,128]{2,1,0:T(8,128)(2,1)S(1)}, u32[]{:S(2)}, u32[]{:S(2)}) async-start(bf16[32,40,128]{2,1,0:T(8,128)(2,1)} %bitcast.11), calls=%async_computation | async-start | bytes 655360 | tf_op jit(solution)/shard_map/all_to_all | solution.py:285
  14.5 0.0 copy-start.6
  14.6 0.0 copy-start.2
  14.6 0.0 copy-start.3
  14.6 0.0 copy-start.4
  14.6 0.0 copy-start.5
  14.7 0.3 collective-permute-start.1
  15.0 0.3 collective-permute-start.2
  15.3 8.9 %all-to-all-done = bf16[32,40,128]{2,1,0:T(8,128)(2,1)S(1)} async-done(((bf16[32,40,128]{2,1,0:T(8,128)(2,1)}), bf16[32,40,128]{2,1,0:T(8,128)(2,1)S(1)}, u32[]{:S(2)}, u32[]{:S(2)}) %all-to-all-start) | async-done | bytes 327712 | tf_op jit(solution)/shard_map/all_to_all | solution.py:285
  24.2 0.0 copy-start
  24.3 2.0 %shard_map.92 = bf16[512,128]{1,0:T(8,128)(2,1)} custom-call(bf16[1280,128]{1,0:T(8,128)(2,1)S(1)} %bitcast.8, f32[3,3,256]{2,1,0:T(4,128)S(1)} %copy-done.6, f32[1,256]{1,0:T(1,128)S(1)} %bitcast.10, bf16[512,256]{1,0:T(8,128)(2,1)S(1)} %copy-done.2, bf16[512,256]{1,0:T(8,128)(2,1)S(1)} %copy-done.3, bf16[512,256]{1,0:T(8,128)(2,1)S(1)} %copy-done.4, ...), custom_call_target="tpu_custom_call" | custom-call | flops 1000 | bytes 1000 | tf_op jit(solution)/shard_map/pallas_call | solution.py:253
  26.3 0.0 collective-permute-start.4
  26.3 3.9 %all-to-all-start.1 = ((bf16[128,4,128]{2,1,0:T(4,128)(2,1)}), bf16[128,4,128]{2,1,0:T(4,128)(2,1)S(1)}, u32[]{:S(2)}, u32[]{:S(2)}) async-start(bf16[128,4,128]{2,1,0:T(4,128)(2,1)} %bitcast.4), calls=%async_computation.1 | async-start | bytes 262144 | tf_op jit(solution)/shard_map/all_to_all | solution.py:294
  30.2 0.3 shard_map.93
  30.6 2.7 %collective-permute-start.5 = (bf16[64,256]{1,0:T(8,128)(2,1)S(1)}, bf16[64,256]{1,0:T(8,128)(2,1)S(1)}, u32[]{:S(2)}, u32[]{:S(2)}) collective-permute-start(bf16[64,256]{1,0:T(8,128)(2,1)S(1)} %get-tuple-element.18), channel_id=1, source_target_pairs={{0,3},{1,0},{2,1},{3,2},{4,7},{5,4},{6,5},{7,6},{8,11},{9,8},{10,9... | collective-permute-start | bytes 98312 | tf_op jit(solution)/shard_map/ppermute | solution.py:287
  33.3 0.5 %collective-permute-start.6 = (bf16[64,256]{1,0:T(8,128)(2,1)S(1)}, bf16[64,256]{1,0:T(8,128)(2,1)S(1)}, u32[]{:S(2)}, u32[]{:S(2)}) collective-permute-start(bf16[64,256]{1,0:T(8,128)(2,1)S(1)} %get-tuple-element.19), channel_id=1, source_target_pairs={{0,2},{1,3},{2,0},{3,1},{4,6},{5,7},{6,4},{7,5},{8,10},{9,11},{10,... | collective-permute-start | bytes 98312 | tf_op jit(solution)/shard_map/ppermute | solution.py:287
  33.8 0.6 %collective-permute-start.7 = (bf16[64,256]{1,0:T(8,128)(2,1)S(1)}, bf16[64,256]{1,0:T(8,128)(2,1)S(1)}, u32[]{:S(2)}, u32[]{:S(2)}) collective-permute-start(bf16[64,256]{1,0:T(8,128)(2,1)S(1)} %get-tuple-element.20), channel_id=1, source_target_pairs={{0,1},{1,2},{2,3},{3,0},{4,5},{5,6},{6,7},{7,4},{8,9},{9,10},{10,1... | collective-permute-start | bytes 98312 | tf_op jit(solution)/shard_map/ppermute | solution.py:287
  34.4 3.4 %collective-permute-done.6.rest_2_ = bf16[64,256]{1,0:T(8,128)(2,1)S(1)} collective-permute-done((bf16[64,256]{1,0:T(8,128)(2,1)S(1)}, bf16[64,256]{1,0:T(8,128)(2,1)S(1)}, u32[]{:S(2)}, u32[]{:S(2)}) %collective-permute-start.6) | collective-permute-done | bytes 32800 | tf_op jit(solution)/shard_map/ppermute | solution.py:287
  37.9 0.4 collective-permute-done.7.rest_3_
  38.2 1.9 %all-to-all-done.1 = bf16[128,4,128]{2,1,0:T(4,128)(2,1)S(1)} async-done(((bf16[128,4,128]{2,1,0:T(4,128)(2,1)}), bf16[128,4,128]{2,1,0:T(4,128)(2,1)S(1)}, u32[]{:S(2)}, u32[]{:S(2)}) %all-to-all-start.1) | async-done | bytes 131104 | tf_op jit(solution)/shard_map/all_to_all | solution.py:294
  40.1 1.2 %shard_map.94 = bf16[64,1024]{1,0:T(8,128)(2,1)} custom-call(bf16[512,128]{1,0:T(8,128)(2,1)S(1)} %bitcast.9, bf16[256,1024]{1,0:T(8,128)(2,1)S(1)} %copy-done.1, bf16[256,1024]{1,0:T(8,128)(2,1)S(1)} %collective-permute-done.near_ref, bf16[128,1024]{1,0:T(8,128)(2,1)S(1)} %collective-permute-done.1.swap_ref, ...), custom_call_target="tpu_custom_call" | custom-call | flops 1000 | bytes 1000 | tf_op jit(solution)/shard_map/pallas_call | solution.py:264
  (17 shorter events, 0.1 us)
Async XLA Ops:
  0.0 14.6 %collective-permute-start = (bf16[256,1024]{1,0:T(8,128)(2,1)}, bf16[256,1024]{1,0:T(8,128)(2,1)S(1)}, u32[]{:S(2)}, u32[]{:S(2)}) collective-permute-start(bf16[256,1024]{1,0:T(8,128)(2,1)} %own_ref.1), channel_id=1, source_target_pairs={{1,0},{2,1},{3,2},{0,3},{7,4},{4,5},{5,6},{6,7},{9,8},{10,9},{11,1... | collective-permute-start | bytes 1572872 | tf_op jit(solution)/shard_map/ppermute | solution.py:277
  4.2 20.0 %copy-start.7 = (f32[256]{0:T(256)S(1)}, f32[256]{0:T(256)}, u32[]{:S(2)}) copy-start(f32[256]{0:T(256)} %param.12) | copy-start | bytes 3076
  4.2 20.0 %all-to-all-start = ((bf16[32,40,128]{2,1,0:T(8,128)(2,1)}), bf16[32,40,128]{2,1,0:T(8,128)(2,1)S(1)}, u32[]{:S(2)}, u32[]{:S(2)}) async-start(bf16[32,40,128]{2,1,0:T(8,128)(2,1)} %bitcast.11), calls=%async_computation | async-start | bytes 655360 | tf_op jit(solution)/shard_map/all_to_all | solution.py:285
  14.5 9.7 %copy-start.6 = (f32[3,3,256]{2,1,0:T(4,128)S(1)}, f32[3,3,256]{2,1,0:T(4,128)}, u32[]{:S(2)}) copy-start(f32[3,3,256]{2,1,0:T(4,128)} %taps_ref.3) | copy-start | bytes 27652
  14.6 9.7 %copy-start.2 = (bf16[512,256]{1,0:T(8,128)(2,1)S(1)}, bf16[512,256]{1,0:T(8,128)(2,1)}, u32[]{:S(2)}) copy-start(bf16[512,256]{1,0:T(8,128)(2,1)} %constant.28.ahead_ref) | copy-start | bytes 786436
  14.6 9.7 %copy-start.3 = (bf16[512,256]{1,0:T(8,128)(2,1)S(1)}, bf16[512,256]{1,0:T(8,128)(2,1)}, u32[]{:S(2)}) copy-start(bf16[512,256]{1,0:T(8,128)(2,1)} %constant.29.fine_ref) | copy-start | bytes 786436
  14.6 9.6 %copy-start.4 = (bf16[512,256]{1,0:T(8,128)(2,1)S(1)}, bf16[512,256]{1,0:T(8,128)(2,1)}, u32[]{:S(2)}) copy-start(bf16[512,256]{1,0:T(8,128)(2,1)} %constant.30.turn_ref) | copy-start | bytes 786436
  14.6 9.6 %copy-start.5 = (bf16[256,512]{1,0:T(8,128)(2,1)S(1)}, bf16[256,512]{1,0:T(8,128)(2,1)}, u32[]{:S(2)}) copy-start(bf16[256,512]{1,0:T(8,128)(2,1)} %constant.31.back_ref) | copy-start | bytes 786436
  14.7 9.5 %collective-permute-start.1 = (bf16[128,1024]{1,0:T(8,128)(2,1)S(1)}, bf16[128,1024]{1,0:T(8,128)(2,1)S(1)}, u32[]{:S(2)}, u32[]{:S(2)}) collective-permute-start(bf16[128,1024]{1,0:T(8,128)(2,1)S(1)} %get-tuple-element.22), channel_id=1, source_target_pairs={{0,4},{4,0},{8,12},{12,8},{16,20},{20,16},{24,28},{28,24},{32,36},... | collective-permute-start | bytes 786440 | tf_op jit(solution)/shard_map/ppermute | solution.py:282
  15.0 9.2 %collective-permute-start.2 = (bf16[128,1024]{1,0:T(8,128)(2,1)S(1)}, bf16[128,1024]{1,0:T(8,128)(2,1)S(1)}, u32[]{:S(2)}, u32[]{:S(2)}) collective-permute-start(bf16[128,1024]{1,0:T(8,128)(2,1)S(1)} %get-tuple-element.21), channel_id=1, source_target_pairs={{0,4},{4,0},{8,12},{12,8},{16,20},{20,16},{24,28},{28,24},{32,36},... | collective-permute-start | bytes 786440 | tf_op jit(solution)/shard_map/ppermute | solution.py:282
  15.3 11.0 %collective-permute-start.3 = (bf16[128,1024]{1,0:T(8,128)(2,1)S(1)}, bf16[128,1024]{1,0:T(8,128)(2,1)S(1)}, u32[]{:S(2)}, u32[]{:S(2)}) collective-permute-start(bf16[128,1024]{1,0:T(8,128)(2,1)S(1)} %get-tuple-element.22), channel_id=1, source_target_pairs={{1,0},{2,1},{3,2},{0,3},{7,4},{4,5},{5,6},{6,7},{9,8},{10,9},{11,1... | collective-permute-start | bytes 786440 | tf_op jit(solution)/shard_map/ppermute | solution.py:281
  24.2 6.0 %copy-start = (bf16[256,3,256]{2,0,1:T(8,128)(2,1)S(1)}, bf16[256,3,256]{2,0,1:T(8,128)(2,1)}, u32[]{:S(2)}) copy-start(bf16[256,3,256]{2,0,1:T(8,128)(2,1)} %param.9) | copy-start | bytes 1179652
  26.3 13.8 %copy-start.1 = (bf16[256,1024]{1,0:T(8,128)(2,1)S(1)}, bf16[256,1024]{1,0:T(8,128)(2,1)}, u32[]{:S(2)}) copy-start(bf16[256,1024]{1,0:T(8,128)(2,1)} %own_ref.1) | copy-start | bytes 1572868
  26.3 13.8 %collective-permute-start.4 = (bf16[128,1024]{1,0:T(8,128)(2,1)S(1)}, bf16[128,1024]{1,0:T(8,128)(2,1)S(1)}, u32[]{:S(2)}, u32[]{:S(2)}) collective-permute-start(bf16[128,1024]{1,0:T(8,128)(2,1)S(1)} %collective-permute-done.3.far_ref), channel_id=1, source_target_pairs={{0,4},{4,0},{8,12},{12,8},{16,20},{20,16},{24,28},{28,24},{32,36},... | collective-permute-start | bytes 786440 | tf_op jit(solution)/shard_map/ppermute | solution.py:293
  26.3 13.8 %all-to-all-start.1 = ((bf16[128,4,128]{2,1,0:T(4,128)(2,1)}), bf16[128,4,128]{2,1,0:T(4,128)(2,1)S(1)}, u32[]{:S(2)}, u32[]{:S(2)}) async-start(bf16[128,4,128]{2,1,0:T(4,128)(2,1)} %bitcast.4), calls=%async_computation.1 | async-start | bytes 262144 | tf_op jit(solution)/shard_map/all_to_all | solution.py:294
  30.6 3.8 %collective-permute-start.5 = (bf16[64,256]{1,0:T(8,128)(2,1)S(1)}, bf16[64,256]{1,0:T(8,128)(2,1)S(1)}, u32[]{:S(2)}, u32[]{:S(2)}) collective-permute-start(bf16[64,256]{1,0:T(8,128)(2,1)S(1)} %get-tuple-element.18), channel_id=1, source_target_pairs={{0,3},{1,0},{2,1},{3,2},{4,7},{5,4},{6,5},{7,6},{8,11},{9,8},{10,9... | collective-permute-start | bytes 98312 | tf_op jit(solution)/shard_map/ppermute | solution.py:287
  33.3 4.6 %collective-permute-start.6 = (bf16[64,256]{1,0:T(8,128)(2,1)S(1)}, bf16[64,256]{1,0:T(8,128)(2,1)S(1)}, u32[]{:S(2)}, u32[]{:S(2)}) collective-permute-start(bf16[64,256]{1,0:T(8,128)(2,1)S(1)} %get-tuple-element.19), channel_id=1, source_target_pairs={{0,2},{1,3},{2,0},{3,1},{4,6},{5,7},{6,4},{7,5},{8,10},{9,11},{10,... | collective-permute-start | bytes 98312 | tf_op jit(solution)/shard_map/ppermute | solution.py:287
  33.8 4.4 %collective-permute-start.7 = (bf16[64,256]{1,0:T(8,128)(2,1)S(1)}, bf16[64,256]{1,0:T(8,128)(2,1)S(1)}, u32[]{:S(2)}, u32[]{:S(2)}) collective-permute-start(bf16[64,256]{1,0:T(8,128)(2,1)S(1)} %get-tuple-element.20), channel_id=1, source_target_pairs={{0,1},{1,2},{2,3},{3,0},{4,5},{5,6},{6,7},{7,4},{8,9},{9,10},{10,1... | collective-permute-start | bytes 98312 | tf_op jit(solution)/shard_map/ppermute | solution.py:287

commit v7 on v6

--- a/solution.py
+++ b/solution.py
@@ -116,7 +116,7 @@
         out_ref[...] = rows_ref[pl.ds(pl.multiple_of(64 * block, 64), 64), :]
 
 
-def conv_kernel(got_ref, taps_ref, skip_ref, ahead_ref, fine_ref, turn_ref, back_ref, out_ref):
+def conv_kernel(got_ref, taps_ref, skip_ref, ahead_ref, fine_ref, turn_ref, back_ref, out_ref, sent_ref, sems):
     place = lax.axis_index("seq")
     lane = lax.broadcasted_iota(jnp.int32, (OWN, SPAN), 1)
     row = lax.broadcasted_iota(jnp.int32, (OWN, SPAN), 0)
@@ -173,19 +173,25 @@
     both = dot(product.astype(BF), gather)
     real, imag = both[:, :SPAN], both[:, SPAN:]
     turned = jnp.concatenate([real * cos - imag * sin, real * sin + imag * cos], axis=0)
-    conv = dot(back_ref[...], turned.astype(BF))
+    turned = turned.astype(BF)
     skip = own(skip_ref[...])
-    direct = (signal.astype(F32).reshape(BLOCKS, OWN, SPAN) * skip).reshape(SPAN, SPAN)
-    mixed = (conv + direct).reshape(BLOCKS, OWN, SPAN)
-    early = jnp.where(thin < 2, mixed[:, :, :128] * shaped(0), mixed[:, :, :128])
-    halves = [[rows.reshape(128, 128) for rows in swap_halves(part)] for part in (early, mixed[:, :, 128:])]
     half = lax.broadcasted_iota(jnp.int32, (128, 128), 1) < 64
+    writes = []
     for h in range(2):
-        low, high = halves[h]
+        columns = slice(128 * h, 128 * h + 128)
+        conv = dot(back_ref[...], turned[:, columns]).reshape(BLOCKS, OWN, 128)
+        part = conv + signal[:, columns].astype(F32).reshape(BLOCKS, OWN, 128) * skip
+        if h == 0:
+            part = jnp.where(thin < 2, part * shaped(0), part)
+        low, high = (rows.reshape(128, 128) for rows in swap_halves(part))
         even = jnp.where(half, low, pltpu.roll(high, 64, 1))
         odd = jnp.where(half, pltpu.roll(low, 64, 1), high)
-        out_ref[256 * h : 256 * h + 128, :] = even.astype(BF)
-        out_ref[256 * h + 128 : 256 * h + 256, :] = odd.astype(BF)
+        sent_ref[256 * h : 256 * h + 256, :] = jnp.concatenate([even, odd], axis=0).astype(BF)
+        rows = pl.ds(256 * h, 256)
+        writes.append(pltpu.make_async_copy(sent_ref.at[rows], out_ref.at[rows], sems.at[h]))
+        writes[h].start()
+    for write in writes:
+        write.wait()
 
 
 def project_kernel(got_ref, own_ref, near_ref, swap_ref, other_ref, far_ref, far_swap_ref, *rest):
@@ -199,9 +205,10 @@
         return (jnp.concatenate([rows[:64], rows[64:]], axis=1) * query_refs[step][...].astype(F32)).astype(BF)
 
     blocks = [gated(step) for step in range(4)]
-    total = dot(blocks[0], own_ref[...]) + dot(jnp.where(odd == 0, blocks[1], blocks[3]), near_ref[...])
+    turned = (odd + place) % 2
+    total = dot(blocks[0], own_ref[...]) + dot(jnp.where(turned == 0, blocks[1], blocks[3]), near_ref[...])
     for rows, here_ref, there_ref in (
-        (jnp.where(odd == 0, blocks[3], blocks[1]), other_ref, swap_ref),
+        (jnp.where(turned == 0, blocks[3], blocks[1]), other_ref, swap_ref),
         (blocks[2], far_ref, far_swap_ref),
     ):
         total = total + dot(jnp.where(odd == 0, rows[:, :128], rows[:, 128:]), here_ref[...])
@@ -254,7 +261,8 @@
         conv_kernel,
         out_shape=jax.ShapeDtypeStruct((512, 128), BF),
         in_specs=[VMEM] * 7,
-        out_specs=VMEM,
+        out_specs=HBM,
+        scratch_shapes=[pltpu.VMEM((512, 128), BF), pltpu.SemaphoreType.DMA((2,))],
         compiler_params=PARAMS,
         cost_estimate=TINY,
     )(got, *held)
@@ -272,14 +280,15 @@
 
 
 def on_device(projected, short_taps, filters, skip_gain, out_weight):
-    ring = [(s * 4 + (j + (1 if s % 2 == 0 else 3)) % 4, s * 4 + j) for s in range(BLOCKS) for j in range(4)]
     pairs = [(s, s ^ 1) for s in range(BLOCKS)]
-    near = lax.ppermute(out_weight, ("seq", "chan"), ring)
+    fetch = [(s * 4 + (3 - j if s % 2 else j ^ 1), s * 4 + j) for s in range(BLOCKS) for j in range(4)]
+    forward = [((s ^ 1) * 4 + (3 - j if s % 2 else j ^ 1), s * 4 + j) for s in range(BLOCKS) for j in range(4)]
+    near = lax.ppermute(out_weight, ("seq", "chan"), fetch)
     core = lax.axis_index("seq") & 1
-    half = lax.dynamic_slice_in_dim(near, 128 * core, 128, 0)
-    other = lax.dynamic_slice_in_dim(near, 128 - 128 * core, 128, 0)
-    far = lax.ppermute(half, ("seq", "chan"), ring)
-    swaps = [lax.ppermute(part, "seq", pairs) for part in (half, other)]
+    passed = lax.dynamic_slice_in_dim(near, 128 - 128 * core, 128, 0)
+    far = lax.ppermute(passed, ("seq", "chan"), forward)
+    kept = lax.dynamic_slice_in_dim(near, 128 * core, 128, 0)
+    swaps = [lax.ppermute(part, "seq", pairs) for part in (kept, passed)]
     by_part = projected.transpose(1, 0, 2)
     packed = pack(by_part, filters, short_taps).reshape(BLOCKS, 40, 128)
     got = lax.all_to_all(packed, "seq", split_axis=0, concat_axis=0, tiled=True).reshape(BLOCKS * 40, 128)

time: 41.6 us -> 41.7 us (level)
    all_to_all x1, starting transfers between devices: 10.3 us -> 8.22 us  [on_device(): lax.all_to_all(packed, 'seq', split_axis=0, concat_axis=0, tiled=True)]
    ppermute x4, starting transfers between devices: 2.63 us -> 3.96 us  [the longest x1 3.31 us: on_device(): near = lax.ppermute(out_weight, ('seq', 'chan'), fetch)]
    all_to_all x1, starting transfers between devices: 3.91 us -> 4.95 us  [on_device(): lax.all_to_all(mixed.reshape(128, 4, 128), ('chan', 'seq'), split_axis=0,...]
where the time goes in v7:
time: 41.7 us; the launch traced here: 41.5 us
  starting transfers between devices  21 us (50%)
  waiting for transfers between devices  14.4 us (35%)
  Pallas kernels  5.7 us (14%)
    all_to_all x1, waiting for transfers between devices, on_device(): lax.all_to_all(packed, 'seq', split_axis=0, concat_axis=0, tiled=True)  8.86 us
    all_to_all x1, starting transfers between devices, on_device(): lax.all_to_all(packed, 'seq', split_axis=0, concat_axis=0, tiled=True)  8.22 us
    all_to_all x1, starting transfers between devices, on_device(): lax.all_to_all(mixed.reshape(128, 4, 128), ('chan', 'seq'), split_axis=0,...  4.95 us
    ppermute x3, starting transfers between devices, on_device(): lax.ppermute(block, 'chan', [(j, (j - step) % 4) for j in range(4)])  3.82 us
    ppermute x3, waiting for transfers between devices, on_device(): lax.ppermute(block, 'chan', [(j, (j - step) % 4) for j in range(4)])  3.76 us
    ppermute x1, starting transfers between devices, on_device(): near = lax.ppermute(out_weight, ('seq', 'chan'), fetch)  3.31 us
    pallas_call x1, Pallas kernels, pack(): pl.pallas_call(pack_kernel, out_shape=jax.ShapeDtypeStruct((BLOCKS * 40,...  2.14 us
    pallas_call x1, Pallas kernels, convolve(): pl.pallas_call(conv_kernel, out_shape=jax.ShapeDtypeStruct((512, 128), BF...  2.02 us
  transfers between devices with their start and end apart: 10, of which 4 were waited for; matrix products, arithmetic and copies ran while one was open for 0% of the time, Pallas kernels for 11%

profile of v7, /device:TPU:1, one launch (start us, length us, event | category | flops | bytes accessed | tf_op | source)
XLA Modules:
  0.0 41.5 jit_solution(2162878301374290801)
XLA Ops:
  0.0 3.3 %collective-permute-start = (bf16[256,1024]{1,0:T(8,128)(2,1)}, bf16[256,1024]{1,0:T(8,128)(2,1)S(1)}, u32[]{:S(2)}, u32[]{:S(2)}) collective-permute-start(bf16[256,1024]{1,0:T(8,128)(2,1)} %own_ref.1), channel_id=1, source_target_pairs={{1,0},{0,1},{3,2},{2,3},{7,4},{6,5},{5,6},{4,7},{9,8},{8,9},{11,10... | collective-permute-start | bytes 1572872 | tf_op jit(solution)/shard_map/ppermute | solution.py:286
  3.3 2.1 %shard_map.91 = bf16[1280,128]{1,0:T(8,128)(2,1)} custom-call(bf16[3,256,256]{2,1,0:T(8,128)(2,1)} %bitcast.6, f32[256,256]{1,0:T(8,128)} %filters_ref.1, f32[3,3,256]{2,1,0:T(4,128)} %taps_ref.3), custom_call_target="tpu_custom_call" | custom-call | flops 1000 | bytes 1000 | tf_op jit(solution)/shard_map/pallas_call | solution.py:228
  5.5 0.0 copy-start.7
  5.5 8.2 %all-to-all-start = ((bf16[32,40,128]{2,1,0:T(8,128)(2,1)}), bf16[32,40,128]{2,1,0:T(8,128)(2,1)S(1)}, u32[]{:S(2)}, u32[]{:S(2)}) async-start(bf16[32,40,128]{2,1,0:T(8,128)(2,1)} %bitcast.11), calls=%async_computation | async-start | bytes 655360 | tf_op jit(solution)/shard_map/all_to_all | solution.py:294
  13.7 0.0 copy-start.6
  13.7 0.0 copy-start.2
  13.7 0.0 copy-start.3
  13.7 0.0 copy-start.4
  13.8 0.0 copy-start.5
  13.8 0.3 collective-permute-start.1
  14.1 0.3 collective-permute-start.2
  14.4 0.1 collective-permute-start.3
  14.5 8.9 %all-to-all-done = bf16[32,40,128]{2,1,0:T(8,128)(2,1)S(1)} async-done(((bf16[32,40,128]{2,1,0:T(8,128)(2,1)}), bf16[32,40,128]{2,1,0:T(8,128)(2,1)S(1)}, u32[]{:S(2)}, u32[]{:S(2)}) %all-to-all-start) | async-done | bytes 327712 | tf_op jit(solution)/shard_map/all_to_all | solution.py:294
  23.4 2.0 %shard_map.92 = bf16[512,128]{1,0:T(8,128)(2,1)} custom-call(bf16[1280,128]{1,0:T(8,128)(2,1)S(1)} %bitcast.8, f32[3,3,256]{2,1,0:T(4,128)S(1)} %copy-done.6, f32[1,256]{1,0:T(1,128)S(1)} %bitcast.10, bf16[512,256]{1,0:T(8,128)(2,1)S(1)} %copy-done.2, bf16[512,256]{1,0:T(8,128)(2,1)S(1)} %copy-done.3, bf16[512,256]{1,0:T(8,128)(2,1)S(1)} %copy-done.4, ...), custom_call_target="tpu_custom_call" | custom-call | flops 1000 | bytes 1000 | tf_op jit(solution)/shard_map/pallas_call | solution.py:260
  25.5 0.1 collective-permute-start.4
  25.6 5.0 %all-to-all-start.1 = ((bf16[128,4,128]{2,1,0:T(4,128)(2,1)}), bf16[128,4,128]{2,1,0:T(4,128)(2,1)S(1)}, u32[]{:S(2)}, u32[]{:S(2)}) async-start(bf16[128,4,128]{2,1,0:T(4,128)(2,1)} %bitcast.4), calls=%async_computation.1 | async-start | bytes 262144 | tf_op jit(solution)/shard_map/all_to_all | solution.py:303
  30.5 0.3 shard_map.93
  30.9 2.7 %collective-permute-start.5 = (bf16[64,256]{1,0:T(8,128)(2,1)S(1)}, bf16[64,256]{1,0:T(8,128)(2,1)S(1)}, u32[]{:S(2)}, u32[]{:S(2)}) collective-permute-start(bf16[64,256]{1,0:T(8,128)(2,1)S(1)} %get-tuple-element.18), channel_id=1, source_target_pairs={{0,3},{1,0},{2,1},{3,2},{4,7},{5,4},{6,5},{7,6},{8,11},{9,8},{10,9... | collective-permute-start | bytes 98312 | tf_op jit(solution)/shard_map/ppermute | solution.py:296
  33.6 0.6 %collective-permute-start.6 = (bf16[64,256]{1,0:T(8,128)(2,1)S(1)}, bf16[64,256]{1,0:T(8,128)(2,1)S(1)}, u32[]{:S(2)}, u32[]{:S(2)}) collective-permute-start(bf16[64,256]{1,0:T(8,128)(2,1)S(1)} %get-tuple-element.19), channel_id=1, source_target_pairs={{0,2},{1,3},{2,0},{3,1},{4,6},{5,7},{6,4},{7,5},{8,10},{9,11},{10,... | collective-permute-start | bytes 98312 | tf_op jit(solution)/shard_map/ppermute | solution.py:296
  34.1 0.6 %collective-permute-start.7 = (bf16[64,256]{1,0:T(8,128)(2,1)S(1)}, bf16[64,256]{1,0:T(8,128)(2,1)S(1)}, u32[]{:S(2)}, u32[]{:S(2)}) collective-permute-start(bf16[64,256]{1,0:T(8,128)(2,1)S(1)} %get-tuple-element.20), channel_id=1, source_target_pairs={{0,1},{1,2},{2,3},{3,0},{4,5},{5,6},{6,7},{7,4},{8,9},{9,10},{10,1... | collective-permute-start | bytes 98312 | tf_op jit(solution)/shard_map/ppermute | solution.py:296
  34.7 3.4 %collective-permute-done.6.rest_2_ = bf16[64,256]{1,0:T(8,128)(2,1)S(1)} collective-permute-done((bf16[64,256]{1,0:T(8,128)(2,1)S(1)}, bf16[64,256]{1,0:T(8,128)(2,1)S(1)}, u32[]{:S(2)}, u32[]{:S(2)}) %collective-permute-start.6) | collective-permute-done | bytes 32800 | tf_op jit(solution)/shard_map/ppermute | solution.py:296
  38.1 0.4 collective-permute-done.7.rest_3_
  38.5 1.8 %all-to-all-done.1 = bf16[128,4,128]{2,1,0:T(4,128)(2,1)S(1)} async-done(((bf16[128,4,128]{2,1,0:T(4,128)(2,1)}), bf16[128,4,128]{2,1,0:T(4,128)(2,1)S(1)}, u32[]{:S(2)}, u32[]{:S(2)}) %all-to-all-start.1) | async-done | bytes 131104 | tf_op jit(solution)/shard_map/all_to_all | solution.py:303
  40.3 1.2 %shard_map.94 = bf16[64,1024]{1,0:T(8,128)(2,1)} custom-call(bf16[512,128]{1,0:T(8,128)(2,1)S(1)} %bitcast.9, bf16[256,1024]{1,0:T(8,128)(2,1)S(1)} %copy-done.1, bf16[256,1024]{1,0:T(8,128)(2,1)S(1)} %collective-permute-done.near_ref, bf16[128,1024]{1,0:T(8,128)(2,1)S(1)} %collective-permute-done.1.swap_ref, ...), custom_call_target="tpu_custom_call" | custom-call | flops 1000 | bytes 1000 | tf_op jit(solution)/shard_map/pallas_call | solution.py:272
  (17 shorter events, 0.1 us)
Async XLA Ops:
  0.0 13.8 %collective-permute-start = (bf16[256,1024]{1,0:T(8,128)(2,1)}, bf16[256,1024]{1,0:T(8,128)(2,1)S(1)}, u32[]{:S(2)}, u32[]{:S(2)}) collective-permute-start(bf16[256,1024]{1,0:T(8,128)(2,1)} %own_ref.1), channel_id=1, source_target_pairs={{1,0},{0,1},{3,2},{2,3},{7,4},{6,5},{5,6},{4,7},{9,8},{8,9},{11,10... | collective-permute-start | bytes 1572872 | tf_op jit(solution)/shard_map/ppermute | solution.py:286
  5.5 17.9 %copy-start.7 = (f32[256]{0:T(256)S(1)}, f32[256]{0:T(256)}, u32[]{:S(2)}) copy-start(f32[256]{0:T(256)} %param.12) | copy-start | bytes 3076
  5.5 17.9 %all-to-all-start = ((bf16[32,40,128]{2,1,0:T(8,128)(2,1)}), bf16[32,40,128]{2,1,0:T(8,128)(2,1)S(1)}, u32[]{:S(2)}, u32[]{:S(2)}) async-start(bf16[32,40,128]{2,1,0:T(8,128)(2,1)} %bitcast.11), calls=%async_computation | async-start | bytes 655360 | tf_op jit(solution)/shard_map/all_to_all | solution.py:294
  13.7 9.7 %copy-start.6 = (f32[3,3,256]{2,1,0:T(4,128)S(1)}, f32[3,3,256]{2,1,0:T(4,128)}, u32[]{:S(2)}) copy-start(f32[3,3,256]{2,1,0:T(4,128)} %taps_ref.3) | copy-start | bytes 27652
  13.7 9.7 %copy-start.2 = (bf16[512,256]{1,0:T(8,128)(2,1)S(1)}, bf16[512,256]{1,0:T(8,128)(2,1)}, u32[]{:S(2)}) copy-start(bf16[512,256]{1,0:T(8,128)(2,1)} %constant.28.ahead_ref) | copy-start | bytes 786436
  13.7 9.7 %copy-start.3 = (bf16[512,256]{1,0:T(8,128)(2,1)S(1)}, bf16[512,256]{1,0:T(8,128)(2,1)}, u32[]{:S(2)}) copy-start(bf16[512,256]{1,0:T(8,128)(2,1)} %constant.29.fine_ref) | copy-start | bytes 786436
  13.7 9.6 %copy-start.4 = (bf16[512,256]{1,0:T(8,128)(2,1)S(1)}, bf16[512,256]{1,0:T(8,128)(2,1)}, u32[]{:S(2)}) copy-start(bf16[512,256]{1,0:T(8,128)(2,1)} %constant.30.turn_ref) | copy-start | bytes 786436
  13.8 9.6 %copy-start.5 = (bf16[256,512]{1,0:T(8,128)(2,1)S(1)}, bf16[256,512]{1,0:T(8,128)(2,1)}, u32[]{:S(2)}) copy-start(bf16[256,512]{1,0:T(8,128)(2,1)} %constant.31.back_ref) | copy-start | bytes 786436
  13.8 9.5 %collective-permute-start.1 = (bf16[128,1024]{1,0:T(8,128)(2,1)S(1)}, bf16[128,1024]{1,0:T(8,128)(2,1)S(1)}, u32[]{:S(2)}, u32[]{:S(2)}) collective-permute-start(bf16[128,1024]{1,0:T(8,128)(2,1)S(1)} %get-tuple-element.22), channel_id=1, source_target_pairs={{0,4},{4,0},{8,12},{12,8},{16,20},{20,16},{24,28},{28,24},{32,36},... | collective-permute-start | bytes 786440 | tf_op jit(solution)/shard_map/ppermute | solution.py:291
  14.1 9.2 %collective-permute-start.2 = (bf16[128,1024]{1,0:T(8,128)(2,1)S(1)}, bf16[128,1024]{1,0:T(8,128)(2,1)S(1)}, u32[]{:S(2)}, u32[]{:S(2)}) collective-permute-start(bf16[128,1024]{1,0:T(8,128)(2,1)S(1)} %get-tuple-element.21), channel_id=1, source_target_pairs={{0,4},{4,0},{8,12},{12,8},{16,20},{20,16},{24,28},{28,24},{32,36},... | collective-permute-start | bytes 786440 | tf_op jit(solution)/shard_map/ppermute | solution.py:291
  14.4 11.0 %collective-permute-start.3 = (bf16[128,1024]{1,0:T(8,128)(2,1)S(1)}, bf16[128,1024]{1,0:T(8,128)(2,1)S(1)}, u32[]{:S(2)}, u32[]{:S(2)}) collective-permute-start(bf16[128,1024]{1,0:T(8,128)(2,1)S(1)} %get-tuple-element.21), channel_id=1, source_target_pairs={{5,0},{4,1},{7,2},{6,3},{3,4},{2,5},{1,6},{0,7},{13,8},{12,9},{15,... | collective-permute-start | bytes 786440 | tf_op jit(solution)/shard_map/ppermute | solution.py:289
  23.4 7.1 %copy-start = (bf16[256,3,256]{2,0,1:T(8,128)(2,1)S(1)}, bf16[256,3,256]{2,0,1:T(8,128)(2,1)}, u32[]{:S(2)}) copy-start(bf16[256,3,256]{2,0,1:T(8,128)(2,1)} %param.9) | copy-start | bytes 1179652
  25.4 14.8 %copy-start.1 = (bf16[256,1024]{1,0:T(8,128)(2,1)S(1)}, bf16[256,1024]{1,0:T(8,128)(2,1)}, u32[]{:S(2)}) copy-start(bf16[256,1024]{1,0:T(8,128)(2,1)} %own_ref.1) | copy-start | bytes 1572868
  25.5 14.8 %collective-permute-start.4 = (bf16[128,1024]{1,0:T(8,128)(2,1)S(1)}, bf16[128,1024]{1,0:T(8,128)(2,1)S(1)}, u32[]{:S(2)}, u32[]{:S(2)}) collective-permute-start(bf16[128,1024]{1,0:T(8,128)(2,1)S(1)} %collective-permute-done.3.far_ref), channel_id=1, source_target_pairs={{0,4},{4,0},{8,12},{12,8},{16,20},{20,16},{24,28},{28,24},{32,36},... | collective-permute-start | bytes 786440 | tf_op jit(solution)/shard_map/ppermute | solution.py:302
  25.6 14.7 %all-to-all-start.1 = ((bf16[128,4,128]{2,1,0:T(4,128)(2,1)}), bf16[128,4,128]{2,1,0:T(4,128)(2,1)S(1)}, u32[]{:S(2)}, u32[]{:S(2)}) async-start(bf16[128,4,128]{2,1,0:T(4,128)(2,1)} %bitcast.4), calls=%async_computation.1 | async-start | bytes 262144 | tf_op jit(solution)/shard_map/all_to_all | solution.py:303
  30.9 3.8 %collective-permute-start.5 = (bf16[64,256]{1,0:T(8,128)(2,1)S(1)}, bf16[64,256]{1,0:T(8,128)(2,1)S(1)}, u32[]{:S(2)}, u32[]{:S(2)}) collective-permute-start(bf16[64,256]{1,0:T(8,128)(2,1)S(1)} %get-tuple-element.18), channel_id=1, source_target_pairs={{0,3},{1,0},{2,1},{3,2},{4,7},{5,4},{6,5},{7,6},{8,11},{9,8},{10,9... | collective-permute-start | bytes 98312 | tf_op jit(solution)/shard_map/ppermute | solution.py:296
  33.6 4.6 %collective-permute-start.6 = (bf16[64,256]{1,0:T(8,128)(2,1)S(1)}, bf16[64,256]{1,0:T(8,128)(2,1)S(1)}, u32[]{:S(2)}, u32[]{:S(2)}) collective-permute-start(bf16[64,256]{1,0:T(8,128)(2,1)S(1)} %get-tuple-element.19), channel_id=1, source_target_pairs={{0,2},{1,3},{2,0},{3,1},{4,6},{5,7},{6,4},{7,5},{8,10},{9,11},{10,... | collective-permute-start | bytes 98312 | tf_op jit(solution)/shard_map/ppermute | solution.py:296
  34.1 4.3 %collective-permute-start.7 = (bf16[64,256]{1,0:T(8,128)(2,1)S(1)}, bf16[64,256]{1,0:T(8,128)(2,1)S(1)}, u32[]{:S(2)}, u32[]{:S(2)}) collective-permute-start(bf16[64,256]{1,0:T(8,128)(2,1)S(1)} %get-tuple-element.20), channel_id=1, source_target_pairs={{0,1},{1,2},{2,3},{3,0},{4,5},{5,6},{6,7},{7,4},{8,9},{9,10},{10,1... | collective-permute-start | bytes 98312 | tf_op jit(solution)/shard_map/ppermute | solution.py:296

commit v8 on v6

--- a/solution.py
+++ b/solution.py
@@ -93,10 +93,14 @@
     blank = jnp.zeros((2, SPAN), F32)
     edges = jnp.concatenate(first + [blank] + last + [blank, jnp.zeros((112, SPAN), F32)], axis=0)
     message = jnp.concatenate(signal + long + [by_device(edges.T)], axis=1)
-    sent_ref[...] = message.reshape(BLOCKS * 40, 128).astype(BF)
-    write = pltpu.make_async_copy(sent_ref, out_ref, sems.at[6])
-    write.start()
-    write.wait()
+    writes = []
+    for part in range(2):
+        rows = pl.ds(640 * part, 640)
+        sent_ref[640 * part : 640 * part + 640, :] = message[16 * part : 16 * part + 16].reshape(640, 128).astype(BF)
+        writes.append(pltpu.make_async_copy(sent_ref.at[rows], out_ref.at[rows], sems.at[6 + part]))
+        writes[part].start()
+    for write in writes:
+        write.wait()
 
 
 def query_kernel(projected_ref, taps_ref, *rest):
@@ -229,7 +233,7 @@
             pltpu.VMEM((SPAN, SPAN), F32),
             pltpu.VMEM((3, 3, SPAN), F32),
             pltpu.VMEM((BLOCKS * 40, 128), BF),
-            pltpu.SemaphoreType.DMA((7,)),
+            pltpu.SemaphoreType.DMA((8,)),
         ],
         cost_estimate=TINY,
     )(projected, filters, short_taps)

time: 41.6 us -> 41.6 us (level)
  no operation moved by 1% of the time
where the time goes in v8:
time: 41.6 us; the launch traced here: 41.3 us
  starting transfers between devices  20.7 us (50%)
  waiting for transfers between devices  14.6 us (35%)
  Pallas kernels  5.71 us (14%)
    all_to_all x1, starting transfers between devices, on_device(): lax.all_to_all(packed, 'seq', split_axis=0, concat_axis=0, tiled=True)  10.3 us
    all_to_all x1, waiting for transfers between devices, on_device(): lax.all_to_all(packed, 'seq', split_axis=0, concat_axis=0, tiled=True)  8.92 us
    all_to_all x1, starting transfers between devices, on_device(): lax.all_to_all(mixed.reshape(128, 4, 128), ('chan', 'seq'), split_axis=0,...  3.91 us
    ppermute x3, starting transfers between devices, on_device(): lax.ppermute(block, 'chan', [(j, (j - step) % 4) for j in range(4)])  3.84 us
    ppermute x3, waiting for transfers between devices, on_device(): lax.ppermute(block, 'chan', [(j, (j - step) % 4) for j in range(4)])  3.78 us
    pallas_call x1, Pallas kernels, pack(): pl.pallas_call(pack_kernel, out_shape=jax.ShapeDtypeStruct((BLOCKS * 40,...  2.14 us
    ppermute x1, starting transfers between devices, on_device(): near = lax.ppermute(out_weight, ('seq', 'chan'), ring)  2.04 us
    pallas_call x1, Pallas kernels, convolve(): pl.pallas_call(conv_kernel, out_shape=jax.ShapeDtypeStruct((512, 128), BF...  2.03 us
  transfers between devices with their start and end apart: 10, of which 4 were waited for; matrix products, arithmetic and copies ran while one was open for 0% of the time, Pallas kernels for 11%

profile of v8, /device:TPU:1, one launch (start us, length us, event | category | flops | bytes accessed | tf_op | source)
XLA Modules:
  0.0 41.3 jit_solution(8092077394499258111)
XLA Ops:
  0.0 2.0 %collective-permute-start = (bf16[256,1024]{1,0:T(8,128)(2,1)}, bf16[256,1024]{1,0:T(8,128)(2,1)S(1)}, u32[]{:S(2)}, u32[]{:S(2)}) collective-permute-start(bf16[256,1024]{1,0:T(8,128)(2,1)} %own_ref.1), channel_id=1, source_target_pairs={{1,0},{2,1},{3,2},{0,3},{7,4},{4,5},{5,6},{6,7},{9,8},{10,9},{11,1... | collective-permute-start | bytes 1572872 | tf_op jit(solution)/shard_map/ppermute | solution.py:281
  2.0 2.1 %shard_map.91 = bf16[1280,128]{1,0:T(8,128)(2,1)} custom-call(bf16[3,256,256]{2,1,0:T(8,128)(2,1)} %bitcast.6, f32[256,256]{1,0:T(8,128)} %filters_ref.1, f32[3,3,256]{2,1,0:T(4,128)} %taps_ref.3), custom_call_target="tpu_custom_call" | custom-call | flops 1000 | bytes 1000 | tf_op jit(solution)/shard_map/pallas_call | solution.py:225
  4.2 0.0 copy-start.7
  4.2 10.3 %all-to-all-start = ((bf16[32,40,128]{2,1,0:T(8,128)(2,1)}), bf16[32,40,128]{2,1,0:T(8,128)(2,1)S(1)}, u32[]{:S(2)}, u32[]{:S(2)}) async-start(bf16[32,40,128]{2,1,0:T(8,128)(2,1)} %bitcast.11), calls=%async_computation | async-start | bytes 655360 | tf_op jit(solution)/shard_map/all_to_all | solution.py:289
  14.5 0.0 copy-start.6
  14.6 0.0 copy-start.2
  14.6 0.0 copy-start.3
  14.6 0.0 copy-start.4
  14.6 0.0 copy-start.5
  14.7 0.3 collective-permute-start.1
  15.0 0.3 collective-permute-start.2
  15.3 8.9 %all-to-all-done = bf16[32,40,128]{2,1,0:T(8,128)(2,1)S(1)} async-done(((bf16[32,40,128]{2,1,0:T(8,128)(2,1)}), bf16[32,40,128]{2,1,0:T(8,128)(2,1)S(1)}, u32[]{:S(2)}, u32[]{:S(2)}) %all-to-all-start) | async-done | bytes 327712 | tf_op jit(solution)/shard_map/all_to_all | solution.py:289
  24.2 0.0 copy-start
  24.3 2.0 %shard_map.92 = bf16[512,128]{1,0:T(8,128)(2,1)} custom-call(bf16[1280,128]{1,0:T(8,128)(2,1)S(1)} %bitcast.8, f32[3,3,256]{2,1,0:T(4,128)S(1)} %copy-done.6, f32[1,256]{1,0:T(1,128)S(1)} %bitcast.10, bf16[512,256]{1,0:T(8,128)(2,1)S(1)} %copy-done.2, bf16[512,256]{1,0:T(8,128)(2,1)S(1)} %copy-done.3, bf16[512,256]{1,0:T(8,128)(2,1)S(1)} %copy-done.4, ...), custom_call_target="tpu_custom_call" | custom-call | flops 1000 | bytes 1000 | tf_op jit(solution)/shard_map/pallas_call | solution.py:257
  26.3 0.0 collective-permute-start.4
  26.3 3.9 %all-to-all-start.1 = ((bf16[128,4,128]{2,1,0:T(4,128)(2,1)}), bf16[128,4,128]{2,1,0:T(4,128)(2,1)S(1)}, u32[]{:S(2)}, u32[]{:S(2)}) async-start(bf16[128,4,128]{2,1,0:T(4,128)(2,1)} %bitcast.4), calls=%async_computation.1 | async-start | bytes 262144 | tf_op jit(solution)/shard_map/all_to_all | solution.py:298
  30.2 0.3 shard_map.93
  30.6 2.7 %collective-permute-start.5 = (bf16[64,256]{1,0:T(8,128)(2,1)S(1)}, bf16[64,256]{1,0:T(8,128)(2,1)S(1)}, u32[]{:S(2)}, u32[]{:S(2)}) collective-permute-start(bf16[64,256]{1,0:T(8,128)(2,1)S(1)} %get-tuple-element.18), channel_id=1, source_target_pairs={{0,3},{1,0},{2,1},{3,2},{4,7},{5,4},{6,5},{7,6},{8,11},{9,8},{10,9... | collective-permute-start | bytes 98312 | tf_op jit(solution)/shard_map/ppermute | solution.py:291
  33.3 0.5 %collective-permute-start.6 = (bf16[64,256]{1,0:T(8,128)(2,1)S(1)}, bf16[64,256]{1,0:T(8,128)(2,1)S(1)}, u32[]{:S(2)}, u32[]{:S(2)}) collective-permute-start(bf16[64,256]{1,0:T(8,128)(2,1)S(1)} %get-tuple-element.19), channel_id=1, source_target_pairs={{0,2},{1,3},{2,0},{3,1},{4,6},{5,7},{6,4},{7,5},{8,10},{9,11},{10,... | collective-permute-start | bytes 98312 | tf_op jit(solution)/shard_map/ppermute | solution.py:291
  33.8 0.6 %collective-permute-start.7 = (bf16[64,256]{1,0:T(8,128)(2,1)S(1)}, bf16[64,256]{1,0:T(8,128)(2,1)S(1)}, u32[]{:S(2)}, u32[]{:S(2)}) collective-permute-start(bf16[64,256]{1,0:T(8,128)(2,1)S(1)} %get-tuple-element.20), channel_id=1, source_target_pairs={{0,1},{1,2},{2,3},{3,0},{4,5},{5,6},{6,7},{7,4},{8,9},{9,10},{10,1... | collective-permute-start | bytes 98312 | tf_op jit(solution)/shard_map/ppermute | solution.py:291
  34.4 3.4 %collective-permute-done.6.rest_2_ = bf16[64,256]{1,0:T(8,128)(2,1)S(1)} collective-permute-done((bf16[64,256]{1,0:T(8,128)(2,1)S(1)}, bf16[64,256]{1,0:T(8,128)(2,1)S(1)}, u32[]{:S(2)}, u32[]{:S(2)}) %collective-permute-start.6) | collective-permute-done | bytes 32800 | tf_op jit(solution)/shard_map/ppermute | solution.py:291
  37.9 0.4 collective-permute-done.7.rest_3_
  38.2 1.9 %all-to-all-done.1 = bf16[128,4,128]{2,1,0:T(4,128)(2,1)S(1)} async-done(((bf16[128,4,128]{2,1,0:T(4,128)(2,1)}), bf16[128,4,128]{2,1,0:T(4,128)(2,1)S(1)}, u32[]{:S(2)}, u32[]{:S(2)}) %all-to-all-start.1) | async-done | bytes 131104 | tf_op jit(solution)/shard_map/all_to_all | solution.py:298
  40.1 1.2 %shard_map.94 = bf16[64,1024]{1,0:T(8,128)(2,1)} custom-call(bf16[512,128]{1,0:T(8,128)(2,1)S(1)} %bitcast.9, bf16[256,1024]{1,0:T(8,128)(2,1)S(1)} %copy-done.1, bf16[256,1024]{1,0:T(8,128)(2,1)S(1)} %collective-permute-done.near_ref, bf16[128,1024]{1,0:T(8,128)(2,1)S(1)} %collective-permute-done.1.swap_ref, ...), custom_call_target="tpu_custom_call" | custom-call | flops 1000 | bytes 1000 | tf_op jit(solution)/shard_map/pallas_call | solution.py:268
  (17 shorter events, 0.1 us)
Async XLA Ops:
  0.0 14.6 %collective-permute-start = (bf16[256,1024]{1,0:T(8,128)(2,1)}, bf16[256,1024]{1,0:T(8,128)(2,1)S(1)}, u32[]{:S(2)}, u32[]{:S(2)}) collective-permute-start(bf16[256,1024]{1,0:T(8,128)(2,1)} %own_ref.1), channel_id=1, source_target_pairs={{1,0},{2,1},{3,2},{0,3},{7,4},{4,5},{5,6},{6,7},{9,8},{10,9},{11,1... | collective-permute-start | bytes 1572872 | tf_op jit(solution)/shard_map/ppermute | solution.py:281
  4.2 20.0 %copy-start.7 = (f32[256]{0:T(256)S(1)}, f32[256]{0:T(256)}, u32[]{:S(2)}) copy-start(f32[256]{0:T(256)} %param.12) | copy-start | bytes 3076
  4.2 20.0 %all-to-all-start = ((bf16[32,40,128]{2,1,0:T(8,128)(2,1)}), bf16[32,40,128]{2,1,0:T(8,128)(2,1)S(1)}, u32[]{:S(2)}, u32[]{:S(2)}) async-start(bf16[32,40,128]{2,1,0:T(8,128)(2,1)} %bitcast.11), calls=%async_computation | async-start | bytes 655360 | tf_op jit(solution)/shard_map/all_to_all | solution.py:289
  14.5 9.7 %copy-start.6 = (f32[3,3,256]{2,1,0:T(4,128)S(1)}, f32[3,3,256]{2,1,0:T(4,128)}, u32[]{:S(2)}) copy-start(f32[3,3,256]{2,1,0:T(4,128)} %taps_ref.3) | copy-start | bytes 27652
  14.6 9.7 %copy-start.2 = (bf16[512,256]{1,0:T(8,128)(2,1)S(1)}, bf16[512,256]{1,0:T(8,128)(2,1)}, u32[]{:S(2)}) copy-start(bf16[512,256]{1,0:T(8,128)(2,1)} %constant.28.ahead_ref) | copy-start | bytes 786436
  14.6 9.7 %copy-start.3 = (bf16[512,256]{1,0:T(8,128)(2,1)S(1)}, bf16[512,256]{1,0:T(8,128)(2,1)}, u32[]{:S(2)}) copy-start(bf16[512,256]{1,0:T(8,128)(2,1)} %constant.29.fine_ref) | copy-start | bytes 786436
  14.6 9.6 %copy-start.4 = (bf16[512,256]{1,0:T(8,128)(2,1)S(1)}, bf16[512,256]{1,0:T(8,128)(2,1)}, u32[]{:S(2)}) copy-start(bf16[512,256]{1,0:T(8,128)(2,1)} %constant.30.turn_ref) | copy-start | bytes 786436
  14.6 9.6 %copy-start.5 = (bf16[256,512]{1,0:T(8,128)(2,1)S(1)}, bf16[256,512]{1,0:T(8,128)(2,1)}, u32[]{:S(2)}) copy-start(bf16[256,512]{1,0:T(8,128)(2,1)} %constant.31.back_ref) | copy-start | bytes 786436
  14.7 9.5 %collective-permute-start.1 = (bf16[128,1024]{1,0:T(8,128)(2,1)S(1)}, bf16[128,1024]{1,0:T(8,128)(2,1)S(1)}, u32[]{:S(2)}, u32[]{:S(2)}) collective-permute-start(bf16[128,1024]{1,0:T(8,128)(2,1)S(1)} %get-tuple-element.22), channel_id=1, source_target_pairs={{0,4},{4,0},{8,12},{12,8},{16,20},{20,16},{24,28},{28,24},{32,36},... | collective-permute-start | bytes 786440 | tf_op jit(solution)/shard_map/ppermute | solution.py:286
  15.0 9.2 %collective-permute-start.2 = (bf16[128,1024]{1,0:T(8,128)(2,1)S(1)}, bf16[128,1024]{1,0:T(8,128)(2,1)S(1)}, u32[]{:S(2)}, u32[]{:S(2)}) collective-permute-start(bf16[128,1024]{1,0:T(8,128)(2,1)S(1)} %get-tuple-element.21), channel_id=1, source_target_pairs={{0,4},{4,0},{8,12},{12,8},{16,20},{20,16},{24,28},{28,24},{32,36},... | collective-permute-start | bytes 786440 | tf_op jit(solution)/shard_map/ppermute | solution.py:286
  15.3 11.0 %collective-permute-start.3 = (bf16[128,1024]{1,0:T(8,128)(2,1)S(1)}, bf16[128,1024]{1,0:T(8,128)(2,1)S(1)}, u32[]{:S(2)}, u32[]{:S(2)}) collective-permute-start(bf16[128,1024]{1,0:T(8,128)(2,1)S(1)} %get-tuple-element.22), channel_id=1, source_target_pairs={{1,0},{2,1},{3,2},{0,3},{7,4},{4,5},{5,6},{6,7},{9,8},{10,9},{11,1... | collective-permute-start | bytes 786440 | tf_op jit(solution)/shard_map/ppermute | solution.py:285
  24.2 6.0 %copy-start = (bf16[256,3,256]{2,0,1:T(8,128)(2,1)S(1)}, bf16[256,3,256]{2,0,1:T(8,128)(2,1)}, u32[]{:S(2)}) copy-start(bf16[256,3,256]{2,0,1:T(8,128)(2,1)} %param.9) | copy-start | bytes 1179652
  26.3 13.8 %copy-start.1 = (bf16[256,1024]{1,0:T(8,128)(2,1)S(1)}, bf16[256,1024]{1,0:T(8,128)(2,1)}, u32[]{:S(2)}) copy-start(bf16[256,1024]{1,0:T(8,128)(2,1)} %own_ref.1) | copy-start | bytes 1572868
  26.3 13.8 %collective-permute-start.4 = (bf16[128,1024]{1,0:T(8,128)(2,1)S(1)}, bf16[128,1024]{1,0:T(8,128)(2,1)S(1)}, u32[]{:S(2)}, u32[]{:S(2)}) collective-permute-start(bf16[128,1024]{1,0:T(8,128)(2,1)S(1)} %collective-permute-done.3.far_ref), channel_id=1, source_target_pairs={{0,4},{4,0},{8,12},{12,8},{16,20},{20,16},{24,28},{28,24},{32,36},... | collective-permute-start | bytes 786440 | tf_op jit(solution)/shard_map/ppermute | solution.py:297
  26.3 13.8 %all-to-all-start.1 = ((bf16[128,4,128]{2,1,0:T(4,128)(2,1)}), bf16[128,4,128]{2,1,0:T(4,128)(2,1)S(1)}, u32[]{:S(2)}, u32[]{:S(2)}) async-start(bf16[128,4,128]{2,1,0:T(4,128)(2,1)} %bitcast.4), calls=%async_computation.1 | async-start | bytes 262144 | tf_op jit(solution)/shard_map/all_to_all | solution.py:298
  30.6 3.8 %collective-permute-start.5 = (bf16[64,256]{1,0:T(8,128)(2,1)S(1)}, bf16[64,256]{1,0:T(8,128)(2,1)S(1)}, u32[]{:S(2)}, u32[]{:S(2)}) collective-permute-start(bf16[64,256]{1,0:T(8,128)(2,1)S(1)} %get-tuple-element.18), channel_id=1, source_target_pairs={{0,3},{1,0},{2,1},{3,2},{4,7},{5,4},{6,5},{7,6},{8,11},{9,8},{10,9... | collective-permute-start | bytes 98312 | tf_op jit(solution)/shard_map/ppermute | solution.py:291
  33.3 4.6 %collective-permute-start.6 = (bf16[64,256]{1,0:T(8,128)(2,1)S(1)}, bf16[64,256]{1,0:T(8,128)(2,1)S(1)}, u32[]{:S(2)}, u32[]{:S(2)}) collective-permute-start(bf16[64,256]{1,0:T(8,128)(2,1)S(1)} %get-tuple-element.19), channel_id=1, source_target_pairs={{0,2},{1,3},{2,0},{3,1},{4,6},{5,7},{6,4},{7,5},{8,10},{9,11},{10,... | collective-permute-start | bytes 98312 | tf_op jit(solution)/shard_map/ppermute | solution.py:291
  33.8 4.4 %collective-permute-start.7 = (bf16[64,256]{1,0:T(8,128)(2,1)S(1)}, bf16[64,256]{1,0:T(8,128)(2,1)S(1)}, u32[]{:S(2)}, u32[]{:S(2)}) collective-permute-start(bf16[64,256]{1,0:T(8,128)(2,1)S(1)} %get-tuple-element.20), channel_id=1, source_target_pairs={{0,1},{1,2},{2,3},{3,0},{4,5},{5,6},{6,7},{7,4},{8,9},{9,10},{10,1... | collective-permute-start | bytes 98312 | tf_op jit(solution)/shard_map/ppermute | solution.py:291

commit v9 on v6

--- a/solution.py
+++ b/solution.py
@@ -130,6 +130,9 @@
     def block(first_row):
         return got[:, first_row : first_row + 8], got[:, first_row + 8 : first_row + 16]
 
+    response = jnp.concatenate([half.reshape(SPAN, 128) for half in block(16)], axis=1).astype(BF)
+    res_half = dot(ahead_ref[...], response)
+
     edges = got[:, 32:40]
     before = jnp.concatenate([jnp.zeros((1, OWN, 128), F32), edges[:-1]], axis=0)
     thin = lax.broadcasted_iota(jnp.int32, (BLOCKS, OWN, 128), 2)
@@ -146,8 +149,6 @@
     early, late = block(0)
     early = jnp.where(thin < 2, shaped(1) * shaped(2), early)
     signal = jnp.concatenate([early.reshape(SPAN, 128), late.reshape(SPAN, 128)], axis=1).astype(BF)
-    response = jnp.concatenate([half.reshape(SPAN, 128) for half in block(16)], axis=1).astype(BF)
-    res_half = dot(ahead_ref[...], response)
     sig_half = dot(ahead_ref[...], signal)
     cos, sin = turn_ref[:SPAN].astype(F32), turn_ref[SPAN:].astype(F32)
     fine_cos, fine_sin = fine_ref[:SPAN], fine_ref[SPAN:]

time: 41.6 us -> 41.6 us (level)
  no operation moved by 1% of the time
where the time goes in v9:
time: 41.6 us; the launch traced here: 41.3 us
  starting transfers between devices  20.7 us (50%)
  waiting for transfers between devices  14.6 us (35%)
  Pallas kernels  5.71 us (14%)
    all_to_all x1, starting transfers between devices, on_device(): lax.all_to_all(packed, 'seq', split_axis=0, concat_axis=0, tiled=True)  10.3 us
    all_to_all x1, waiting for transfers between devices, on_device(): lax.all_to_all(packed, 'seq', split_axis=0, concat_axis=0, tiled=True)  8.92 us
    all_to_all x1, starting transfers between devices, on_device(): lax.all_to_all(mixed.reshape(128, 4, 128), ('chan', 'seq'), split_axis=0,...  3.91 us
    ppermute x3, starting transfers between devices, on_device(): lax.ppermute(block, 'chan', [(j, (j - step) % 4) for j in range(4)])  3.84 us
    ppermute x3, waiting for transfers between devices, on_device(): lax.ppermute(block, 'chan', [(j, (j - step) % 4) for j in range(4)])  3.78 us
    pallas_call x1, Pallas kernels, pack(): pl.pallas_call(pack_kernel, out_shape=jax.ShapeDtypeStruct((BLOCKS * 40,...  2.14 us
    ppermute x1, starting transfers between devices, on_device(): near = lax.ppermute(out_weight, ('seq', 'chan'), ring)  2.04 us
    pallas_call x1, Pallas kernels, convolve(): pl.pallas_call(conv_kernel, out_shape=jax.ShapeDtypeStruct((512, 128), BF...  2.03 us
  transfers between devices with their start and end apart: 10, of which 4 were waited for; matrix products, arithmetic and copies ran while one was open for 0% of the time, Pallas kernels for 11%

profile of v9, /device:TPU:1, one launch (start us, length us, event | category | flops | bytes accessed | tf_op | source)
XLA Modules:
  0.0 41.3 jit_solution(13206633445268862782)
XLA Ops:
  0.0 2.0 %collective-permute-start = (bf16[256,1024]{1,0:T(8,128)(2,1)}, bf16[256,1024]{1,0:T(8,128)(2,1)S(1)}, u32[]{:S(2)}, u32[]{:S(2)}) collective-permute-start(bf16[256,1024]{1,0:T(8,128)(2,1)} %own_ref.1), channel_id=1, source_target_pairs={{1,0},{2,1},{3,2},{0,3},{7,4},{4,5},{5,6},{6,7},{9,8},{10,9},{11,1... | collective-permute-start | bytes 1572872 | tf_op jit(solution)/shard_map/ppermute | solution.py:278
  2.0 2.1 %shard_map.91 = bf16[1280,128]{1,0:T(8,128)(2,1)} custom-call(bf16[3,256,256]{2,1,0:T(8,128)(2,1)} %bitcast.6, f32[256,256]{1,0:T(8,128)} %filters_ref.1, f32[3,3,256]{2,1,0:T(4,128)} %taps_ref.3), custom_call_target="tpu_custom_call" | custom-call | flops 1000 | bytes 1000 | tf_op jit(solution)/shard_map/pallas_call | solution.py:222
  4.2 0.0 copy-start.7
  4.2 10.3 %all-to-all-start = ((bf16[32,40,128]{2,1,0:T(8,128)(2,1)}), bf16[32,40,128]{2,1,0:T(8,128)(2,1)S(1)}, u32[]{:S(2)}, u32[]{:S(2)}) async-start(bf16[32,40,128]{2,1,0:T(8,128)(2,1)} %bitcast.11), calls=%async_computation | async-start | bytes 655360 | tf_op jit(solution)/shard_map/all_to_all | solution.py:286
  14.5 0.0 copy-start.6
  14.6 0.0 copy-start.2
  14.6 0.0 copy-start.3
  14.6 0.0 copy-start.4
  14.6 0.0 copy-start.5
  14.7 0.3 collective-permute-start.1
  15.0 0.3 collective-permute-start.2
  15.3 8.9 %all-to-all-done = bf16[32,40,128]{2,1,0:T(8,128)(2,1)S(1)} async-done(((bf16[32,40,128]{2,1,0:T(8,128)(2,1)}), bf16[32,40,128]{2,1,0:T(8,128)(2,1)S(1)}, u32[]{:S(2)}, u32[]{:S(2)}) %all-to-all-start) | async-done | bytes 327712 | tf_op jit(solution)/shard_map/all_to_all | solution.py:286
  24.2 0.0 copy-start
  24.3 2.0 %shard_map.92 = bf16[512,128]{1,0:T(8,128)(2,1)} custom-call(bf16[1280,128]{1,0:T(8,128)(2,1)S(1)} %bitcast.8, f32[3,3,256]{2,1,0:T(4,128)S(1)} %copy-done.6, f32[1,256]{1,0:T(1,128)S(1)} %bitcast.10, bf16[512,256]{1,0:T(8,128)(2,1)S(1)} %copy-done.2, bf16[512,256]{1,0:T(8,128)(2,1)S(1)} %copy-done.3, bf16[512,256]{1,0:T(8,128)(2,1)S(1)} %copy-done.4, ...), custom_call_target="tpu_custom_call" | custom-call | flops 1000 | bytes 1000 | tf_op jit(solution)/shard_map/pallas_call | solution.py:254
  26.3 0.0 collective-permute-start.4
  26.3 3.9 %all-to-all-start.1 = ((bf16[128,4,128]{2,1,0:T(4,128)(2,1)}), bf16[128,4,128]{2,1,0:T(4,128)(2,1)S(1)}, u32[]{:S(2)}, u32[]{:S(2)}) async-start(bf16[128,4,128]{2,1,0:T(4,128)(2,1)} %bitcast.4), calls=%async_computation.1 | async-start | bytes 262144 | tf_op jit(solution)/shard_map/all_to_all | solution.py:295
  30.2 0.3 shard_map.93
  30.6 2.7 %collective-permute-start.5 = (bf16[64,256]{1,0:T(8,128)(2,1)S(1)}, bf16[64,256]{1,0:T(8,128)(2,1)S(1)}, u32[]{:S(2)}, u32[]{:S(2)}) collective-permute-start(bf16[64,256]{1,0:T(8,128)(2,1)S(1)} %get-tuple-element.18), channel_id=1, source_target_pairs={{0,3},{1,0},{2,1},{3,2},{4,7},{5,4},{6,5},{7,6},{8,11},{9,8},{10,9... | collective-permute-start | bytes 98312 | tf_op jit(solution)/shard_map/ppermute | solution.py:288
  33.3 0.5 %collective-permute-start.6 = (bf16[64,256]{1,0:T(8,128)(2,1)S(1)}, bf16[64,256]{1,0:T(8,128)(2,1)S(1)}, u32[]{:S(2)}, u32[]{:S(2)}) collective-permute-start(bf16[64,256]{1,0:T(8,128)(2,1)S(1)} %get-tuple-element.19), channel_id=1, source_target_pairs={{0,2},{1,3},{2,0},{3,1},{4,6},{5,7},{6,4},{7,5},{8,10},{9,11},{10,... | collective-permute-start | bytes 98312 | tf_op jit(solution)/shard_map/ppermute | solution.py:288
  33.8 0.6 %collective-permute-start.7 = (bf16[64,256]{1,0:T(8,128)(2,1)S(1)}, bf16[64,256]{1,0:T(8,128)(2,1)S(1)}, u32[]{:S(2)}, u32[]{:S(2)}) collective-permute-start(bf16[64,256]{1,0:T(8,128)(2,1)S(1)} %get-tuple-element.20), channel_id=1, source_target_pairs={{0,1},{1,2},{2,3},{3,0},{4,5},{5,6},{6,7},{7,4},{8,9},{9,10},{10,1... | collective-permute-start | bytes 98312 | tf_op jit(solution)/shard_map/ppermute | solution.py:288
  34.4 3.4 %collective-permute-done.6.rest_2_ = bf16[64,256]{1,0:T(8,128)(2,1)S(1)} collective-permute-done((bf16[64,256]{1,0:T(8,128)(2,1)S(1)}, bf16[64,256]{1,0:T(8,128)(2,1)S(1)}, u32[]{:S(2)}, u32[]{:S(2)}) %collective-permute-start.6) | collective-permute-done | bytes 32800 | tf_op jit(solution)/shard_map/ppermute | solution.py:288
  37.9 0.4 collective-permute-done.7.rest_3_
  38.2 1.9 %all-to-all-done.1 = bf16[128,4,128]{2,1,0:T(4,128)(2,1)S(1)} async-done(((bf16[128,4,128]{2,1,0:T(4,128)(2,1)}), bf16[128,4,128]{2,1,0:T(4,128)(2,1)S(1)}, u32[]{:S(2)}, u32[]{:S(2)}) %all-to-all-start.1) | async-done | bytes 131104 | tf_op jit(solution)/shard_map/all_to_all | solution.py:295
  40.1 1.2 %shard_map.94 = bf16[64,1024]{1,0:T(8,128)(2,1)} custom-call(bf16[512,128]{1,0:T(8,128)(2,1)S(1)} %bitcast.9, bf16[256,1024]{1,0:T(8,128)(2,1)S(1)} %copy-done.1, bf16[256,1024]{1,0:T(8,128)(2,1)S(1)} %collective-permute-done.near_ref, bf16[128,1024]{1,0:T(8,128)(2,1)S(1)} %collective-permute-done.1.swap_ref, ...), custom_call_target="tpu_custom_call" | custom-call | flops 1000 | bytes 1000 | tf_op jit(solution)/shard_map/pallas_call | solution.py:265
  (17 shorter events, 0.1 us)
Async XLA Ops:
  0.0 14.6 %collective-permute-start = (bf16[256,1024]{1,0:T(8,128)(2,1)}, bf16[256,1024]{1,0:T(8,128)(2,1)S(1)}, u32[]{:S(2)}, u32[]{:S(2)}) collective-permute-start(bf16[256,1024]{1,0:T(8,128)(2,1)} %own_ref.1), channel_id=1, source_target_pairs={{1,0},{2,1},{3,2},{0,3},{7,4},{4,5},{5,6},{6,7},{9,8},{10,9},{11,1... | collective-permute-start | bytes 1572872 | tf_op jit(solution)/shard_map/ppermute | solution.py:278
  4.2 20.0 %copy-start.7 = (f32[256]{0:T(256)S(1)}, f32[256]{0:T(256)}, u32[]{:S(2)}) copy-start(f32[256]{0:T(256)} %param.12) | copy-start | bytes 3076
  4.2 20.0 %all-to-all-start = ((bf16[32,40,128]{2,1,0:T(8,128)(2,1)}), bf16[32,40,128]{2,1,0:T(8,128)(2,1)S(1)}, u32[]{:S(2)}, u32[]{:S(2)}) async-start(bf16[32,40,128]{2,1,0:T(8,128)(2,1)} %bitcast.11), calls=%async_computation | async-start | bytes 655360 | tf_op jit(solution)/shard_map/all_to_all | solution.py:286
  14.5 9.7 %copy-start.6 = (f32[3,3,256]{2,1,0:T(4,128)S(1)}, f32[3,3,256]{2,1,0:T(4,128)}, u32[]{:S(2)}) copy-start(f32[3,3,256]{2,1,0:T(4,128)} %taps_ref.3) | copy-start | bytes 27652
  14.6 9.7 %copy-start.2 = (bf16[512,256]{1,0:T(8,128)(2,1)S(1)}, bf16[512,256]{1,0:T(8,128)(2,1)}, u32[]{:S(2)}) copy-start(bf16[512,256]{1,0:T(8,128)(2,1)} %constant.28.ahead_ref) | copy-start | bytes 786436
  14.6 9.7 %copy-start.3 = (bf16[512,256]{1,0:T(8,128)(2,1)S(1)}, bf16[512,256]{1,0:T(8,128)(2,1)}, u32[]{:S(2)}) copy-start(bf16[512,256]{1,0:T(8,128)(2,1)} %constant.29.fine_ref) | copy-start | bytes 786436
  14.6 9.6 %copy-start.4 = (bf16[512,256]{1,0:T(8,128)(2,1)S(1)}, bf16[512,256]{1,0:T(8,128)(2,1)}, u32[]{:S(2)}) copy-start(bf16[512,256]{1,0:T(8,128)(2,1)} %constant.30.turn_ref) | copy-start | bytes 786436
  14.6 9.6 %copy-start.5 = (bf16[256,512]{1,0:T(8,128)(2,1)S(1)}, bf16[256,512]{1,0:T(8,128)(2,1)}, u32[]{:S(2)}) copy-start(bf16[256,512]{1,0:T(8,128)(2,1)} %constant.31.back_ref) | copy-start | bytes 786436
  14.7 9.5 %collective-permute-start.1 = (bf16[128,1024]{1,0:T(8,128)(2,1)S(1)}, bf16[128,1024]{1,0:T(8,128)(2,1)S(1)}, u32[]{:S(2)}, u32[]{:S(2)}) collective-permute-start(bf16[128,1024]{1,0:T(8,128)(2,1)S(1)} %get-tuple-element.22), channel_id=1, source_target_pairs={{0,4},{4,0},{8,12},{12,8},{16,20},{20,16},{24,28},{28,24},{32,36},... | collective-permute-start | bytes 786440 | tf_op jit(solution)/shard_map/ppermute | solution.py:283
  15.0 9.2 %collective-permute-start.2 = (bf16[128,1024]{1,0:T(8,128)(2,1)S(1)}, bf16[128,1024]{1,0:T(8,128)(2,1)S(1)}, u32[]{:S(2)}, u32[]{:S(2)}) collective-permute-start(bf16[128,1024]{1,0:T(8,128)(2,1)S(1)} %get-tuple-element.21), channel_id=1, source_target_pairs={{0,4},{4,0},{8,12},{12,8},{16,20},{20,16},{24,28},{28,24},{32,36},... | collective-permute-start | bytes 786440 | tf_op jit(solution)/shard_map/ppermute | solution.py:283
  15.3 11.0 %collective-permute-start.3 = (bf16[128,1024]{1,0:T(8,128)(2,1)S(1)}, bf16[128,1024]{1,0:T(8,128)(2,1)S(1)}, u32[]{:S(2)}, u32[]{:S(2)}) collective-permute-start(bf16[128,1024]{1,0:T(8,128)(2,1)S(1)} %get-tuple-element.22), channel_id=1, source_target_pairs={{1,0},{2,1},{3,2},{0,3},{7,4},{4,5},{5,6},{6,7},{9,8},{10,9},{11,1... | collective-permute-start | bytes 786440 | tf_op jit(solution)/shard_map/ppermute | solution.py:282
  24.2 6.0 %copy-start = (bf16[256,3,256]{2,0,1:T(8,128)(2,1)S(1)}, bf16[256,3,256]{2,0,1:T(8,128)(2,1)}, u32[]{:S(2)}) copy-start(bf16[256,3,256]{2,0,1:T(8,128)(2,1)} %param.9) | copy-start | bytes 1179652
  26.3 13.8 %copy-start.1 = (bf16[256,1024]{1,0:T(8,128)(2,1)S(1)}, bf16[256,1024]{1,0:T(8,128)(2,1)}, u32[]{:S(2)}) copy-start(bf16[256,1024]{1,0:T(8,128)(2,1)} %own_ref.1) | copy-start | bytes 1572868
  26.3 13.8 %collective-permute-start.4 = (bf16[128,1024]{1,0:T(8,128)(2,1)S(1)}, bf16[128,1024]{1,0:T(8,128)(2,1)S(1)}, u32[]{:S(2)}, u32[]{:S(2)}) collective-permute-start(bf16[128,1024]{1,0:T(8,128)(2,1)S(1)} %collective-permute-done.3.far_ref), channel_id=1, source_target_pairs={{0,4},{4,0},{8,12},{12,8},{16,20},{20,16},{24,28},{28,24},{32,36},... | collective-permute-start | bytes 786440 | tf_op jit(solution)/shard_map/ppermute | solution.py:294
  26.3 13.8 %all-to-all-start.1 = ((bf16[128,4,128]{2,1,0:T(4,128)(2,1)}), bf16[128,4,128]{2,1,0:T(4,128)(2,1)S(1)}, u32[]{:S(2)}, u32[]{:S(2)}) async-start(bf16[128,4,128]{2,1,0:T(4,128)(2,1)} %bitcast.4), calls=%async_computation.1 | async-start | bytes 262144 | tf_op jit(solution)/shard_map/all_to_all | solution.py:295
  30.6 3.8 %collective-permute-start.5 = (bf16[64,256]{1,0:T(8,128)(2,1)S(1)}, bf16[64,256]{1,0:T(8,128)(2,1)S(1)}, u32[]{:S(2)}, u32[]{:S(2)}) collective-permute-start(bf16[64,256]{1,0:T(8,128)(2,1)S(1)} %get-tuple-element.18), channel_id=1, source_target_pairs={{0,3},{1,0},{2,1},{3,2},{4,7},{5,4},{6,5},{7,6},{8,11},{9,8},{10,9... | collective-permute-start | bytes 98312 | tf_op jit(solution)/shard_map/ppermute | solution.py:288
  33.3 4.6 %collective-permute-start.6 = (bf16[64,256]{1,0:T(8,128)(2,1)S(1)}, bf16[64,256]{1,0:T(8,128)(2,1)S(1)}, u32[]{:S(2)}, u32[]{:S(2)}) collective-permute-start(bf16[64,256]{1,0:T(8,128)(2,1)S(1)} %get-tuple-element.19), channel_id=1, source_target_pairs={{0,2},{1,3},{2,0},{3,1},{4,6},{5,7},{6,4},{7,5},{8,10},{9,11},{10,... | collective-permute-start | bytes 98312 | tf_op jit(solution)/shard_map/ppermute | solution.py:288
  33.8 4.4 %collective-permute-start.7 = (bf16[64,256]{1,0:T(8,128)(2,1)S(1)}, bf16[64,256]{1,0:T(8,128)(2,1)S(1)}, u32[]{:S(2)}, u32[]{:S(2)}) collective-permute-start(bf16[64,256]{1,0:T(8,128)(2,1)S(1)} %get-tuple-element.20), channel_id=1, source_target_pairs={{0,1},{1,2},{2,3},{3,0},{4,5},{5,6},{6,7},{7,4},{8,9},{9,10},{10,1... | collective-permute-start | bytes 98312 | tf_op jit(solution)/shard_map/ppermute | solution.py:288
